TPU v7x, 32 devices: a whole 2x2x4 slice. The times are simulated.
32 devices in a mesh: dp: 8 (over y, x, core), space: 4 (over z).
Axes of the slice: x: 2, y: 2, z: 4, core: 2. Of those that a mesh axis runs over, the one named last changes fastest.
Arguments:
- clip_maps: bfloat16 [384, 8, 8, 2048], P('dp', 'space'), may hold values from -6 to 6
- next_frame: int32 [384], P('dp'), may hold values from 1 to 383, as said below
- valid_rows: int32 [384, 8], P('dp', 'space'), may hold values from 0 to 1, as said below
- proj_in: bfloat16 [2, 2048, 512], replicated, may hold values from -0.125 to 0.125
- conv_mid: bfloat16 [2, 4608, 512], replicated, may hold values from -0.09375 to 0.09375
- proj_out: bfloat16 [2, 512, 2048], replicated, may hold values from -0.25 to 0.25
- gate_reduce: bfloat16 [2, 2048, 128], replicated, may hold values from -0.125 to 0.125
- gate_convs: bfloat16 [2, 3, 1152, 128], replicated, may hold values from -0.1875 to 0.1875
- gate_expand: bfloat16 [2, 128, 2048], replicated, may hold values from -0.5 to 0.5
- norm_gain: float32 [2, 3072], replicated, may hold values from 0.5 to 1.5
- norm_bias: float32 [2, 3072], replicated, may hold values from -1.5 to 1.5
- out_grad: bfloat16 [384, 8, 8, 2048], P('dp', 'space'), may hold values from -6 to 6
Outputs:
- out_maps: bfloat16 [384, 8, 8, 2048], P('dp', 'space')
- grad_maps: bfloat16 [384, 8, 8, 2048], P('dp', 'space')
- grad_proj_in: float32 [2, 2048, 512], P(None, 'dp')
- grad_conv_mid: float32 [2, 4608, 512], P(None, 'dp')
- grad_proj_out: float32 [2, 512, 2048], P(None, 'dp')
- grad_gate_reduce: float32 [2, 2048, 128], P(None, 'dp')
- grad_gate_convs: float32 [2, 3, 1152, 128], replicated
- grad_gate_expand: float32 [2, 128, 2048], replicated
- grad_norm_gain: float32 [2, 3072], replicated
- grad_norm_bias: float32 [2, 3072], replicated
Inputs may be any that keep to these rules, and one draw needn't show every extreme that they name: `next_frame`: for each frame, the index of the next segment's frame of its clip, or its own index for a clip's last segment. Clips are runs of 8 or 16 consecutive frames starting at a multiple of their length and lie inside one block of 48 frames. `valid_rows`: 1 on the first rows of a frame and 0 below; the frames of one clip share the same count of such rows, 4 to 8; in every block of 48 frames some clip has all 8 rows.
All inputs are finite; a program needn't handle non-finite values.
Results may differ from a plain program's by a relative error of at most 0.023.
Values may be sent and summed in bfloat16 or wider, within the bound.
No kernel may reach another device: no remote copies, remote signals or barrier semaphores. Data moves between devices by JAX's collectives and lax.ppermute only.
A program may use at most 320 MiB of HBM per device.

v0:
```python
import jax
import jax.numpy as jnp
from jax import lax
from jax.sharding import PartitionSpec as P

norm_eps = 1e-05


def with_halo(block, sides, width):
    for axis, dim in sides:
        count = lax.axis_size(axis)
        forward = [(i, i + 1) for i in range(count - 1)]
        backward = [(target, source) for source, target in forward]
        low = lax.ppermute(
            lax.slice_in_dim(block, block.shape[dim] - width, None, axis=dim), axis, forward
        )
        high = lax.ppermute(lax.slice_in_dim(block, 0, width, axis=dim), axis, backward)
        block = jnp.concatenate([low, block, high], axis=dim)
    return block


def matmul_plain(left_side, right_side):
    return jnp.dot(left_side, right_side, preferred_element_type=jnp.float32)


def matmul_inner(left_side, right_side):
    return lax.dot_general(
        left_side, right_side, (((0,), (0,)), ((), ())), preferred_element_type=jnp.float32
    )


def matmul_back(left_side, right_side):
    return lax.dot_general(
        left_side, right_side, (((1,), (1,)), ((), ())), preferred_element_type=jnp.float32
    )


def tap_stack(padded, num_rows, num_cols, flipped):
    windows = []
    for tap_row in range(3):
        for tap_col in range(3):
            first_row = 2 - tap_row if flipped else tap_row
            first_col = 2 - tap_col if flipped else tap_col
            windows.append(
                padded[:, first_row : first_row + num_rows, first_col : first_col + num_cols, :]
            )
    stacked = jnp.concatenate(windows, axis=-1)
    return stacked.reshape(-1, stacked.shape[-1])


def pad_columns(values):
    return jnp.pad(values, ((0, 0), (0, 0), (1, 1), (0, 0)))


def full_taps(values, flipped):
    padded = jnp.pad(values, ((0, 0), (1, 1), (1, 1), (0, 0)))
    return tap_stack(padded, values.shape[1], values.shape[2], flipped)


def flip_weight(weight, channels_in):
    tap_blocks = weight.reshape(9, channels_in, -1)
    return jnp.swapaxes(tap_blocks, 1, 2).reshape(-1, channels_in)


def pool_map(values, factor):
    frames, height, map_width, channels = values.shape
    shaped = values.reshape(frames, height // factor, factor, map_width // factor, factor, channels)
    return jnp.mean(shaped, axis=(2, 4))


def expand_map(values, factor):
    return jnp.repeat(jnp.repeat(values, factor, axis=1), factor, axis=2)


def normalize_then_activate(
    values,
    sum_values,
    sum_squares,
    pixel_total,
    gain_part,
    bias_part,
    mask_for_rows,
    apply_activation,
):
    mean_value = sum_values / pixel_total
    variance = sum_squares / pixel_total - mean_value * mean_value
    normed = (values - mean_value) * lax.rsqrt(variance + norm_eps) * gain_part + bias_part
    if apply_activation:
        return jax.nn.silu(normed) * mask_for_rows
    return normed


def norm_stats(values, mask_for_rows):
    masked = values * mask_for_rows
    return lax.psum(
        (jnp.sum(masked, axis=0), jnp.sum(masked * values, axis=0), jnp.sum(mask_for_rows)),
        ("dp", "space"),
    )


def norm_back(values, norm_sums, gain_part, bias_part, mask_for_rows, apply_activation, grad_norm):
    sum_values, sum_squares, pixel_total = norm_sums

    def norm_within_device(value_entries, summed_entries, squared_sums, gain_entries, bias_entries):
        return normalize_then_activate(
            value_entries,
            summed_entries,
            squared_sums,
            pixel_total,
            gain_entries,
            bias_entries,
            mask_for_rows,
            apply_activation,
        )

    unused_out, pullback = jax.vjp(
        norm_within_device, values, sum_values, sum_squares, gain_part, bias_part
    )
    grad_values, grad_sum, grad_squares, grad_gain, grad_bias = pullback(grad_norm)
    total_sum, total_squares = lax.psum((grad_sum, grad_squares), ("dp", "space"))
    grad_values = grad_values + mask_for_rows * (total_sum + 2.0 * total_squares * values)
    return (grad_values, grad_gain, grad_bias)


def output_piece(resid, branch_val, pre_val, mask_for_rows):
    return jax.nn.silu(resid + branch_val * jax.nn.sigmoid(pre_val)) * mask_for_rows


def gate_forward(rows_full, next_local, convs_layer, own_start, rows_dev):
    reduced = rows_full.shape[3]
    shifted = jnp.take(rows_full, next_local, axis=0)
    diff_taps = full_taps(shifted, False)
    difference = matmul_plain(diff_taps, convs_layer[0]).reshape(
        rows_full.shape
    ) - rows_full.astype(jnp.float32)
    coarse_two = pool_map(difference, 2).astype(jnp.bfloat16)
    coarse_four = pool_map(difference, 4).astype(jnp.bfloat16)
    two_taps = full_taps(coarse_two, False)
    four_taps = full_taps(coarse_four, False)
    conv_two = matmul_plain(two_taps, convs_layer[1]).reshape(coarse_two.shape)
    conv_four = matmul_plain(four_taps, convs_layer[2]).reshape(coarse_four.shape)
    summed = difference + expand_map(conv_two, 2) + expand_map(conv_four, 4)
    gate_own = (
        lax.dynamic_slice_in_dim(summed, own_start, rows_dev, axis=1)
        .astype(jnp.bfloat16)
        .reshape(-1, reduced)
    )
    return (gate_own, (diff_taps, two_taps, four_taps, rows_full.shape))


def gate_backward(grad_own, gate_kept, convs_layer, next_local, own_start):
    diff_taps, two_taps, four_taps, full_shape = gate_kept
    reduced = full_shape[3]
    grad_summed = lax.dynamic_update_slice_in_dim(
        jnp.zeros(full_shape, jnp.float32), grad_own, own_start, axis=1
    )
    grad_two = (pool_map(grad_summed, 2) * 4.0).astype(jnp.bfloat16)
    grad_four = (pool_map(grad_summed, 4) * 16.0).astype(jnp.bfloat16)
    weight_two = matmul_inner(two_taps, grad_two.reshape(-1, reduced))
    weight_four = matmul_inner(four_taps, grad_four.reshape(-1, reduced))
    back_two = matmul_plain(
        full_taps(grad_two, True), flip_weight(convs_layer[1], reduced)
    ).reshape(grad_two.shape)
    back_four = matmul_plain(
        full_taps(grad_four, True), flip_weight(convs_layer[2], reduced)
    ).reshape(grad_four.shape)
    grad_diff = grad_summed + expand_map(back_two, 2) / 4.0 + expand_map(back_four, 4) / 16.0
    grad_diff_low = grad_diff.astype(jnp.bfloat16)
    weight_diff = matmul_inner(diff_taps, grad_diff_low.reshape(-1, reduced))
    back_shift = matmul_plain(
        full_taps(grad_diff_low, True), flip_weight(convs_layer[0], reduced)
    ).reshape(full_shape)
    grad_rows = jnp.zeros(full_shape, jnp.float32).at[next_local].add(back_shift) - grad_diff
    return (grad_rows, jnp.stack([weight_diff, weight_two, weight_four], axis=0))


def block_forward(block_in, weights, mask_maps, mask_for_rows, next_local, own_start):
    proj_w, conv_w, out_w, reduce_w, convs_w, expand_w, gain_all, bias_all = weights
    frames, rows_dev, map_width, channels = block_in.shape
    middle = proj_w.shape[1]
    reduced = reduce_w.shape[1]
    low_in = block_in.astype(jnp.bfloat16).reshape(-1, channels)
    first = matmul_plain(low_in, proj_w)
    reduce_rows = (
        matmul_plain(low_in, reduce_w)
        .astype(jnp.bfloat16)
        .reshape(frames, rows_dev, map_width, reduced)
    )
    reduce_rows = reduce_rows * mask_maps.astype(jnp.bfloat16)
    rows_full = lax.all_gather(reduce_rows, "space", axis=1, tiled=True)
    sums_one = norm_stats(first, mask_for_rows)
    hidden_one = normalize_then_activate(
        first,
        sums_one[0],
        sums_one[1],
        sums_one[2],
        gain_all[:middle],
        bias_all[:middle],
        mask_for_rows,
        True,
    ).astype(jnp.bfloat16)
    extended = with_halo(
        hidden_one.reshape(frames, rows_dev, map_width, middle), (("space", 1),), 1
    )
    mid_taps = tap_stack(pad_columns(extended), rows_dev, map_width, False)
    second = matmul_plain(mid_taps, conv_w)
    sums_two = norm_stats(second, mask_for_rows)
    hidden_two = normalize_then_activate(
        second,
        sums_two[0],
        sums_two[1],
        sums_two[2],
        gain_all[middle : 2 * middle],
        bias_all[middle : 2 * middle],
        mask_for_rows,
        True,
    ).astype(jnp.bfloat16)
    third = matmul_plain(hidden_two, out_w)
    sums_three = norm_stats(third, mask_for_rows)
    branch = normalize_then_activate(
        third,
        sums_three[0],
        sums_three[1],
        sums_three[2],
        gain_all[2 * middle :],
        bias_all[2 * middle :],
        mask_for_rows,
        False,
    )
    gate_own, gate_kept = gate_forward(rows_full, next_local, convs_w, own_start, rows_dev)
    gate_pre = matmul_plain(gate_own, expand_w)
    block_out = output_piece(block_in.reshape(-1, channels), branch, gate_pre, mask_for_rows)
    kept_state = (
        low_in,
        first,
        sums_one,
        mid_taps,
        second,
        sums_two,
        hidden_two,
        third,
        sums_three,
        branch,
        gate_own,
        gate_pre,
        gate_kept,
    )
    return (block_out.reshape(block_in.shape), kept_state)


def sum_weights(grad_proj, grad_conv, grad_out_w, grad_reduce):
    partial_sums = (
        lax.psum_scatter(
            grad_proj.astype(jnp.bfloat16), "dp", scatter_dimension=0, tiled=True
        ).astype(jnp.float32),
        lax.psum_scatter(
            grad_conv.astype(jnp.bfloat16), "dp", scatter_dimension=0, tiled=True
        ).astype(jnp.float32),
        lax.psum_scatter(
            grad_out_w.astype(jnp.bfloat16), "dp", scatter_dimension=0, tiled=True
        ).astype(jnp.float32),
        lax.psum_scatter(
            grad_reduce.astype(jnp.bfloat16), "dp", scatter_dimension=0, tiled=True
        ).astype(jnp.float32),
    )
    return (
        lax.psum(partial_sums[0].astype(jnp.bfloat16), "space").astype(jnp.float32),
        lax.psum(partial_sums[1].astype(jnp.bfloat16), "space").astype(jnp.float32),
        lax.psum(partial_sums[2].astype(jnp.bfloat16), "space").astype(jnp.float32),
        lax.psum(partial_sums[3].astype(jnp.bfloat16), "space").astype(jnp.float32),
    )


def block_backward(
    block_in, kept_state, weights, grad_out, mask_maps, mask_for_rows, next_local, own_start
):
    proj_w, conv_w, out_w, reduce_w, convs_w, expand_w, gain_all, bias_all = weights
    (
        low_in,
        first,
        sums_one,
        mid_taps,
        second,
        sums_two,
        hidden_two,
        third,
        sums_three,
        branch,
        gate_own,
        gate_pre,
        gate_kept,
    ) = kept_state
    frames, rows_dev, map_width, channels = block_in.shape
    middle = proj_w.shape[1]
    reduced = reduce_w.shape[1]

    def out_local(resid, branch_val, pre_val):
        return output_piece(resid, branch_val, pre_val, mask_for_rows)

    unused_out, pull_out = jax.vjp(out_local, block_in.reshape(-1, channels), branch, gate_pre)
    grad_in, grad_branch, grad_pre = pull_out(grad_out)
    grad_pre_low = grad_pre.astype(jnp.bfloat16)
    grad_expand = matmul_inner(gate_own, grad_pre_low)
    grad_gate_own = matmul_back(grad_pre_low, expand_w)
    grad_rows_full, grad_convs = gate_backward(
        grad_gate_own.reshape(frames, rows_dev, map_width, reduced),
        gate_kept,
        convs_w,
        next_local,
        own_start,
    )
    grad_rows = lax.psum_scatter(
        grad_rows_full.astype(jnp.bfloat16), "space", scatter_dimension=1, tiled=True
    ).astype(jnp.float32)
    grad_rows_low = (grad_rows * mask_maps).astype(jnp.bfloat16).reshape(-1, reduced)
    grad_reduce = matmul_inner(low_in, grad_rows_low)
    grad_in = grad_in + matmul_back(grad_rows_low, reduce_w)
    grad_third, gain_three, bias_three = norm_back(
        third,
        sums_three,
        gain_all[2 * middle :],
        bias_all[2 * middle :],
        mask_for_rows,
        False,
        grad_branch,
    )
    grad_third_low = grad_third.astype(jnp.bfloat16)
    grad_out_w = matmul_inner(hidden_two, grad_third_low)
    grad_hidden_two = matmul_back(grad_third_low, out_w)
    grad_second, gain_two, bias_two = norm_back(
        second,
        sums_two,
        gain_all[middle : 2 * middle],
        bias_all[middle : 2 * middle],
        mask_for_rows,
        True,
        grad_hidden_two,
    )
    grad_second_low = grad_second.astype(jnp.bfloat16)
    grad_conv = matmul_inner(mid_taps, grad_second_low)
    grad_ext = with_halo(
        grad_second_low.reshape(frames, rows_dev, map_width, middle), (("space", 1),), 1
    )
    grad_hidden_one = matmul_plain(
        tap_stack(pad_columns(grad_ext), rows_dev, map_width, True), flip_weight(conv_w, middle)
    )
    grad_first, gain_one, bias_one = norm_back(
        first, sums_one, gain_all[:middle], bias_all[:middle], mask_for_rows, True, grad_hidden_one
    )
    grad_first_low = grad_first.astype(jnp.bfloat16)
    grad_proj = matmul_inner(low_in, grad_first_low)
    grad_in = grad_in + matmul_back(grad_first_low, proj_w)
    large_sums = sum_weights(grad_proj, grad_conv, grad_out_w, grad_reduce)
    grad_gain = jnp.concatenate([gain_one, gain_two, gain_three])
    grad_bias = jnp.concatenate([bias_one, bias_two, bias_three])
    small_sums = lax.psum((grad_convs, grad_expand, grad_gain, grad_bias), ("dp", "space"))
    return (grad_in, large_sums, small_sums)


def body(
    clip_maps,
    next_frame,
    valid_rows,
    proj_in,
    conv_mid,
    proj_out,
    gate_reduce,
    gate_convs,
    gate_expand,
    norm_gain,
    norm_bias,
    out_grad,
):
    frames, rows_dev, map_width, channels = clip_maps.shape
    mask_maps = valid_rows.astype(jnp.float32)[:, :, None, None]
    mask_for_rows = jnp.broadcast_to(mask_maps, (frames, rows_dev, map_width, 1)).reshape(-1, 1)
    next_local = next_frame - lax.axis_index("dp") * frames
    own_start = lax.axis_index("space") * rows_dev

    def layer_weights(layer_index):
        return (
            proj_in[layer_index],
            conv_mid[layer_index],
            proj_out[layer_index],
            gate_reduce[layer_index],
            gate_convs[layer_index],
            gate_expand[layer_index],
            norm_gain[layer_index],
            norm_bias[layer_index],
        )

    current = clip_maps.astype(jnp.float32) * mask_maps
    layer_inputs = []
    layer_kept = []
    for layer_index in range(2):
        layer_inputs.append(current)
        current, kept_state = block_forward(
            current, layer_weights(layer_index), mask_maps, mask_for_rows, next_local, own_start
        )
        layer_kept.append(kept_state)
    final_maps = current.astype(jnp.bfloat16)
    grad_flow = out_grad.astype(jnp.float32).reshape(-1, channels)
    large_parts = [None, None]
    small_parts = [None, None]
    for layer_index in (1, 0):
        kept_state = block_forward(
            layer_inputs[layer_index],
            layer_weights(layer_index),
            mask_maps,
            mask_for_rows,
            next_local,
            own_start,
        )[1]
        grad_flow, large_sums, small_sums = block_backward(
            layer_inputs[layer_index],
            kept_state,
            layer_weights(layer_index),
            grad_flow,
            mask_maps,
            mask_for_rows,
            next_local,
            own_start,
        )
        large_parts[layer_index] = large_sums
        small_parts[layer_index] = small_sums
    grad_maps = (grad_flow.reshape(clip_maps.shape) * mask_maps).astype(jnp.bfloat16)

    def stacked(position, pieces_list):
        return jnp.stack([pieces_list[0][position], pieces_list[1][position]], axis=0)

    return (
        final_maps,
        grad_maps,
        stacked(0, large_parts),
        stacked(1, large_parts),
        stacked(2, large_parts),
        stacked(3, large_parts),
        stacked(0, small_parts),
        stacked(1, small_parts),
        stacked(2, small_parts),
        stacked(3, small_parts),
    )


def solution(mesh):
    in_specs = (
        P("dp", "space", None, None),
        P("dp"),
        P("dp", "space"),
        P(),
        P(),
        P(),
        P(),
        P(),
        P(),
        P(),
        P(),
        P("dp", "space", None, None),
    )
    out_specs = (
        P("dp", "space", None, None),
        P("dp", "space", None, None),
        P(None, "dp", None),
        P(None, "dp", None),
        P(None, "dp", None),
        P(None, "dp", None),
        P(),
        P(),
        P(),
        P(),
    )
    return jax.shard_map(body, mesh=mesh, in_specs=in_specs, out_specs=out_specs, check_vma=False)
```

profile of v0, /device:TPU:0, one launch (start us, length us, event | category | flops | bytes accessed | tf_op | source)
XLA Modules:
  0.0 1405.8 jit_solution(15498899281874108061)
XLA Ops:
  21.7 42.3 %all-reduce.29 = (f32[512]{0:T(512)S(1)}, f32[]{:T(128)}, f32[512]{0:T(512)S(1)}) all-reduce(f32[512]{0:T(512)S(1)} %get-tuple-element.42, f32[]{:T(128)} %broadcast_reduce_fusion, f32[512]{0:T(512)S(1)} %get-tuple-element.41), channel_id=1, replica_groups=mesh['dp'=8,'space'=4] {'dp','space'}, use_global_device_ids=true, to_apply=%region_5.0 | all-reduce | flops 1025 | bytes 8200 | tf_op jit(solution)/shard_map/psum | solution.py:95
  74.3 25.1 %all_gather.8 = bf16[48,8,8,128]{3,2,1,0:T(8,128)(2,1)S(1)} all-gather(bf16[48,2,8,128]{3,2,1,0:T(8,128)(2,1)S(1)} %broadcast_multiply_fusion.1), channel_id=1, replica_groups=mesh['dp'=8,'space'=4] {'space'}, dimensions={1}, use_global_device_ids=true | all-gather | bytes 983040 | tf_op jit(solution)/shard_map/all_gather | solution.py:190
  160.2 38.8 %all-reduce.28 = (f32[512]{0:T(512)S(1)}, f32[512]{0:T(512)S(1)}) all-reduce(f32[512]{0:T(512)S(1)} %get-tuple-element.40, f32[512]{0:T(512)S(1)} %get-tuple-element.39), channel_id=1, replica_groups=mesh['dp'=8,'space'=4] {'dp','space'}, use_global_device_ids=true, to_apply=%region_9.10 | all-reduce | flops 1024 | bytes 8192 | tf_op jit(solution)/shard_map/psum | solution.py:95
  206.2 40.7 %all-reduce.27 = (f32[2048]{0:T(1024)S(1)}, f32[2048]{0:T(1024)S(1)}) all-reduce(f32[2048]{0:T(1024)S(1)} %get-tuple-element.20, f32[2048]{0:T(1024)S(1)} %get-tuple-element.19), channel_id=1, replica_groups=mesh['dp'=8,'space'=4] {'dp','space'}, use_global_device_ids=true, to_apply=%region_13.14 | all-reduce | flops 4096 | bytes 32768 | tf_op jit(solution)/shard_map/psum | solution.py:95
  247.6 9.5 fusion.146
  263.1 18.1 %all_gather.9 = bf16[48,8,8,128]{3,2,1,0:T(8,128)(2,1)S(1)} all-gather(bf16[48,2,8,128]{3,2,1,0:T(8,128)(2,1)S(1)} %broadcast_multiply_fusion), channel_id=1, replica_groups=mesh['dp'=8,'space'=4] {'space'}, dimensions={1}, use_global_device_ids=true | all-gather | bytes 983040 | tf_op jit(solution)/shard_map/all_gather | solution.py:190
  300.3 39.6 %all-reduce.26 = (f32[512]{0:T(512)S(1)}, f32[512]{0:T(512)S(1)}) all-reduce(f32[512]{0:T(512)S(1)} %copy-done.153, f32[512]{0:T(512)S(1)} %copy-done.152), channel_id=1, replica_groups=mesh['dp'=8,'space'=4] {'dp','space'}, use_global_device_ids=true, to_apply=%region_19.21 | all-reduce | flops 1024 | bytes 8192 | tf_op jit(solution)/shard_map/psum | solution.py:95
  366.7 39.6 %all-reduce.25 = (f32[512]{0:T(512)S(1)}, f32[512]{0:T(512)S(1)}) all-reduce(f32[512]{0:T(512)S(1)} %get-tuple-element.36, f32[512]{0:T(512)S(1)} %get-tuple-element.35), channel_id=1, replica_groups=mesh['dp'=8,'space'=4] {'dp','space'}, use_global_device_ids=true, to_apply=%region_23.25 | all-reduce | flops 1024 | bytes 8192 | tf_op jit(solution)/shard_map/psum | solution.py:95
  413.4 39.7 %all-reduce.24 = (f32[2048]{0:T(1024)S(1)}, f32[2048]{0:T(1024)S(1)}) all-reduce(f32[2048]{0:T(1024)S(1)} %get-tuple-element.18, f32[2048]{0:T(1024)S(1)} %get-tuple-element.17), channel_id=1, replica_groups=mesh['dp'=8,'space'=4] {'dp','space'}, use_global_device_ids=true, to_apply=%region_27.29 | all-reduce | flops 4096 | bytes 32768 | tf_op jit(solution)/shard_map/psum | solution.py:95
  453.7 17.1 %fusion.5 = (bf16[768,2048]{1,0:T(8,128)(2,1)S(1)}, f32[768,2048]{1,0:T(8,128)}, f32[768,2048]{1,0:T(8,128)}, f32[768,2048]{1,0:T(8,128)}) fusion(f32[768,2048]{1,0:T(8,128)} %get-tuple-element.202, f32[2048]{0:T(1024)S(1)} %bitcast.571, f32[2048]{0:T(1024)S(1)} %bitcast.535, f32[2048]{0:T(1024)S(1)} %get-tuple-element.177, ...), kind=kOutput, calls=%fused_computation.21 | convolution fusion | flops 449839104 | bytes 38505472 | tf_op jit(solution)/shard_map/dot_general | solution.py:23
  493.2 41.1 %all-reduce.23 = (f32[2048]{0:T(1024)S(1)}, f32[2048]{0:T(1024)S(1)}) all-reduce(f32[2048]{0:T(1024)S(1)} %get-tuple-element.163, f32[2048]{0:T(1024)S(1)} %get-tuple-element.162), channel_id=1, replica_groups=mesh['dp'=8,'space'=4] {'dp','space'}, use_global_device_ids=true, to_apply=%region_37.39 | all-reduce | flops 4096 | bytes 32768 | tf_op jit(solution)/shard_map/psum | solution.py:120
  545.8 39.5 %all-reduce.22 = (f32[512]{0:T(512)S(1)}, f32[512]{0:T(512)S(1)}) all-reduce(f32[512]{0:T(512)S(1)} %get-tuple-element.189, f32[512]{0:T(512)S(1)} %get-tuple-element.188), channel_id=1, replica_groups=mesh['dp'=8,'space'=4] {'dp','space'}, use_global_device_ids=true, to_apply=%region_41.43 | all-reduce | flops 1024 | bytes 8192 | tf_op jit(solution)/shard_map/psum | solution.py:120
  623.6 43.4 %all-reduce.21 = (f32[512]{0:T(512)S(1)}, f32[512]{0:T(512)S(1)}) all-reduce(f32[512]{0:T(512)S(1)} %get-tuple-element.187, f32[512]{0:T(512)S(1)} %get-tuple-element.186), channel_id=1, replica_groups=mesh['dp'=8,'space'=4] {'dp','space'}, use_global_device_ids=true, to_apply=%region_45.47 | all-reduce | flops 1024 | bytes 8192 | tf_op jit(solution)/shard_map/psum | solution.py:120
  676.4 18.1 %multiply_reduce_fusion.3 = (f32[2048]{0:T(1024)S(1)}, f32[2048]{0:T(1024)S(1)}, f32[2048]{0:T(1024)S(1)}, f32[2048]{0:T(1024)S(1)}, f32[768,2048]{1,0:T(8,128)}...) fusion(f32[768,2048]{1,0:T(8,128)} %get-tuple-element.198, f32[2048]{0:T(1024)S(1)} %copy-done.96, ...), kind=kOutput, calls=%fused_computation.31 | convolution fusion | flops 449830912 | bytes 47976448 | tf_op jit(solution)/shard_map/dot_general | solution.py:33
  723.4 38.7 %all-reduce.39.cloned.1.call-done = bf16[48,8,8,128]{3,2,1,0:T(8,128)(2,1)} async-done(((bf16[48,8,8,128]{3,2,1,0:T(8,128)(2,1)}), bf16[48,8,8,128]{3,2,1,0:T(8,128)(2,1)}) %all-reduce.39.cloned.1.call-update) | async-done | bytes 786448
  785.6 40.2 %all-reduce.20 = (f32[2048]{0:T(1024)S(1)}, f32[2048]{0:T(1024)S(1)}) all-reduce(f32[2048]{0:T(1024)S(1)} %get-tuple-element.161, f32[2048]{0:T(1024)S(1)} %get-tuple-element.160), channel_id=1, replica_groups=mesh['dp'=8,'space'=4] {'dp','space'}, use_global_device_ids=true, to_apply=%region_53.55 | all-reduce | flops 4096 | bytes 32768 | tf_op jit(solution)/shard_map/psum | solution.py:120
  825.8 9.6 add_convert_fusion
  840.0 39.3 %all-reduce.19 = (f32[512]{0:T(512)S(1)}, f32[512]{0:T(512)S(1)}) all-reduce(f32[512]{0:T(512)S(1)} %get-tuple-element.183, f32[512]{0:T(512)S(1)} %get-tuple-element.182), channel_id=1, replica_groups=mesh['dp'=8,'space'=4] {'dp','space'}, use_global_device_ids=true, to_apply=%region_57.59 | all-reduce | flops 1024 | bytes 8192 | tf_op jit(solution)/shard_map/psum | solution.py:120
  908.9 40.0 %all-reduce.18 = (f32[512]{0:T(512)S(1)}, f32[512]{0:T(512)S(1)}, f32[1,3072]{1,0:T(1,128)S(1)}, f32[1,3072]{1,0:T(1,128)S(1)}, f32[1,3072]{1,0:T(1,128)S(1)}, /*index=5*/f32[1,3072]{1,0:T(1,128)S(1)}) all-reduce(f32[512]{0:T(512)S(1)} %get-tuple-element.181, ...), channel_id=1, replica_groups=mesh['dp'=8,'space'=4] {'dp','space'}, use_global_device_ids=true, to_apply=%region_61.63 | all-reduce | flops 13312 | bytes 106496 | tf_op jit(solution)/shard_map/psum | solution.py:120
  1004.8 12.2 reduce-scatter.15.cloned.1.call-done
  1017.0 57.4 %reduce-scatter.21.cloned.1.call-done = bf16[576,512]{1,0:T(8,128)(2,1)} async-done(((bf16[4608,512]{1,0:T(8,128)(2,1)}), bf16[576,512]{1,0:T(8,128)(2,1)}) %reduce-scatter.21.cloned.1.call-update) | async-done | bytes 589840 | tf_op jit(solution)/shard_map/reduce_scatter | solution.py:256
  1074.4 57.6 %reduce-scatter.19.cloned.1.call-done = bf16[576,512]{1,0:T(8,128)(2,1)} async-done(((bf16[4608,512]{1,0:T(8,128)(2,1)}), bf16[576,512]{1,0:T(8,128)(2,1)}) %reduce-scatter.19.cloned.1.call-update) | async-done | bytes 589840 | tf_op jit(solution)/shard_map/reduce_scatter | solution.py:256
  1140.3 150.2 %all-reduce.41.cloned.1.call-done = (f32[1,3,1152,128]{3,2,1,0:T(8,128)}, f32[1,3,1152,128]{3,2,1,0:T(8,128)}, f32[1,128,2048]{2,1,0:T(8,128)}, f32[1,128,2048]{2,1,0:T(8,128)}) async-done(((f32[1,3,1152,128]{3,2,1,0:T(8,128)}, f32[1,3,1152,128]{3,2,1,0:T(8,128)}, f32[1,128,2048]{2,1,0:T(8,128)}, f32[1,128,2048]{2,1,0:T(8,128)}), (f32[1,3,1152,128]{3,2,1,0:T(8,128)}, f32[1,3,1152,128]{3,2,1,0:T(8,128)}, ...) | async-done | bytes 5636112 | tf_op jit(solution)/shard_map/psum | solution.py:356
  1295.8 95.0 %all-reduce.43.cloned.1.call-done = (bf16[1,256,512]{2,1,0:T(8,128)(2,1)}, bf16[1,256,512]{2,1,0:T(8,128)(2,1)}, bf16[1,576,512]{2,1,0:T(8,128)(2,1)}, bf16[1,57...) async-done(((bf16[1,256,512]{2,1,0:T(8,128)(2,1)}, ...) | async-done | bytes 2359312 | tf_op jit(solution)/shard_map/psum | solution.py:267
  (745 shorter events, 394.1 us)
Async XLA Ops:
  7.2 668.1 %all-reduce.37.cloned.1.call-start = ((), (), s32[]{:S(2)}) async-start(), calls=%async_computation.16 | async-start | bytes 1572864
  21.7 132.5 %copy-start.4 = (f32[768,512]{1,0:T(8,128)}, f32[768,512]{1,0:T(8,128)S(1)}, u32[]{:S(2)}) copy-start(f32[768,512]{1,0:T(8,128)S(1)} %get-tuple-element.196) | copy-start | bytes 4718596
  66.9 81.6 %collective-permute-start = (bf16[48,1,8,512]{3,2,1,0:T(8,128)(2,1)}, bf16[48,1,8,512]{3,2,1,0:T(8,128)(2,1)}, u32[]{:S(2)}, u32[]{:S(2)}) collective-permute-start(bf16[48,1,8,512]{3,2,1,0:T(8,128)(2,1)} %get-tuple-element.158), channel_id=1, source_target_pairs={{0,1},{1,2},{2,3},{4,5},{5,6},{6,7},{8,9},{9,10},{10,11},{12,13},{... | collective-permute-start | bytes 1179656 | tf_op jit(solution)/shard_map/ppermute | solution.py:14
  71.1 77.4 %collective-permute-start.1 = (bf16[48,1,8,512]{3,2,1,0:T(8,128)(2,1)}, bf16[48,1,8,512]{3,2,1,0:T(8,128)(2,1)}, u32[]{:S(2)}, u32[]{:S(2)}) collective-permute-start(bf16[48,1,8,512]{3,2,1,0:T(8,128)(2,1)} %get-tuple-element.159), channel_id=1, source_target_pairs={{1,0},{2,1},{3,2},{5,4},{6,5},{7,6},{9,8},{10,9},{11,10},{13,12},{... | collective-permute-start | bytes 1179656 | tf_op jit(solution)/shard_map/ppermute | solution.py:17
  341.7 11.5 collective-permute-start.2
  345.6 11.7 collective-permute-start.3
  350.8 102.9 %copy-start.66 = (bf16[48,2,8,128]{3,2,1,0:T(8,128)(2,1)}, bf16[48,2,8,128]{3,2,1,0:T(8,128)(2,1)S(1)}, u32[]{:S(2)}) copy-start(bf16[48,2,8,128]{3,2,1,0:T(8,128)(2,1)S(1)} %fusion.110) | copy-start | bytes 589828
  588.6 22.6 %collective-permute-start.4 = (bf16[48,1,8,512]{3,2,1,0:T(8,128)(2,1)}, bf16[48,1,8,512]{3,2,1,0:T(8,128)(2,1)S(1)}, u32[]{:S(2)}, u32[]{:S(2)}) collective-permute-start(bf16[48,1,8,512]{3,2,1,0:T(8,128)(2,1)} %get-tuple-element.150), channel_id=1, source_target_pairs={{0,1},{1,2},{2,3},{4,5},{5,6},{6,7},{8,9},{9,10},{10,11},{12,13},{... | collective-permute-start | bytes 1179656 | tf_op jit(solution)/shard_map/ppermute | solution.py:14
  591.3 19.9 %collective-permute-start.5 = (bf16[48,1,8,512]{3,2,1,0:T(8,128)(2,1)}, bf16[48,1,8,512]{3,2,1,0:T(8,128)(2,1)S(1)}, u32[]{:S(2)}, u32[]{:S(2)}) collective-permute-start(bf16[48,1,8,512]{3,2,1,0:T(8,128)(2,1)} %get-tuple-element.151), channel_id=1, source_target_pairs={{1,0},{2,1},{3,2},{5,4},{6,5},{7,6},{9,8},{10,9},{11,10},{13,12},{... | collective-permute-start | bytes 1179656 | tf_op jit(solution)/shard_map/ppermute | solution.py:17
  611.1 151.0 %all-reduce.39.cloned.1.call-start = ((), (), s32[]{:S(2)}) async-start(), calls=%async_computation.17 | async-start | bytes 1572864
  719.2 285.5 %reduce-scatter.29.cloned.1.call-start = ((), (), s32[]{:S(2)}) async-start(), calls=%async_computation.15 | async-start | bytes 589824 | tf_op jit(solution)/shard_map/reduce_scatter | solution.py:262
  723.4 281.4 %reduce-scatter.27.cloned.1.call-start = ((), (), s32[]{:S(2)}) async-start(), calls=%async_computation.14 | async-start | bytes 589824 | tf_op jit(solution)/shard_map/reduce_scatter | solution.py:262
  767.5 237.3 %reduce-scatter.25.cloned.1.call-start = ((), (), s32[]{:S(2)}) async-start(), calls=%async_computation.13 | async-start | bytes 2359296 | tf_op jit(solution)/shard_map/reduce_scatter | solution.py:259
  772.9 231.9 %reduce-scatter.17.cloned.1.call-start = ((), (), s32[]{:S(2)}) async-start(), calls=%async_computation.9 | async-start | bytes 2359296 | tf_op jit(solution)/shard_map/reduce_scatter | solution.py:253
  784.9 219.9 %reduce-scatter.23.cloned.1.call-start = ((), (), s32[]{:S(2)}) async-start(), calls=%async_computation.12 | async-start | bytes 2359296 | tf_op jit(solution)/shard_map/reduce_scatter | solution.py:259
  881.3 11.1 collective-permute-start.6
  884.5 12.1 collective-permute-start.7
  889.3 127.8 %reduce-scatter.15.cloned.1.call-start = ((), (), s32[]{:S(2)}) async-start(), calls=%async_computation.8 | async-start | bytes 2359296 | tf_op jit(solution)/shard_map/reduce_scatter | solution.py:253
  954.9 119.5 %reduce-scatter.21.cloned.1.call-start = ((), (), s32[]{:S(2)}) async-start(), calls=%async_computation.11 | async-start | bytes 5308416 | tf_op jit(solution)/shard_map/reduce_scatter | solution.py:256
  963.7 168.3 %reduce-scatter.19.cloned.1.call-start = ((), (), s32[]{:S(2)}) async-start(), calls=%async_computation.10 | async-start | bytes 5308416 | tf_op jit(solution)/shard_map/reduce_scatter | solution.py:256
  978.5 312.1 %all-reduce.41.cloned.1.call-start = ((), (), s32[]{:S(2)}) async-start(), calls=%async_computation.18 | async-start | bytes 11272192 | tf_op jit(solution)/shard_map/psum | solution.py:356
  997.5 393.3 %all-reduce.43.cloned.1.call-start = ((), (), s32[]{:S(2)}) async-start(), calls=%async_computation.19 | async-start | bytes 4718592 | tf_op jit(solution)/shard_map/psum | solution.py:267
  998.6 134.1 %copy-start.63 = (bf16[48,2,8,128]{3,2,1,0:T(8,128)(2,1)S(1)}, bf16[48,2,8,128]{3,2,1,0:T(8,128)(2,1)}, u32[]{:S(2)}) copy-start(bf16[48,2,8,128]{3,2,1,0:T(8,128)(2,1)} %copy-done.62) | copy-start | bytes 589828
  998.6 134.1 %copy-start.76 = (bf16[2,2048,128]{2,1,0:T(8,128)(2,1)S(1)}, bf16[2,2048,128]{2,1,0:T(8,128)(2,1)}, u32[]{:S(2)}) copy-start(bf16[2,2048,128]{2,1,0:T(8,128)(2,1)} %param.20) | copy-start | bytes 3145732
  (178 other events, 1783.5 us)
Sparse Core Ops, SparseCore 0:
  611.3 46.2 all-reduce.36
  719.4 42.7 all-reduce.38
  765.2 33.4 reduce-scatter.28
  801.9 34.2 reduce-scatter.26
  839.4 41.8 reduce-scatter.24
  885.3 41.1 reduce-scatter.16
  930.4 41.1 reduce-scatter.22
  975.8 41.2 reduce-scatter.14
  1020.5 53.8 reduce-scatter.20
  1078.1 53.8 reduce-scatter.18
  1138.7 151.7 all-reduce.40
  1293.4 97.4 all-reduce.42
where the time goes:
time: 1410 us
  blocking collectives  527 us (37%)
  waiting for transfers between devices  425 us (30%)
  matrix products  201 us (14%)
  other arithmetic  117 us (8%)
  local copies, waits for them, and re-layouts  95.6 us (7%)
  starting transfers between devices  20.4 us (1%)
  between operations  18.9 us (1%)
    psum x6, blocking collectives, norm_back(): lax.psum((grad_sum, grad_squares), ('dp', 'space'))  244 us
    psum x6, blocking collectives, norm_stats(): lax.psum((jnp.sum(masked, axis=0), jnp.sum(masked * values, axis=0), jnp....  241 us
    psum x1, waiting for transfers between devices, block_backward(): lax.psum((grad_convs, grad_expand, grad_gain, grad_bias), ('dp', 'space'))  150 us
    reduce_scatter x2, waiting for transfers between devices, sum_weights(): lax.psum_scatter(grad_conv.astype(jnp.bfloat16), 'dp', scatter_dimension=...  115 us
    psum x1, waiting for transfers between devices, sum_weights(): lax.psum(partial_sums[0].astype(jnp.bfloat16), 'space').astype(jnp.float32)  95 us
    dot_general x24, matrix products, matmul_plain(): return jnp.dot(left_side, right_side, preferred_element_type=jnp.float32)  90 us
    dot_general x16, matrix products, matmul_inner(): lax.dot_general(left_side, right_side, (((0,), (0,)), ((), ())), preferre...  62.6 us
    dot_general x8, matrix products, matmul_back(): lax.dot_general(left_side, right_side, (((1,), (1,)), ((), ())), preferre...  48.8 us
  transfers between devices with their start and end apart: 20, of which 10 were waited for; matrix products, arithmetic and copies ran while one was open for 15% of the time, Pallas kernels for 0%

commit v1 on v0

v1 whole, which is shorter than its diff:
```python
import jax
import jax.numpy as jnp
from jax import lax
from jax.sharding import PartitionSpec as P

norm_eps = 1e-05
both = ("dp", "space")
f32 = jnp.float32
bf16 = jnp.bfloat16


def mm(left, right):
    return jnp.dot(left, right, preferred_element_type=f32)


def mm_inner(left, right):
    return lax.dot_general(left, right, (((0,), (0,)), ((), ())), preferred_element_type=f32)


def mm_back(left, right):
    return lax.dot_general(left, right, (((1,), (1,)), ((), ())), preferred_element_type=f32)


def all_sum(block):
    count = lax.axis_size("dp") * lax.axis_size("space")
    spread = jnp.broadcast_to(block[None], (count,) + block.shape)
    return jnp.sum(lax.all_to_all(spread, both, 0, 0), axis=0)


def sum_pair(first, second):
    width = first.shape[0]
    packed = all_sum(jnp.concatenate([first, second]).reshape(-1, 128)).reshape(2, width)
    return packed[0], packed[1]


def halo_rows(block):
    count = lax.axis_size("space")
    forward = [(i, i + 1) for i in range(count - 1)]
    backward = [(i + 1, i) for i in range(count - 1)]
    rows = block.shape[1]
    low = lax.ppermute(block[:, rows - 1 : rows], "space", forward)
    high = lax.ppermute(block[:, :1], "space", backward)
    return low, high


def tap_stack(padded, num_rows, num_cols, flipped):
    windows = []
    for tap_row in range(3):
        for tap_col in range(3):
            first_row = 2 - tap_row if flipped else tap_row
            first_col = 2 - tap_col if flipped else tap_col
            windows.append(
                padded[:, first_row : first_row + num_rows, first_col : first_col + num_cols, :]
            )
    stacked = jnp.concatenate(windows, axis=-1)
    return stacked.reshape(-1, stacked.shape[-1])


def pad_columns(values):
    return jnp.pad(values, ((0, 0), (0, 0), (1, 1), (0, 0)))


def full_taps(values, flipped):
    padded = jnp.pad(values, ((0, 0), (1, 1), (1, 1), (0, 0)))
    return tap_stack(padded, values.shape[1], values.shape[2], flipped)


def flip_weight(weight, channels_in):
    tap_blocks = weight.reshape(9, channels_in, -1)
    return jnp.swapaxes(tap_blocks, 1, 2).reshape(-1, channels_in)


def pool_map(values, factor):
    frames, height, map_width, channels = values.shape
    shaped = values.reshape(frames, height // factor, factor, map_width // factor, factor, channels)
    return jnp.mean(shaped, axis=(2, 4))


def expand_map(values, factor):
    return jnp.repeat(jnp.repeat(values, factor, axis=1), factor, axis=2)


def norm_scale(sum_values, sum_squares, total, gain, bias):
    mean = sum_values / total
    variance = sum_squares / total - mean * mean
    inverse = lax.rsqrt(variance + norm_eps)
    scale = inverse * gain
    return mean, inverse, scale, bias - mean * scale


def back_terms(sums, total, mean, inverse, scale):
    sum_bias, sum_gain = sums
    factor = -scale / total
    return factor * (sum_bias - inverse * sum_gain * mean), factor * inverse * sum_gain


def silu_slope(value):
    sig = jax.nn.sigmoid(value)
    return sig * (1.0 + value * (1.0 - sig))


group_size = 16


def to_frames(own_rows):
    space = lax.axis_size("space")
    frames, rows, cols, channels = own_rows.shape
    padded = jnp.pad(own_rows, ((0, space * group_size - frames), (0, 0), (0, 0), (0, 0))) if space * group_size > frames else own_rows
    return lax.all_to_all(padded, "space", 0, 1, tiled=True)


def to_rows(full_rows, frames):
    return lax.all_to_all(full_rows, "space", 1, 0, tiled=True)[:frames]


def gate_forward(reduce_rows, next_group, convs_layer):
    reduced = reduce_rows.shape[3]
    shifted = jnp.take(reduce_rows, next_group, axis=0)
    diff_taps = full_taps(shifted, False)
    difference = mm(diff_taps, convs_layer[0]).reshape(reduce_rows.shape) - reduce_rows.astype(f32)
    coarse_two = pool_map(difference, 2).astype(bf16)
    coarse_four = pool_map(difference, 4).astype(bf16)
    two_taps = full_taps(coarse_two, False)
    four_taps = full_taps(coarse_four, False)
    conv_two = mm(two_taps, convs_layer[1]).reshape(coarse_two.shape)
    conv_four = mm(four_taps, convs_layer[2]).reshape(coarse_four.shape)
    summed = difference + expand_map(conv_two, 2) + expand_map(conv_four, 4)
    return summed.astype(bf16), (diff_taps, two_taps, four_taps)


def gate_backward(grad_low, gate_kept, convs_layer, next_group):
    diff_taps, two_taps, four_taps = gate_kept
    reduced = grad_low.shape[3]
    grad_summed = grad_low.astype(f32)
    grad_two = (pool_map(grad_summed, 2) * 4.0).astype(bf16)
    grad_four = (pool_map(grad_summed, 4) * 16.0).astype(bf16)
    weight_two = mm_inner(two_taps, grad_two.reshape(-1, reduced))
    weight_four = mm_inner(four_taps, grad_four.reshape(-1, reduced))
    back_two = mm(full_taps(grad_two, True), flip_weight(convs_layer[1], reduced)).reshape(
        grad_two.shape
    )
    back_four = mm(full_taps(grad_four, True), flip_weight(convs_layer[2], reduced)).reshape(
        grad_four.shape
    )
    grad_diff = grad_summed + expand_map(back_two, 2) / 4.0 + expand_map(back_four, 4) / 16.0
    grad_diff_low = grad_diff.astype(bf16)
    weight_diff = mm_inner(diff_taps, grad_diff_low.reshape(-1, reduced))
    back_shift = mm(full_taps(grad_diff_low, True), flip_weight(convs_layer[0], reduced)).reshape(
        grad_low.shape
    )
    chosen = (next_group[None, :] == jnp.arange(group_size)[:, None]).astype(f32)
    grad_rows = jnp.einsum("ef,fhwc->ehwc", chosen, back_shift) - grad_diff
    return grad_rows.astype(bf16), jnp.stack([weight_diff, weight_two, weight_four], axis=0)


def halve(parts, axis_name, bit):
    index = lax.axis_index(axis_name)
    count = lax.axis_size(axis_name)
    mine = (index // bit) % 2
    kept = lax.dynamic_index_in_dim(parts, mine, 0, keepdims=False)
    sent = lax.dynamic_index_in_dim(parts, 1 - mine, 0, keepdims=False)
    got = lax.ppermute(sent, axis_name, [(i, i ^ bit) for i in range(count)])
    return (kept.astype(f32) + got.astype(f32)).astype(bf16)


def chain_sum(own):
    count = lax.axis_size("space")
    index = lax.axis_index("space")
    low = jnp.zeros_like(own)
    high = jnp.zeros_like(own)
    total_low = own
    total_high = own
    for step in range(1, count):
        got_low = lax.ppermute(total_low, "space", [(step - 1, step)])
        got_high = lax.ppermute(total_high, "space", [(count - step, count - step - 1)])
        low = low + got_low
        high = high + got_high
        total_low = (own.astype(f32) + low.astype(f32)).astype(bf16)
        total_high = (own.astype(f32) + high.astype(f32)).astype(bf16)
    return own.astype(f32) + low.astype(f32) + high.astype(f32)


def reduce_fast(grad):
    count = lax.axis_size("dp")
    bits = []
    bit = 2
    while bit < count:
        bits.append(bit)
        bit *= 2
    rows, cols = grad.shape[1:]
    order = [1] + bits
    view = grad.reshape((2,) * len(order) + (rows, cols))

    def along(parts, current, chosen):
        at = len(current) - 1 - current.index(chosen)
        return jnp.moveaxis(parts, at, 0), [b for b in current if b != chosen]

    parts, current = along(view, order, 1)
    parts = halve(parts, "dp", 1)
    outs = []
    half = len(bits) // 2
    for which, sequence in enumerate((bits, bits[half:] + bits[:half])):
        piece = parts[..., which * (rows // 2) : (which + 1) * (rows // 2), :]
        left = current
        for chosen in sequence:
            piece, left = along(piece, left, chosen)
            piece = halve(piece, "dp", chosen)
        outs.append(chain_sum(piece))
    return jnp.concatenate(outs, axis=0)


def reduce_slow(grad):
    part = lax.psum_scatter(grad, "dp", scatter_dimension=0, tiled=False)
    return lax.psum(part, "space").astype(f32)


def chunks(grad):
    count = lax.axis_size("dp")
    return grad.astype(bf16).reshape(count, -1, 512)


def body(
    clip_maps,
    next_frame,
    valid_rows,
    proj_in,
    conv_mid,
    proj_out,
    gate_reduce,
    gate_convs,
    gate_expand,
    norm_gain,
    norm_bias,
    out_grad,
):
    frames, rows_dev, map_width, channels = clip_maps.shape
    middle = proj_in.shape[2]
    reduced = gate_reduce.shape[2]
    mask_maps = valid_rows.astype(f32)[:, :, None, None]
    mask_rows = jnp.broadcast_to(mask_maps, (frames, rows_dev, map_width, 1)).reshape(-1, 1)
    mask_low, mask_high = halo_rows(mask_maps)
    group_base = lax.axis_index("dp") * frames + lax.axis_index("space") * group_size
    padded_next = jnp.pad(next_frame, (0, lax.axis_size("space") * group_size - frames))
    own_next = lax.dynamic_slice_in_dim(
        padded_next, lax.axis_index("space") * group_size, group_size
    )
    next_group = jnp.clip(own_next - group_base, 0, group_size - 1)
    flat = (-1, middle)
    maps4 = (frames, rows_dev, map_width, middle)

    def forward(layer, values, low_in, total):
        gains, biases = norm_gain[layer], norm_bias[layer]
        first = mm(low_in, proj_in[layer])
        reduce_rows = mm(low_in, gate_reduce[layer]).astype(bf16).reshape(
            frames, rows_dev, map_width, reduced
        ) * mask_maps.astype(bf16)
        first_low, first_high = halo_rows(first.astype(bf16).reshape(maps4))
        own_sum, own_square = jnp.sum(first, axis=0), jnp.sum(first * first, axis=0)
        if total is None:
            packed = jnp.concatenate(
                [own_sum, own_square, jnp.full((128,), jnp.sum(mask_rows))]
            ).reshape(-1, 128)
            packed = all_sum(packed).reshape(-1)
            sums_one = packed[:middle], packed[middle : 2 * middle]
            total = packed[2 * middle]
        else:
            sums_one = sum_pair(own_sum, own_square)
        full_rows = to_frames(reduce_rows)
        gate_full, gate_kept = gate_forward(full_rows, next_group, gate_convs[layer])
        gate_own = to_rows(gate_full, frames).reshape(-1, reduced)
        norm_one = norm_scale(*sums_one, total, gains[:middle], biases[:middle])

        def activate(block, scales, mask):
            return (jax.nn.silu(block * scales[2] + scales[3]) * mask).astype(bf16)

        hidden_one = jnp.concatenate(
            [
                activate(first_low.astype(f32), norm_one, mask_low),
                activate(first.reshape(maps4), norm_one, mask_maps),
                activate(first_high.astype(f32), norm_one, mask_high),
            ],
            axis=1,
        )
        mid_taps = tap_stack(pad_columns(hidden_one), rows_dev, map_width, False)
        second = mm(mid_taps, conv_mid[layer])
        masked = second * mask_rows
        sums_two = sum_pair(jnp.sum(masked, axis=0), jnp.sum(masked * second, axis=0))
        norm_two = norm_scale(
            *sums_two, total, gains[middle : 2 * middle], biases[middle : 2 * middle]
        )
        hidden_two = activate(second, norm_two, mask_rows)
        third = mm(hidden_two, proj_out[layer])
        sums_three = sum_pair(jnp.sum(third, axis=0), jnp.sum(third * third, axis=0))
        norm_three = norm_scale(*sums_three, total, gains[2 * middle :], biases[2 * middle :])
        second_halo = halo_rows(second.astype(bf16).reshape(maps4))
        branch = third * norm_three[2] + norm_three[3]
        gate_sig = jax.nn.sigmoid(mm(gate_own, gate_expand[layer]))
        summed = values + branch * gate_sig
        out = jax.nn.silu(summed) * mask_rows
        kept = (
            low_in,
            first,
            norm_one,
            mid_taps,
            second,
            second_halo,
            norm_two,
            hidden_two,
            third,
            norm_three,
            gate_own,
            gate_kept,
            summed,
            branch,
            gate_sig,
        )
        return out, kept, total

    def backward(layer, kept, grad_out, total):
        (
            low_in,
            first,
            norm_one,
            mid_taps,
            second,
            second_halo,
            norm_two,
            hidden_two,
            third,
            norm_three,
            gate_own,
            gate_kept,
            summed,
            branch,
            gate_sig,
        ) = kept
        grad_in = grad_out * mask_rows * silu_slope(summed)
        grad_branch = grad_in * gate_sig
        grad_pre = (grad_branch * branch * (1.0 - gate_sig)).astype(bf16)
        sums_three = sum_pair(
            jnp.sum(grad_branch, axis=0),
            jnp.sum(grad_branch * ((third - norm_three[0]) * norm_three[1]), axis=0),
        )
        grad_gate = to_frames(
            mm_back(grad_pre, gate_expand[layer])
            .astype(bf16)
            .reshape(frames, rows_dev, map_width, reduced)
        )
        grad_rows, grad_convs = gate_backward(grad_gate, gate_kept, gate_convs[layer], next_group)
        grad_rows = (to_rows(grad_rows, frames) * mask_maps.astype(bf16)).reshape(-1, reduced)
        grad_expand = mm_inner(gate_own, grad_pre)
        grad_reduce = mm_inner(low_in, grad_rows)

        def spread(grad, values, scales, terms, mask):
            return (grad + mask * (terms[0] + terms[1] * values)).astype(bf16)

        terms = back_terms(sums_three, total, *norm_three[:3])
        grad_third = spread(grad_branch * norm_three[2], third, norm_three, terms, mask_rows)
        grad_out_w = mm_inner(hidden_two, grad_third)
        grad_norm = mm_back(grad_third, proj_out[layer]) * (
            silu_slope(second * norm_two[2] + norm_two[3]) * mask_rows
        )
        part_two = grad_norm * norm_two[2]
        part_low, part_high = halo_rows(part_two.astype(bf16).reshape(maps4))
        sums_two = sum_pair(
            jnp.sum(grad_norm, axis=0),
            jnp.sum(grad_norm * ((second - norm_two[0]) * norm_two[1]), axis=0),
        )
        terms = back_terms(sums_two, total, *norm_two[:3])
        grad_second = spread(part_two, second, norm_two, terms, mask_rows)
        grad_ext = jnp.concatenate(
            [
                spread(part_low.astype(f32), second_halo[0].astype(f32), norm_two, terms, mask_low),
                grad_second.reshape(maps4),
                spread(
                    part_high.astype(f32), second_halo[1].astype(f32), norm_two, terms, mask_high
                ),
            ],
            axis=1,
        )
        grad_norm = mm(
            tap_stack(pad_columns(grad_ext), rows_dev, map_width, True),
            flip_weight(conv_mid[layer], middle),
        ) * (silu_slope(first * norm_one[2] + norm_one[3]) * mask_rows)
        sums_one = sum_pair(
            jnp.sum(grad_norm, axis=0),
            jnp.sum(grad_norm * ((first - norm_one[0]) * norm_one[1]), axis=0),
        )
        grad_conv = mm_inner(mid_taps, grad_second)
        terms = back_terms(sums_one, total, *norm_one[:3])
        grad_first = spread(grad_norm * norm_one[2], first, norm_one, terms, mask_rows)
        grad_proj = mm_inner(low_in, grad_first)
        grad_in = (
            grad_in
            + mm_back(grad_first, proj_in[layer])
            + mm_back(grad_rows, gate_reduce[layer])
        )
        large = (grad_proj, grad_conv, grad_out_w, grad_reduce)
        small = (
            grad_convs,
            grad_expand,
            jnp.concatenate([sums_one[1], sums_two[1], sums_three[1]]),
            jnp.concatenate([sums_one[0], sums_two[0], sums_three[0]]),
        )
        return grad_in, large, small

    start = clip_maps.astype(f32).reshape(-1, channels) * mask_rows
    mid_out, kept_zero, total_rows = forward(0, start, start.astype(bf16), None)
    total = total_rows * 1.0
    final, kept_one, total = forward(1, mid_out, mid_out.astype(bf16), total)
    final_maps = final.astype(bf16).reshape(clip_maps.shape)
    grad = out_grad.astype(f32).reshape(-1, channels)
    grad, large_one, small_one = backward(1, kept_one, grad, total)
    sum_one = reduce_slow(jnp.concatenate([chunks(g) for g in large_one], axis=1))
    grad, large_zero, small_zero = backward(0, kept_zero, grad, total)
    sum_zero = jnp.concatenate(
        [
            reduce_fast(jnp.concatenate([chunks(g) for g in large_zero[:2]], axis=1)),
            reduce_slow(jnp.concatenate([chunks(g) for g in large_zero[2:]], axis=1)),
        ],
        axis=0,
    )
    grad_maps = (grad * mask_rows).astype(bf16).reshape(clip_maps.shape)

    def unpack(position):
        pieces = []
        for summed, large in ((sum_zero, large_zero), (sum_one, large_one)):
            offset = 0
            for at in range(position):
                offset += large[at].size // (lax.axis_size("dp") * 512)
            size = large[position].size // (lax.axis_size("dp") * 512)
            pieces.append(summed[offset : offset + size].reshape(-1, large[position].shape[1]))
        return jnp.stack(pieces)

    convs, expand = lax.psum(
        (
            jnp.stack([small_zero[0], small_one[0]]).astype(bf16),
            jnp.stack([small_zero[1], small_one[1]]).astype(bf16),
        ),
        both,
    )
    return (
        final_maps,
        grad_maps,
        unpack(0),
        unpack(1),
        unpack(2),
        unpack(3),
        convs.astype(f32),
        expand.astype(f32),
        jnp.stack([small_zero[2], small_one[2]]),
        jnp.stack([small_zero[3], small_one[3]]),
    )


def solution(mesh):
    maps = P("dp", "space", None, None)
    in_specs = (maps, P("dp"), P("dp", "space")) + (P(),) * 8 + (maps,)
    out_specs = (maps, maps) + (P(None, "dp", None),) * 4 + (P(),) * 4
    return jax.shard_map(body, mesh=mesh, in_specs=in_specs, out_specs=out_specs, check_vma=False)
```

time: 1410 us -> 805 us (0.57)
  blocking collectives: 527 us -> 0 us
  waiting for transfers between devices: 425 us -> 217 us
  starting transfers between devices: 20.4 us -> 150 us
  matrix products: 201 us -> 169 us
  local copies, waits for them, and re-layouts: 95.6 us -> 117 us
    psum x12 -> x0, blocking collectives: 484 us -> none  [the longest x6 244 us: norm_back(): lax.psum((grad_sum, grad_squares), ('dp', 'space'))]
    psum x2, waiting for transfers between devices: 245 us -> 39.7 us  [the longest x1 34.2 us: reduce_slow(): return lax.psum(part, 'space').astype(f32)]
    reduce_scatter x8 -> x2, waiting for transfers between devices: 127 us -> 0.04 us  [reduce_slow(): part = lax.psum_scatter(grad, 'dp', scatter_dimension=0, tiled=False)]
    ppermute x8 -> x31, waiting for transfers between devices: 13.7 us -> 109 us  [the longest x6 44.8 us: chain_sum(): lax.ppermute(total_high, 'space', [(count - step, count - step - 1)])]
    all_to_all x0 -> x20, starting transfers between devices: none -> 87.3 us  [the longest x12 52 us: all_sum(): return jnp.sum(lax.all_to_all(spread, both, 0, 0), axis=0)]
    all_to_all x0 -> x20, waiting for transfers between devices: none -> 68.2 us  [the longest x12 41.1 us: all_sum(): return jnp.sum(lax.all_to_all(spread, both, 0, 0), axis=0)]
    all_gather x2 -> x0, blocking collectives: 43.1 us -> none  [block_forward(): rows_full = lax.all_gather(reduce_rows, 'space', axis=1, tiled=True)]
    ppermute x8 -> x31, starting transfers between devices: 19.3 us -> 62.2 us  [the longest x7 28.8 us: halo_rows(): low = lax.ppermute(block[:, rows - 1:rows], 'space', forward)]
  transfers between devices with their start and end apart: 20 -> 55, of which waited for: 10 -> 26; matrix products, arithmetic and copies ran while one was open for 15% -> 30% of each run, Pallas kernels for 0% -> 0%
where the time goes in v1:
time: 805 us; the launch traced here: 798 us
  waiting for transfers between devices  217 us (27%)
  matrix products  169 us (21%)
  starting transfers between devices  150 us (19%)
  other arithmetic  125 us (16%)
  local copies, waits for them, and re-layouts  117 us (15%)
  between operations  19.6 us (2%)
    dot_general x22, matrix products, mm(): return jnp.dot(left, right, preferred_element_type=f32)  81.2 us
    all_to_all x12, starting transfers between devices, all_sum(): return jnp.sum(lax.all_to_all(spread, both, 0, 0), axis=0)  52 us
    dot_general x16, matrix products, mm_inner(): lax.dot_general(left, right, (((0,), (0,)), ((), ())), preferred_element_...  46.2 us
    ppermute x6, waiting for transfers between devices, chain_sum(): lax.ppermute(total_high, 'space', [(count - step, count - step - 1)])  44.8 us
    ppermute x5, waiting for transfers between devices, halve(): got = lax.ppermute(sent, axis_name, [(i, i ^ bit) for i in range(count)])  44.4 us
    all_to_all x12, waiting for transfers between devices, all_sum(): return jnp.sum(lax.all_to_all(spread, both, 0, 0), axis=0)  41.1 us
    dot_general x8, matrix products, mm_back(): lax.dot_general(left, right, (((1,), (1,)), ((), ())), preferred_element_...  36.3 us
    psum x1, waiting for transfers between devices, reduce_slow(): return lax.psum(part, 'space').astype(f32)  34.2 us
  transfers between devices with their start and end apart: 55, of which 26 were waited for; matrix products, arithmetic and copies ran while one was open for 30% of the time, Pallas kernels for 0%

profile of v1, /device:TPU:0, one launch (start us, length us, event | category | flops | bytes accessed | tf_op | source)
XLA Modules:
  0.0 798.1 jit_solution(5735009879218088765)
XLA Ops:
  24.0 6.9 all-to-all-start
  71.6 10.0 %multiply_reduce_fusion.5 = (f32[512]{0:T(512)S(1)}, f32[512]{0:T(512)S(1)}, f32[768,512]{1,0:T(8,128)}) fusion(f32[768]{0:T(1024)S(1)} %broadcast_in_dim.76, bf16[768,4608]{1,0:T(8,128)(2,1)S(1)} %bitcast.789, bf16[2,4608,512]{2,1,0:T(8,128)(2,1)} %param.18), kind=kOutput, calls=%fused_computation.88 | convolution fusion | flops 3625450496 | bytes 13376512 | tf_op jit(solution)/shard_map/dot_general | solution.py:13
  87.3 7.1 all-to-all-done.1
  99.6 6.8 fusion.148
  128.8 9.7 %fusion.144 = (bf16[768,2048]{1,0:T(8,128)(2,1)S(1)}, f32[768,2048]{1,0:T(8,128)}, bf16[768,2048]{1,0:T(8,128)(2,1)}, f32[768,2048]{1,0:T(8,128)}) fusion(f32[768]{0:T(1024)S(1)} %broadcast_in_dim.76, f32[2048]{0:T(1024)S(1)} %bitcast.815, f32[768,2048]{1,0:T(8,128)} %get-tuple-element.211, f32[2048]{0:T(1024)S(1)} %bitcast.780, ...), kind=kOutput, calls=%fused_computation.635 | convolution fusion | flops 427819008 | bytes 29051904 | tf_op jit(solution)/shard_map/dot_general | solution.py:13
  165.1 10.0 %all-to-all-done.8 = bf16[64,2,8,128]{3,2,1,0:T(8,128)(2,1)S(1)} async-done(((bf16[64,2,8,128]{3,2,1,0:T(8,128)(2,1)}), bf16[64,2,8,128]{3,2,1,0:T(8,128)(2,1)S(1)}, u32[]{:S(2)}, u32[]{:S(2)}) %all-to-all-start.8) | async-done | bytes 262176 | tf_op jit(solution)/shard_map/all_to_all | solution.py:109
  199.6 7.1 all-to-all-done.6
  212.0 6.8 fusion.147
  224.2 8.1 %fusion.162 = (bf16[1,4608,512]{2,1,0:T(8,128)(2,1)}, bf16[1,4608,512]{2,1,0:T(8,128)(2,1)}) fusion(bf16[2,4608,512]{2,1,0:T(8,128)(2,1)} %param.18), kind=kLoop, calls=%fused_computation.648 | loop fusion | bytes 18874368 | tf_op jit(solution)/shard_map/slice | solution.py:285
  232.4 6.7 copy.284
  246.4 16.4 %multiply_convert_fusion.2 = (bf16[768,2048]{1,0:T(8,128)(2,1)S(1)}, f32[768,2048]{1,0:T(8,128)}, f32[768,2048]{1,0:T(8,128)}, f32[768,2048]{1,0:T(8,128)}) fusion(f32[768,2048]{1,0:T(8,128)} %get-tuple-element.215, f32[2048]{0:T(1024)S(1)} %bitcast.884, f32[2048]{0:T(1024)S(1)} %bitcast.793, f32[768]{0:T(1024)S(1)} %broadcast_in_dim.76, ...), kind=kOutput, calls=%fused_computation.21 | convolution fusion | flops 445120512 | bytes 38489088 | tf_op jit(solution)/shard_map/dot_general | solution.py:13
  311.6 11.9 %all-to-all-done.10 = f32[32,32,128]{2,1,0:T(8,128)S(1)} async-done(((f32[32,32,128]{2,1,0:T(8,128)}), f32[32,32,128]{2,1,0:T(8,128)S(1)}, u32[]{:S(2)}, u32[]{:S(2)}) %all-to-all-start.10) | async-done | bytes 524320 | tf_op jit(solution)/shard_map/all_to_all | solution.py:27
  394.8 8.6 %convolution_convert_fusion = bf16[4608,512]{1,0:T(8,128)(2,1)} fusion(bf16[768,4608]{1,0:T(8,128)(2,1)} %bitcast.792, bf16[768,512]{1,0:T(8,128)(2,1)S(1)} %get-tuple-element.132), kind=kOutput, calls=%fused_computation.7 | convolution fusion | flops 3626237952 | bytes 12582912 | tf_op jit(solution)/shard_map/dot_general | solution.py:17
  410.2 13.7 %multiply_convert_fusion.1 = (bf16[768,2048]{1,0:T(8,128)(2,1)}, f32[768,2048]{1,0:T(8,128)}, f32[768,2048]{1,0:T(8,128)}) fusion(f32[768,2048]{1,0:T(8,128)} %get-tuple-element.212, f32[768,2048]{1,0:T(8,128)} %get-tuple-element.211, f32[2048]{0:T(1024)S(1)} %bitcast.816, f32[2048]{0:T(1024)S(1)} %bitcast.781, f32[768,2048]{1,0:T(8,128)} %get-tuple-element.95, ...), kind=kOutput, calls=%fused_computation.17 | convolution fusion | flops 430964736 | bytes 47926272 | tf_op jit(solution)/shard_map/dot_general | solution.py:21
  471.6 6.9 all-to-all-done.15
  480.9 9.8 %add_convert_fusion = (bf16[768,2048]{1,0:T(8,128)(2,1)S(1)}, bf16[768,2048]{1,0:T(8,128)(2,1)}) fusion(f32[768,2048]{1,0:T(8,128)} %get-tuple-element.211, f32[768,2048]{1,0:T(8,128)} %get-tuple-element.50, f32[2048]{0:T(1024)S(1)} %bitcast.812, f32[2048]{0:T(1024)S(1)} %bitcast.811, f32[2048]{0:T(1024)S(1)} %bitcast.782, f32[768]{0:T(1024)S(1)} %broadcast_in_dim.76, ...), kind=kLoop, calls=%fused_computation.18 | loop fusion | flops 18874368 | bytes 25193472 | tf_op jit(solution)/shard_map/convert_element_type | solution.py:355
  498.9 6.7 fusion.150
  532.9 6.7 pad_maximum_fusion
  565.7 9.5 %convolution_convert_fusion.1 = bf16[4608,512]{1,0:T(8,128)(2,1)} fusion(bf16[768,4608]{1,0:T(8,128)(2,1)} %bitcast.790, bf16[768,512]{1,0:T(8,128)(2,1)S(1)} %get-tuple-element.130), kind=kOutput, calls=%fused_computation.8 | convolution fusion | flops 3626237952 | bytes 12582912 | tf_op jit(solution)/shard_map/dot_general | solution.py:17
  599.5 35.9 %collective-permute-done.15 = bf16[2,416,512]{2,1,0:T(8,128)(2,1)} collective-permute-done((bf16[2,416,512]{2,1,0:T(8,128)(2,1)}, bf16[2,416,512]{2,1,0:T(8,128)(2,1)}, u32[]{:S(2)}, u32[]{:S(2)}) %collective-permute-start.15) | collective-permute-done | bytes 852000 | tf_op jit(solution)/shard_map/ppermute | solution.py:162
  667.0 7.5 collective-permute-done.25
  690.8 15.1 %collective-permute-done.22 = bf16[416,512]{1,0:T(8,128)(2,1)} collective-permute-done((bf16[416,512]{1,0:T(8,128)(2,1)}, bf16[416,512]{1,0:T(8,128)(2,1)}, u32[]{:S(2)}, u32[]{:S(2)}) %collective-permute-start.22) | collective-permute-done | bytes 426016 | tf_op jit(solution)/shard_map/ppermute | solution.py:175
  707.3 29.6 %collective-permute-done.30 = bf16[416,512]{1,0:T(8,128)(2,1)S(1)} collective-permute-done((bf16[416,512]{1,0:T(8,128)(2,1)S(1)}, bf16[416,512]{1,0:T(8,128)(2,1)S(1)}, u32[]{:S(2)}, u32[]{:S(2)}) %collective-permute-start.30) | collective-permute-done | bytes 426016 | tf_op jit(solution)/shard_map/ppermute | solution.py:175
  739.1 34.2 %all-reduce.28.cloned.1.call-done = (bf16[1152,512]{1,0:T(8,128)(2,1)}, bf16[320,512]{1,0:T(8,128)(2,1)}) async-done(((bf16[1152,512]{1,0:T(8,128)(2,1)}, bf16[320,512]{1,0:T(8,128)(2,1)}), (bf16[1152,512]{1,0:T(8,128)(2,1)}, bf16[320,512]{1,0:T(8,128)(2,1)})) %all-reduce.28.cloned.1.call-update) | async-done | bytes 1507344 | tf_op jit(solution)/shard_map/psum | solution.py:214
  (811 shorter events, 486.6 us)
Async XLA Ops:
  9.2 56.6 %collective-permute-start.1 = (f32[48,1,1,1]{0,1,3,2:T(1,128)}, f32[48,1,1,1]{0,1,3,2:T(1,128)S(1)}, u32[]{:S(2)}, u32[]{:S(2)}) collective-permute-start(f32[48,1,1,1]{0,1,3,2:T(1,128)} %get-tuple-element.204), channel_id=1, source_target_pairs={{0,1},{1,2},{2,3},{4,5},{5,6},{6,7},{8,9},{9,10},{10,11},{12,13},{... | collective-permute-start | bytes 584 | tf_op jit(solution)/shard_map/ppermute | solution.py:41
  14.1 51.7 %collective-permute-start.3 = (f32[48,1,1,1]{0,1,3,2:T(1,128)}, f32[48,1,1,1]{0,1,3,2:T(1,128)S(1)}, u32[]{:S(2)}, u32[]{:S(2)}) collective-permute-start(f32[48,1,1,1]{0,1,3,2:T(1,128)} %get-tuple-element.205), channel_id=1, source_target_pairs={{1,0},{2,1},{3,2},{5,4},{6,5},{7,6},{9,8},{10,9},{11,10},{13,12},{... | collective-permute-start | bytes 584 | tf_op jit(solution)/shard_map/ppermute | solution.py:42
  24.0 21.0 %all-to-all-start = ((f32[32,9,128]{2,1,0:T(8,128)}), f32[32,9,128]{2,1,0:T(8,128)S(1)}, u32[]{:S(2)}, u32[]{:S(2)}) async-start(f32[32,9,128]{2,1,0:T(8,128)} %broadcast_in_dim.79), calls=%async_computation | async-start | bytes 524288 | tf_op jit(solution)/shard_map/all_to_all | solution.py:27
  33.0 32.8 %collective-permute-start = (bf16[48,1,8,512]{3,2,1,0:T(8,128)(2,1)}, bf16[48,1,8,512]{3,2,1,0:T(8,128)(2,1)}, u32[]{:S(2)}, u32[]{:S(2)}) collective-permute-start(bf16[48,1,8,512]{3,2,1,0:T(8,128)(2,1)} %get-tuple-element.152), channel_id=1, source_target_pairs={{0,1},{1,2},{2,3},{4,5},{5,6},{6,7},{8,9},{9,10},{10,11},{12,13},{... | collective-permute-start | bytes 1179656 | tf_op jit(solution)/shard_map/ppermute | solution.py:41
  37.4 28.4 %collective-permute-start.2 = (bf16[48,1,8,512]{3,2,1,0:T(8,128)(2,1)}, bf16[48,1,8,512]{3,2,1,0:T(8,128)(2,1)}, u32[]{:S(2)}, u32[]{:S(2)}) collective-permute-start(bf16[48,1,8,512]{3,2,1,0:T(8,128)(2,1)} %get-tuple-element.153), channel_id=1, source_target_pairs={{1,0},{2,1},{3,2},{5,4},{6,5},{7,6},{9,8},{10,9},{11,10},{13,12},{... | collective-permute-start | bytes 1179656 | tf_op jit(solution)/shard_map/ppermute | solution.py:42
  107.3 19.3 %all-to-all-start.2 = ((f32[32,32,128]{2,1,0:T(8,128)}), f32[32,32,128]{2,1,0:T(8,128)}, u32[]{:S(2)}, u32[]{:S(2)}) async-start(f32[32,32,128]{2,1,0:T(8,128)} %broadcast_in_dim.82), calls=%async_computation.2 | async-start | bytes 1048576 | tf_op jit(solution)/shard_map/all_to_all | solution.py:27
  151.9 32.2 %collective-permute-start.4 = (bf16[48,1,8,512]{3,2,1,0:T(8,128)(2,1)}, bf16[48,1,8,512]{3,2,1,0:T(8,128)(2,1)}, u32[]{:S(2)}, u32[]{:S(2)}) collective-permute-start(bf16[48,1,8,512]{3,2,1,0:T(8,128)(2,1)} %get-tuple-element.150), channel_id=1, source_target_pairs={{0,1},{1,2},{2,3},{4,5},{5,6},{6,7},{8,9},{9,10},{10,11},{12,13},{... | collective-permute-start | bytes 1179656 | tf_op jit(solution)/shard_map/ppermute | solution.py:41
  156.3 27.8 %collective-permute-start.5 = (bf16[48,1,8,512]{3,2,1,0:T(8,128)(2,1)}, bf16[48,1,8,512]{3,2,1,0:T(8,128)(2,1)}, u32[]{:S(2)}, u32[]{:S(2)}) collective-permute-start(bf16[48,1,8,512]{3,2,1,0:T(8,128)(2,1)} %get-tuple-element.151), channel_id=1, source_target_pairs={{1,0},{2,1},{3,2},{5,4},{6,5},{7,6},{9,8},{10,9},{11,10},{13,12},{... | collective-permute-start | bytes 1179656 | tf_op jit(solution)/shard_map/ppermute | solution.py:42
  219.7 26.1 %all-to-all-start.7 = ((f32[32,32,128]{2,1,0:T(8,128)}), f32[32,32,128]{2,1,0:T(8,128)S(1)}, u32[]{:S(2)}, u32[]{:S(2)}) async-start(f32[32,32,128]{2,1,0:T(8,128)} %broadcast_in_dim.89), calls=%async_computation.7 | async-start | bytes 1048576 | tf_op jit(solution)/shard_map/all_to_all | solution.py:27
  305.3 18.3 %all-to-all-start.10 = ((f32[32,32,128]{2,1,0:T(8,128)}), f32[32,32,128]{2,1,0:T(8,128)S(1)}, u32[]{:S(2)}, u32[]{:S(2)}) async-start(f32[32,32,128]{2,1,0:T(8,128)} %broadcast_in_dim.94), calls=%async_computation.10 | async-start | bytes 1048576 | tf_op jit(solution)/shard_map/all_to_all | solution.py:27
  354.4 18.6 %collective-permute-start.6 = (bf16[48,1,8,512]{3,2,1,0:T(8,128)(2,1)}, bf16[48,1,8,512]{3,2,1,0:T(8,128)(2,1)}, u32[]{:S(2)}, u32[]{:S(2)}) collective-permute-start(bf16[48,1,8,512]{3,2,1,0:T(8,128)(2,1)} %get-tuple-element.146), channel_id=1, source_target_pairs={{0,1},{1,2},{2,3},{4,5},{5,6},{6,7},{8,9},{9,10},{10,11},{12,13},{... | collective-permute-start | bytes 1179656 | tf_op jit(solution)/shard_map/ppermute | solution.py:41
  460.4 18.2 %all-to-all-start.15 = ((f32[32,32,128]{2,1,0:T(8,128)}), f32[32,32,128]{2,1,0:T(8,128)}, u32[]{:S(2)}, u32[]{:S(2)}) async-start(f32[32,32,128]{2,1,0:T(8,128)} %broadcast_in_dim.101), calls=%async_computation.15 | async-start | bytes 1048576 | tf_op jit(solution)/shard_map/all_to_all | solution.py:27
  464.2 183.0 %all-reduce.26.cloned.1.call-start = ((), (), s32[]{:S(2)}) async-start(), calls=%async_computation.24 | async-start | bytes 5636096 | tf_op jit(solution)/shard_map/psum | solution.py:435
  510.5 177.1 %reduce-scatter.5.cloned.1.call-start = ((), (), s32[]{:S(2)}) async-start(), calls=%async_computation.23 | async-start | bytes 2949120 | tf_op jit(solution)/shard_map/reduce_scatter | solution.py:213
  512.4 175.2 %reduce-scatter.3.cloned.1.call-start = ((), (), s32[]{:S(2)}) async-start(), calls=%async_computation.22 | async-start | bytes 10616832 | tf_op jit(solution)/shard_map/reduce_scatter | solution.py:213
  522.5 18.4 %collective-permute-start.10 = (bf16[48,1,8,512]{3,2,1,0:T(8,128)(2,1)S(1)}, bf16[48,1,8,512]{3,2,1,0:T(8,128)(2,1)S(1)}, u32[]{:S(2)}, u32[]{:S(2)}) collective-permute-start(bf16[48,1,8,512]{3,2,1,0:T(8,128)(2,1)S(1)} %get-tuple-element.140), channel_id=1, source_target_pairs={{0,1},{1,2},{2,3},{4,5},{5,6},{6,7},{8,9},{9,10},{10,11},{12,13},{... | collective-permute-start | bytes 1179656 | tf_op jit(solution)/shard_map/ppermute | solution.py:41
  526.8 16.6 %collective-permute-start.11 = (bf16[48,1,8,512]{3,2,1,0:T(8,128)(2,1)S(1)}, bf16[48,1,8,512]{3,2,1,0:T(8,128)(2,1)S(1)}, u32[]{:S(2)}, u32[]{:S(2)}) collective-permute-start(bf16[48,1,8,512]{3,2,1,0:T(8,128)(2,1)S(1)} %get-tuple-element.142), channel_id=1, source_target_pairs={{0,1},{1,2},{2,3},{4,5},{5,6},{6,7},{8,9},{9,10},{10,11},{12,13},{... | collective-permute-start | bytes 1179656 | tf_op jit(solution)/shard_map/ppermute | solution.py:41
  565.7 207.7 %all-reduce.28.cloned.1.call-start = ((), (), s32[]{:S(2)}) async-start(), calls=%async_computation.25 | async-start | bytes 3014656 | tf_op jit(solution)/shard_map/psum | solution.py:214
  595.3 40.1 %collective-permute-start.15 = (bf16[2,416,512]{2,1,0:T(8,128)(2,1)}, bf16[2,416,512]{2,1,0:T(8,128)(2,1)}, u32[]{:S(2)}, u32[]{:S(2)}) collective-permute-start(bf16[2,416,512]{2,1,0:T(8,128)(2,1)} %dynamic-slice_bitcast_fusion.1), channel_id=1, source_target_pairs={{0,8},{4,12},{8,0},{12,4},{16,24},{20,28},{24,16},{28,20},{1,9},{5... | collective-permute-start | bytes 2555912 | tf_op jit(solution)/shard_map/ppermute | solution.py:162
  598.0 40.6 %collective-permute-start.23 = (bf16[2,416,512]{2,1,0:T(8,128)(2,1)}, bf16[2,416,512]{2,1,0:T(8,128)(2,1)}, u32[]{:S(2)}, u32[]{:S(2)}) collective-permute-start(bf16[2,416,512]{2,1,0:T(8,128)(2,1)} %dynamic-slice_bitcast_fusion), channel_id=1, source_target_pairs={{0,16},{4,20},{8,24},{12,28},{16,0},{20,4},{24,8},{28,12},{1,17},{... | collective-permute-start | bytes 2555912 | tf_op jit(solution)/shard_map/ppermute | solution.py:162
  640.1 18.1 %collective-permute-start.24 = (bf16[416,512]{1,0:T(8,128)(2,1)S(1)}, bf16[416,512]{1,0:T(8,128)(2,1)}, u32[]{:S(2)}, u32[]{:S(2)}) collective-permute-start(bf16[416,512]{1,0:T(8,128)(2,1)S(1)} %dynamic-slice_bitcast_fusion.2), channel_id=1, source_target_pairs={{0,8},{4,12},{8,0},{12,4},{16,24},{20,28},{24,16},{28,20},{1,9},{5... | collective-permute-start | bytes 1277960 | tf_op jit(solution)/shard_map/ppermute | solution.py:162
  683.7 23.6 %collective-permute-start.27 = (bf16[416,512]{1,0:T(8,128)(2,1)S(1)}, bf16[416,512]{1,0:T(8,128)(2,1)}, u32[]{:S(2)}, u32[]{:S(2)}) collective-permute-start(bf16[416,512]{1,0:T(8,128)(2,1)S(1)} %get-tuple-element.39), channel_id=1, source_target_pairs={{2,3},{6,7},{10,11},{14,15},{18,19},{22,23},{26,27},{30,31}} | collective-permute-start | bytes 1277960 | tf_op jit(solution)/shard_map/ppermute | solution.py:174
  686.2 19.6 %collective-permute-start.22 = (bf16[416,512]{1,0:T(8,128)(2,1)}, bf16[416,512]{1,0:T(8,128)(2,1)}, u32[]{:S(2)}, u32[]{:S(2)}) collective-permute-start(bf16[416,512]{1,0:T(8,128)(2,1)} %get-tuple-element.45), channel_id=1, source_target_pairs={{1,0},{5,4},{9,8},{13,12},{17,16},{21,20},{25,24},{29,28}} | collective-permute-start | bytes 1277960 | tf_op jit(solution)/shard_map/ppermute | solution.py:175
  688.8 48.1 %collective-permute-start.30 = (bf16[416,512]{1,0:T(8,128)(2,1)S(1)}, bf16[416,512]{1,0:T(8,128)(2,1)S(1)}, u32[]{:S(2)}, u32[]{:S(2)}) collective-permute-start(bf16[416,512]{1,0:T(8,128)(2,1)S(1)} %get-tuple-element.41), channel_id=1, source_target_pairs={{1,0},{5,4},{9,8},{13,12},{17,16},{21,20},{25,24},{29,28}} | collective-permute-start | bytes 1277960 | tf_op jit(solution)/shard_map/ppermute | solution.py:175
  (172 other events, 1834.5 us)
Sparse Core Ops, SparseCore 0:
  472.1 175.0 all-reduce.25
Sparse Core Ops, SparseCore 1:
  514.3 44.7 reduce-scatter.4
  562.4 102.5 reduce-scatter.2
  687.7 85.6 all-reduce.27

commit v2 on v1

v2 whole, which is shorter than its diff:
```python
import functools

import jax
import jax.numpy as jnp
from jax import lax
from jax.experimental import pallas as pl
from jax.experimental.pallas import tpu as pltpu
from jax.sharding import PartitionSpec as P

norm_eps = 1e-05
both = ("dp", "space")
f32 = jnp.float32
bf16 = jnp.bfloat16
group = 16
part = 512
chunk = 16
absent = -1e30
MB = 1024 * 1024


def dot(left, right):
    return jnp.dot(left, right, preferred_element_type=f32)


def dot_back(left, right):
    return lax.dot_general(left, right, (((1,), (1,)), ((), ())), preferred_element_type=f32)


def dot_inner(left, right):
    return lax.dot_general(left, right, (((0,), (0,)), ((), ())), preferred_element_type=f32)


def sigmoid(value):
    return 0.5 * jnp.tanh(0.5 * value) + 0.5


def silu(value):
    return value * sigmoid(value)


def silu_slope(value):
    sig = sigmoid(value)
    return sig * (1.0 + value * (1.0 - sig))


def lanes(rows):
    return jnp.concatenate([rows[i : i + 1] for i in range(rows.shape[0])], axis=1)


def unlanes(vector):
    return jnp.concatenate(
        [vector[:, 128 * i : 128 * (i + 1)] for i in range(vector.shape[1] // 128)], axis=0
    )


def pair_sum(ref):
    total = jnp.sum(ref[...], axis=0)
    return lanes(total[0:4]), lanes(total[4:8])


def norm_scale(sums, inv_count, gain, bias):
    mean = sums[0] * inv_count
    variance = sums[1] * inv_count - mean * mean
    inverse = lax.rsqrt(variance + norm_eps)
    scale = inverse * gain
    return mean, inverse, scale, bias - mean * scale


def store_pair(ref, first, second):
    rows = jnp.concatenate([unlanes(first), unlanes(second)], axis=0)
    ref[...] = jnp.broadcast_to(rows[None], (ref.shape[0], 8, 128))


def fold(value):
    return jnp.sum(value.reshape(-1, 8, value.shape[-1]), axis=0)


def squash(value):
    return jnp.sum(value, axis=0, keepdims=True)


def loop(count, body, init):
    return lax.fori_loop(0, count, body, init, unroll=True)


def at(index):
    return pl.ds(pl.multiple_of(index * chunk, chunk), chunk)


def columns(shape):
    return lax.broadcasted_iota(jnp.int32, shape, 0) % 8


def shift_columns(value, step):
    if step == 0:
        return value
    size = value.shape[0]
    col = columns(value.shape)
    moved = pltpu.roll(value, (-step) % size, 0)
    keep = (col + step >= 0) & (col + step < 8)
    return jnp.where(keep, moved, 0.0)


def params():
    return pltpu.CompilerParams(vmem_limit_bytes=60 * MB, dimension_semantics=("arbitrary",))


def whole(array):
    zeros = (0,) * array.ndim
    return pl.BlockSpec(array.shape, lambda *_: zeros)


def full(shape):
    zeros = (0,) * len(shape)
    return pl.BlockSpec(shape, lambda *_: zeros)


def gate_conv_rows(owners):
    return -(-7 * 128 // (owners * 16)) * 16


def wide_rows(owners, channels):
    return 9 * part // owners, channels // owners, channels // 4 // owners, gate_conv_rows(owners)


def shape_of(shape, kind):
    return jax.ShapeDtypeStruct(shape, kind)


def in_hbm(array):
    return pltpu.with_memory_space_constraint(array, pltpu.HBM)


def hbm_shape(shape, kind):
    return pltpu.HBM(shape, kind)


def cost(flops, moved, special=0):
    return pl.CostEstimate(flops=flops // 4, bytes_accessed=moved // 4, transcendentals=special)


def store_halo(low_ref, high_ref, value_of, mask_ref, sums, rows, size):
    mean = (sums * (1.0 / (rows * size))).astype(bf16)
    centre = mean.astype(f32)
    for ref, row in ((low_ref, 0), (high_ref, rows - 1)):

        def piece(i, _, ref=ref, row=row):
            value = value_of(row, i) - centre
            ref[at(i), :] = jnp.where(mask_ref[row, at(i), :] > 0.0, value, absent).astype(bf16)
            return 0

        loop(size // chunk, piece, 0)
        ref[pl.ds(size, 16), :] = jnp.broadcast_to(mean.astype(f32), (16, mean.shape[1])).astype(
            bf16
        )


def store_reduce(ref, acc, mask_ref, rows, size):
    space = ref.shape[0]
    for g in range(space):
        for r in range(rows):
            if g * group * 8 < size:
                lo = g * group * 8
                value = acc[r, lo : lo + group * 8, :].astype(bf16).astype(f32)
                ref[g, r] = (value * mask_ref[r, lo : lo + group * 8, :]).astype(bf16)
            else:
                ref[g, r] = jnp.zeros((group * 8, ref.shape[3]), bf16)


def finish_first(acc, acc_red, mask_ref, first, red, pay, low, high, rows, size):
    def piece(i, carry):
        s, q = carry
        for r in range(rows):
            value = acc[r, at(i), :] * mask_ref[r, at(i), :]
            first[r, at(i), :] = value
            s = s + fold(value)
            q = q + fold(value * value)
        return s, q

    zero = jnp.zeros((8, part), f32)
    s, q = loop(size // chunk, piece, (zero, zero))
    s, q = squash(s), squash(q)
    store_pair(pay, s, q)
    store_halo(low, high, lambda r, i: first[r, at(i), :], mask_ref, s, rows, size)
    store_reduce(red, acc_red, mask_ref, rows, size)


def first_kernel(rows, size, steps, x, w, w_red, mask, first, red, pay, low, high, acc, acc_red):
    step = pl.program_id(0)
    for r in range(rows):
        value = x[:, r].reshape(size, part)
        new, new_red = dot(value, w[...]), dot(value, w_red[...])

        @pl.when(step == 0)
        def _():
            acc[r] = new
            acc_red[r] = new_red

        @pl.when(step > 0)
        def _():
            acc[r] += new
            acc_red[r] += new_red

    @pl.when(step == steps - 1)
    def _():
        finish_first(acc, acc_red, mask, first, red, pay, low, high, rows, size)


def first_outputs(rows, size, devices, space, reduced):
    shapes = (
        shape_of((rows, size, part), f32),
        shape_of((space, rows, group * 8, reduced), bf16),
        shape_of((devices, 8, 128), f32),
        shape_of((size + 16, part), bf16),
        shape_of((size + 16, part), bf16),
    )
    return shapes, tuple(full(s.shape) for s in shapes)


def run_first(maps, layer, w, w_red, mask, devices, space):
    frames, rows, cols, channels = maps.shape
    size = frames * cols
    steps = channels // part
    reduced = w_red.shape[2]
    shapes, specs = first_outputs(rows, size, devices, space, reduced)
    return pl.pallas_call(
        functools.partial(first_kernel, rows, size, steps),
        grid=(steps,),
        in_specs=[
            pl.BlockSpec((frames, rows, cols, part), lambda k: (0, 0, 0, k)),
            pl.BlockSpec((None, part, part), lambda k: (layer, k, 0)),
            pl.BlockSpec((None, part, reduced), lambda k: (layer, k, 0)),
            whole(mask),
        ],
        out_specs=specs,
        out_shape=shapes,
        scratch_shapes=[pltpu.VMEM((rows, size, part), f32), pltpu.VMEM((rows, size, reduced), f32)],
        compiler_params=params(),
        cost_estimate=cost(2 * rows * size * channels * 640, 8 * MB),
        name="first",
    )(in_hbm(maps), in_hbm(w), in_hbm(w_red), mask)


def conv_kernel(rows, size, first, sums, inv, gain, bias, mask, w, hidden, out, shifted):
    step = pl.program_id(0)

    @pl.when(step == 0)
    def _():
        mean, inverse, scale, offset = norm_scale(
            pair_sum(sums), inv[0:1, 0:1], gain[...], bias[...]
        )

        def own(i, _):
            for r in range(rows):
                value = silu(first[r, at(i), :] * scale + offset) * mask[r, at(i), :]
                hidden[r, at(i), :] = value.astype(bf16)
                for j in range(3):
                    shifted[j, r, at(i), :] = shift_columns(value, j - 1).astype(bf16)
            return 0

        loop(size // chunk, own, 0)

    def taps(lo, hi, source):
        new = None
        for j in range(3):
            left = shifted[j, source : source + hi - lo].reshape((hi - lo) * size, part)
            term = dot(left, w[j * part : (j + 1) * part, :])
            new = term if new is None else new + term
        return new.reshape(hi - lo, size, part)

    own_taps(rows, step, out, taps)


def own_taps(rows, step, out, taps):
    @pl.when(step == 0)
    def _():
        out[...] = taps(0, rows, 0)

    if rows > 1:

        @pl.when(step == 1)
        def _():
            out[1:rows] += taps(1, rows, 0)

        @pl.when(step == 2)
        def _():
            out[0 : rows - 1] += taps(0, rows - 1, 1)


smem = pl.BlockSpec(memory_space=pltpu.SMEM)


def tap_order(step):
    return lax.rem(step + 1, 3)


def run_conv(first, sums, inv, gain, bias, mask, layer, w):
    rows, size = first.shape[:2]
    shapes = (shape_of((rows, size, part), bf16), shape_of((rows, size, part), f32))
    return pl.pallas_call(
        functools.partial(conv_kernel, rows, size),
        grid=(3 if rows > 1 else 1,),
        in_specs=[whole(first), whole(sums), whole(inv), whole(gain), whole(bias), whole(mask),
                  pl.BlockSpec((None, 3 * part, part), lambda i: (layer, jnp.where(i == 0, 1, jnp.where(i == 1, 0, 2)), 0))],
        out_specs=tuple(full(s.shape) for s in shapes),
        out_shape=shapes,
        scratch_shapes=[pltpu.VMEM((3, rows, size, part), bf16)],
        compiler_params=params(),
        cost_estimate=cost(2 * rows * size * 6 * part * part, 8 * MB),
        name="conv",
    )(first, sums, inv, gain, bias, mask, in_hbm(w))


def conv_edge_kernel(rows, size, before, low, high, edge, sums, inv, gain, bias, mask, w,
                     second, hidden, pay, send_low, send_high, shifted):
    step = pl.program_id(0)
    mean, inverse, scale, offset = norm_scale(pair_sum(sums), inv[0:1, 0:1], gain[...], bias[...])

    @pl.when(step == 0)
    def _():
        second[...] = before[...]

    for which, ref, row in ((0, low, 0), (1, high, rows - 1)):

        @pl.when(step == which)
        def _():
            centre = ref[pl.ds(size, 16), :].astype(f32)[0:1]
            here = edge[which] > 0

            def piece(i, _):
                got = ref[at(i), :].astype(f32)
                value = silu((got + centre) * scale + offset)
                value = jnp.where((got > 0.5 * absent) & here, value, 0.0)
                hidden[which, at(i), :] = value.astype(bf16)
                for j in range(3):
                    shifted[j, at(i), :] = shift_columns(value, j - 1).astype(bf16)
                return 0

            loop(size // chunk, piece, 0)
            new = None
            for j in range(3):
                term = dot(shifted[j], w[j * part : (j + 1) * part, :])
                new = term if new is None else new + term
            second[row] += new

    @pl.when(step == 1)
    def _():
        def piece(i, carry):
            s, q = carry
            for r in range(rows):
                value = second[r, at(i), :]
                masked = value * mask[r, at(i), :]
                s = s + fold(masked)
                q = q + fold(masked * value)
            return s, q

        zero = jnp.zeros((8, part), f32)
        s, q = loop(size // chunk, piece, (zero, zero))
        s, q = squash(s), squash(q)
        store_pair(pay, s, q)
        store_halo(send_low, send_high, lambda r, i: second[r, at(i), :], mask, s, rows, size)


def run_conv_edge(before, low, high, edge, sums, inv, gain, bias, mask, layer, w):
    rows, size = before.shape[:2]
    devices = sums.shape[0]
    shapes = (
        shape_of((rows, size, part), f32),
        shape_of((2, size, part), bf16),
        shape_of((devices, 8, 128), f32),
        shape_of((size + 16, part), bf16),
        shape_of((size + 16, part), bf16),
    )
    return pl.pallas_call(
        functools.partial(conv_edge_kernel, rows, size),
        grid=(2,),
        in_specs=[whole(before), whole(low), whole(high), smem, whole(sums), whole(inv), whole(gain),
                  whole(bias), whole(mask),
                  pl.BlockSpec((None, 3 * part, part), lambda i: (layer, 2 * i, 0))],
        out_specs=tuple(full(s.shape) for s in shapes),
        out_shape=shapes,
        scratch_shapes=[pltpu.VMEM((3, size, part), bf16)],
        compiler_params=params(),
        cost_estimate=cost(2 * size * 6 * part * part, 8 * MB),
        name="conv_edge",
    )(before, low, high, edge, sums, inv, gain, bias, mask, in_hbm(w))


def third_kernel(rows, size, second, sums, inv, gain, bias, mask, w, hidden, pay, prod):
    @pl.when(pl.program_id(0) == 0)
    def _():
        mean, inverse, scale, offset = norm_scale(
            pair_sum(sums), inv[0:1, 0:1], gain[...], bias[...]
        )

        def own(i, _):
            for r in range(rows):
                value = silu(second[r, at(i), :] * scale + offset) * mask[r, at(i), :]
                hidden[r, at(i), :] = value.astype(bf16)
            return 0

        loop(size // chunk, own, 0)

    prod[...] = dot(hidden[...].reshape(rows * size, part), w[...])

    def piece(i, carry):
        value = prod[at(i), :]
        return carry[0] + fold(value), carry[1] + fold(value * value)

    zero = jnp.zeros((8, part), f32)
    s, q = loop(rows * size // chunk, piece, (zero, zero))
    store_pair(pay, squash(s), squash(q))


def run_third(second, sums, inv, gain, bias, mask, layer, w):
    rows, size = second.shape[:2]
    devices = sums.shape[0]
    channels = w.shape[2]
    steps = channels // part
    return pl.pallas_call(
        functools.partial(third_kernel, rows, size),
        grid=(steps,),
        in_specs=[whole(second), whole(sums), whole(inv), whole(gain), whole(bias), whole(mask),
                  pl.BlockSpec((None, part, part), lambda k: (layer, 0, k))],
        out_specs=(full((rows, size, part)), pl.BlockSpec((devices, 8, 128), lambda k: (0, k, 0))),
        out_shape=(shape_of((rows, size, part), bf16), shape_of((devices, 8 * steps, 128), f32)),
        scratch_shapes=[pltpu.VMEM((rows * size, part), f32)],
        compiler_params=params(),
        cost_estimate=cost(2 * rows * size * channels * part, 5 * MB),
        name="third",
    )(second, sums, inv, gain, bias, mask, in_hbm(w))


def flat_gate(gate, rows, size):
    pieces = []
    for r in range(rows):
        for g in range(size // (group * 8)):
            pieces.append(gate[g, r])
    return jnp.concatenate(pieces, axis=0)


def mid_kernel(rows, size, steps, hidden, w_out, sums, inv, gain, bias, x, gate, w_exp, mask,
               w_next, red_next,
               out, branch, sig_out, slope, first, red, pay, low, high,
               prod, pre, acc, acc_red):
    step = pl.program_id(0)
    prod[...] = dot(hidden[...].reshape(rows * size, part), w_out[...]).reshape(rows, size, part)
    pre[...] = dot(flat_gate(gate, rows, size), w_exp[...]).reshape(rows, size, part)
    mean, inverse, scale, offset = norm_scale(pair_sum(sums), inv[0:1, 0:1], gain[...], bias[...])
    frames = chunk // 8

    def piece(i, _):
        for r in range(rows):
            b = prod[r, at(i), :] * scale + offset
            sig = sigmoid(pre[r, at(i), :])
            z = x[pl.ds(i * frames, frames), r].astype(f32).reshape(chunk, part) + b * sig
            zs = sigmoid(z)
            m = mask[r, at(i), :]
            out[r, at(i), :] = (z * zs * m).astype(bf16)
            slope[r, at(i), :] = (zs * (1.0 + z * (1.0 - zs)) * m).astype(bf16)
            branch[r, at(i), :] = b.astype(bf16)
            sig_out[r, at(i), :] = sig.astype(bf16)
        return 0

    loop(size // chunk, piece, 0)
    value = out[...].reshape(rows * size, part)
    new = dot(value, w_next[...]).reshape(rows, size, part)
    new_red = dot(value, red_next[...]).reshape(rows, size, acc_red.shape[2])

    @pl.when(step == 0)
    def _():
        acc[...] = new
        acc_red[...] = new_red

    @pl.when(step > 0)
    def _():
        acc[...] += new
        acc_red[...] += new_red

    @pl.when(step == steps - 1)
    def _():
        finish_first(acc, acc_red, mask, first, red, pay, low, high, rows, size)


def run_mid(layer, hidden, w_out, sums, inv, gain, bias, maps, gate, w_exp, mask, w_next, red_next):
    frames, rows, cols, channels = maps.shape
    size = frames * cols
    steps = channels // part
    devices, space = sums.shape[0], gate.shape[0]
    reduced = w_exp.shape[1]
    more, more_specs = first_outputs(rows, size, devices, space, reduced)
    wide = hbm_shape((rows, size, channels), bf16)
    slab = pl.BlockSpec((rows, size, part), lambda k: (0, 0, k))
    return pl.pallas_call(
        functools.partial(mid_kernel, rows, size, steps),
        grid=(steps,),
        in_specs=[
            whole(hidden),
            pl.BlockSpec((None, part, part), lambda k: (layer, 0, k)),
            pl.BlockSpec((devices, 8, 128), lambda k: (0, k, 0)),
            whole(inv),
            pl.BlockSpec((1, part), lambda k: (0, k)),
            pl.BlockSpec((1, part), lambda k: (0, k)),
            pl.BlockSpec((frames, rows, cols, part), lambda k: (0, 0, 0, k)),
            whole(gate),
            pl.BlockSpec((None, reduced, part), lambda k: (layer, 0, k)),
            whole(mask),
            pl.BlockSpec((None, part, part), lambda k: (layer + 1, k, 0)),
            pl.BlockSpec((None, part, reduced), lambda k: (layer + 1, k, 0)),
        ],
        out_specs=(slab,) * 4 + more_specs,
        out_shape=(wide,) * 4 + more,
        scratch_shapes=[pltpu.VMEM((rows, size, part), f32)] * 3
        + [pltpu.VMEM((rows, size, reduced), f32)],
        compiler_params=params(),
        cost_estimate=cost(2 * rows * size * channels * (part + part + 256), 20 * MB),
        name="mid",
    )(hidden, in_hbm(w_out), sums, inv, gain, bias, in_hbm(maps), gate, in_hbm(w_exp), mask,
      in_hbm(w_next), in_hbm(red_next))


def place(owner, owners, me):
    if me is None:
        return owner
    other = jnp.bitwise_xor(owner, me[0])
    return lax.rem(other, 2) * (owners // 2) + other // 2


def put_rows(ref, me, begin, per, value):
    done = 0
    while done < value.shape[0]:
        owner, offset = (begin + done) // per, (begin + done) % per
        length = min(value.shape[0] - done, per - offset)
        ref[place(owner, ref.shape[0], me), offset : offset + length, :] = value[done : done + length]
        done += length


def gate_grads(step, steps, rows, size, me, pre_grad, gate, w_exp, grad_exp, grad_gate, acc):
    left = flat_gate(gate, rows, size)
    right = pre_grad[...].reshape(rows * size, part)
    value = dot_inner(left, right).astype(bf16)
    owners, per = grad_exp.shape[:2]
    for i in range(steps):

        @pl.when(step == i)
        def _():
            put_rows(grad_exp, me, i * value.shape[0], per, value)

    new = dot_back(right, w_exp[...]).reshape(rows, size, acc.shape[2])

    @pl.when(step == 0)
    def _():
        acc[...] = new

    @pl.when(step > 0)
    def _():
        acc[...] += new

    @pl.when(step == steps - 1)
    def _():
        for g in range(grad_gate.shape[0]):
            for r in range(rows):
                lo = g * group * 8
                if lo < size:
                    grad_gate[g, r] = acc[r, lo : lo + group * 8, :].astype(bf16)
                else:
                    grad_gate[g, r] = jnp.zeros((group * 8, acc.shape[2]), bf16)


def last_kernel(rows, size, steps, hidden, w_out, sums, inv, gain, bias, x, gate, w_exp, mask,
                grad_out,
                out, branch, grad_branch, grad_in, grad_exp, grad_gate, pay,
                prod, pre, pre_grad, acc):
    step = pl.program_id(0)
    prod[...] = dot(hidden[...].reshape(rows * size, part), w_out[...]).reshape(rows, size, part)
    pre[...] = dot(flat_gate(gate, rows, size), w_exp[...]).reshape(rows, size, part)
    mean, inverse, scale, offset = norm_scale(pair_sum(sums), inv[0:1, 0:1], gain[...], bias[...])
    frames = chunk // 8

    def piece(i, carry):
        s, q = carry
        for r in range(rows):
            n = (prod[r, at(i), :] - mean) * inverse
            b = n * gain[...] + bias[...]
            sig = sigmoid(pre[r, at(i), :])
            z = x[r, at(i), :].astype(f32) + b * sig
            zs = sigmoid(z)
            m = mask[r, at(i), :]
            out[pl.ds(i * frames, frames), r] = (z * zs * m).reshape(frames, 8, part).astype(bf16)
            dz = grad_out[pl.ds(i * frames, frames), r].astype(f32).reshape(chunk, part)
            dz = dz * m * (zs * (1.0 + z * (1.0 - zs)))
            db = dz * sig
            s = s + fold(db)
            q = q + fold(db * n)
            branch[r, at(i), :] = b.astype(bf16)
            grad_branch[r, at(i), :] = db.astype(bf16)
            grad_in[r, at(i), :] = dz.astype(bf16)
            pre_grad[r, at(i), :] = (db * b * (1.0 - sig)).astype(bf16)
        return s, q

    zero = jnp.zeros((8, part), f32)
    s, q = loop(size // chunk, piece, (zero, zero))
    store_pair(pay, squash(s), squash(q))
    gate_grads(step, steps, rows, size, None, pre_grad, gate, w_exp, grad_exp, grad_gate, acc)


def expand_spec(owners, channels):
    rows = wide_rows(owners, channels)
    return pl.BlockSpec((owners, rows[2], part), lambda *_: (0, (rows[0] + rows[1]) // rows[2], 0))


def run_last(owners, layer, hidden, w_out, sums, inv, gain, bias, maps, gate, w_exp, mask, grad_out):
    frames, rows, cols, channels = grad_out.shape
    size = frames * cols
    steps = channels // part
    devices, space = sums.shape[0], gate.shape[0]
    reduced = w_exp.shape[1]
    wide = hbm_shape((rows, size, channels), bf16)
    slab = pl.BlockSpec((rows, size, part), lambda k: (0, 0, k))
    outside = pl.BlockSpec((frames, rows, cols, part), lambda k: (0, 0, 0, k))
    pays = pl.BlockSpec((devices, 8, 128), lambda k: (0, k, 0))
    row = pl.BlockSpec((1, part), lambda k: (0, k))
    return pl.pallas_call(
        functools.partial(last_kernel, rows, size, steps),
        grid=(steps,),
        in_specs=[
            whole(hidden), pl.BlockSpec((None, part, part), lambda k: (layer, 0, k)), pays, whole(inv),
            row, row, slab, whole(gate), pl.BlockSpec((None, reduced, part), lambda k: (layer, 0, k)),
            whole(mask), outside,
        ],
        out_specs=(outside, slab, slab, slab, expand_spec(owners, channels), full(gate.shape), pays),
        out_shape=(hbm_shape(grad_out.shape, bf16), wide, wide, wide,
                   hbm_shape((owners, sum(wide_rows(owners, channels)), part), bf16),
                   shape_of(gate.shape, bf16), shape_of(sums.shape, f32)),
        scratch_shapes=[pltpu.VMEM((rows, size, part), f32)] * 2
        + [pltpu.VMEM((rows, size, part), bf16), pltpu.VMEM((rows, size, reduced), f32)],
        compiler_params=params(),
        cost_estimate=cost(2 * rows * size * channels * (part + 512), 20 * MB),
        name="last",
    )(hidden, in_hbm(w_out), sums, inv, gain, bias, in_hbm(maps), gate, in_hbm(w_exp), mask,
      in_hbm(grad_out))


def third_back_kernel(rows, size, steps, fixed, me, buffer, grad_branch, branch, back_sums, sums, inv, gain, bias, mask,
                      hidden, w_out, second, sums_two, gain_two, bias_two,
                      grad_w, part_two, pay, low, high, third_grad, hidden_t, acc):
    step = pl.program_id(0)

    @pl.when(step == 0)
    def _():
        hidden_t[...] = hidden[...].reshape(rows * size, part).T

    inv_count = inv[0:1, 0:1]
    mean, inverse, scale, offset = norm_scale(pair_sum(sums), inv_count, gain[...], bias[...])
    sum_bias, sum_gain = pair_sum(back_sums)
    inv_gain = 1.0 / gain[...]
    slope = -scale * inv_count * sum_gain * inv_gain
    const = -scale * inv_count * sum_bias - slope * bias[...]

    def piece(i, _):
        for r in range(rows):
            db = grad_branch[r, at(i), :].astype(f32)
            b = branch[r, at(i), :].astype(f32)
            value = scale * db + mask[r, at(i), :] * (const + slope * b)
            third_grad[r, at(i), :] = value.astype(bf16)
        return 0

    loop(size // chunk, piece, 0)
    right = third_grad[...].reshape(rows * size, part)
    new = dot_back(right, w_out[...]).reshape(rows, size, part)

    @pl.when(step == 0)
    def _():
        acc[...] = new

    @pl.when(step > 0)
    def _():
        acc[...] += new

    put_rows(grad_w, None if fixed else me, 0, grad_w.shape[1], dot(hidden_t[...], right).astype(bf16))

    @pl.when(step == steps - 1)
    def _():
        finish_back(rows, size, acc, second, sums_two, inv, gain_two, bias_two, mask,
                    part_two, pay, low, high)


def finish_back(rows, size, acc, value_ref, sums, inv, gain, bias, mask, part_ref, pay, low, high):
    mean, inverse, scale, offset = norm_scale(pair_sum(sums), inv[0:1, 0:1], gain[...], bias[...])

    def piece(i, carry):
        s, q = carry
        for r in range(rows):
            n = (value_ref[r, at(i), :] - mean) * inverse
            grad = acc[r, at(i), :] * silu_slope(n * gain[...] + bias[...]) * mask[r, at(i), :]
            s = s + fold(grad)
            q = q + fold(grad * n)
            part_ref[r, at(i), :] = grad * scale
        return s, q

    zero = jnp.zeros((8, part), f32)
    s, q = loop(size // chunk, piece, (zero, zero))
    s, q = squash(s), squash(q)
    store_pair(pay, s, q)
    if low is not None:
        store_halo(low, high, lambda r, i: part_ref[r, at(i), :], mask, s * scale, rows, size)


def run_third_back(me, fixed, buffer, layer, grad_branch, branch, back_sums, sums, inv, gain, bias, mask,
                   hidden, w_out, second, sums_two, gain_two, bias_two):
    rows, size, channels = branch.shape
    steps = channels // part
    devices = sums.shape[0]
    owners = buffer.shape[0]
    slab = pl.BlockSpec((rows, size, part), lambda k: (0, 0, k))
    pays = pl.BlockSpec((devices, 8, 128), lambda k: (0, k, 0))
    row = pl.BlockSpec((1, part), lambda k: (0, k))
    return pl.pallas_call(
        functools.partial(third_back_kernel, rows, size, steps, fixed),
        grid=(steps,),
        in_specs=[smem, pl.BlockSpec(memory_space=pl.ANY), slab, slab, pays, pays, whole(inv), row, row, whole(mask), whole(hidden),
                  pl.BlockSpec((None, part, part), lambda k: (layer, 0, k)), whole(second), whole(sums_two),
                  whole(gain_two), whole(bias_two)],
        out_specs=(pl.BlockSpec((owners, part // owners, part), lambda k: (0, 9 + k, 0)),
                   full((rows, size, part)),
                   full((devices, 8, 128)), full((size + 16, part)), full((size + 16, part))),
        out_shape=(hbm_shape(buffer.shape, bf16), shape_of((rows, size, part), f32),
                   shape_of((devices, 8, 128), f32), shape_of((size + 16, part), bf16),
                   shape_of((size + 16, part), bf16)),
        scratch_shapes=[pltpu.VMEM((rows, size, part), bf16), pltpu.VMEM((part, rows * size), bf16),
                        pltpu.VMEM((rows, size, part), f32)],
        compiler_params=params(),
        cost_estimate=cost(4 * rows * size * channels * part, 12 * MB),
        input_output_aliases={1: 0},
        name="third_back",
    )(me, in_hbm(buffer), in_hbm(grad_branch), in_hbm(branch), back_sums, sums, inv, gain, bias, mask, hidden,
      in_hbm(w_out), second, sums_two, gain_two, bias_two)


def conv_back_kernel(rows, size, part_two, second, back_sums, sums_two, gain_two, bias_two, inv, mask,
                     w, grad_second, out, shifted):
    step = pl.program_id(0)

    @pl.when(step == 0)
    def _():
        inv_count = inv[0:1, 0:1]
        mean, inverse, scale, offset = norm_scale(
            pair_sum(sums_two), inv_count, gain_two[...], bias_two[...]
        )
        sum_bias, sum_gain = pair_sum(back_sums)
        slope = -scale * inv_count * sum_gain * inverse
        const = -scale * inv_count * sum_bias

        def own(i, _):
            for r in range(rows):
                centred = second[r, at(i), :] - mean
                value = part_two[r, at(i), :] + mask[r, at(i), :] * (const + slope * centred)
                grad_second[r, at(i), :] = value.astype(bf16)
                for j in range(3):
                    shifted[j, r, at(i), :] = shift_columns(value, 1 - j).astype(bf16)
            return 0

        loop(size // chunk, own, 0)

    def taps(lo, hi, source):
        new = None
        for j in range(3):
            left = shifted[j, source : source + hi - lo].reshape((hi - lo) * size, part)
            term = dot_back(left, w[j * part : (j + 1) * part, :])
            new = term if new is None else new + term
        return new.reshape(hi - lo, size, part)

    own_taps(rows, step, out, taps)


def run_conv_back(part_two, second, back_sums, sums_two, gain_two, bias_two, inv, mask, layer, w):
    rows, size = second.shape[:2]
    args = (part_two, second, back_sums, sums_two, gain_two, bias_two, inv, mask)
    shapes = (shape_of((rows, size, part), bf16), shape_of((rows, size, part), f32))
    return pl.pallas_call(
        functools.partial(conv_back_kernel, rows, size),
        grid=(3 if rows > 1 else 1,),
        in_specs=[whole(a) for a in args]
        + [pl.BlockSpec((None, 3 * part, part), lambda i: (layer, jnp.where(i == 0, 1, jnp.where(i == 1, 2, 0)), 0))],
        out_specs=tuple(full(s.shape) for s in shapes),
        out_shape=shapes,
        scratch_shapes=[pltpu.VMEM((3, rows, size, part), bf16)],
        compiler_params=params(),
        cost_estimate=cost(2 * rows * size * 6 * part * part, 8 * MB),
        name="conv_back",
    )(*args, in_hbm(w))


def conv_back_edge_kernel(rows, size, before, part_low, part_high, second_low, second_high, edge,
                          back_sums, sums_two, gain_two, bias_two, inv, mask, w,
                          first, sums_one, gain_one, bias_one, part_one, pay, shifted, acc):
    step = pl.program_id(0)
    inv_count = inv[0:1, 0:1]
    mean, inverse, scale, offset = norm_scale(
        pair_sum(sums_two), inv_count, gain_two[...], bias_two[...]
    )
    sum_bias, sum_gain = pair_sum(back_sums)
    slope = -scale * inv_count * sum_gain * inverse
    const = -scale * inv_count * sum_bias

    @pl.when(step == 0)
    def _():
        acc[...] = before[...]

    for which, ref, val, row, side in (
        (0, part_high, second_high, rows - 1, 1), (1, part_low, second_low, 0, 0)
    ):

        @pl.when(step == which)
        def _():
            middle = val[pl.ds(size, 16), :].astype(f32)[0:1] - mean
            base = ref[pl.ds(size, 16), :].astype(f32)[0:1] + const + slope * middle
            here = edge[side] > 0

            def piece(i, _):
                got = ref[at(i), :].astype(f32)
                value = got + base + slope * val[at(i), :].astype(f32)
                value = jnp.where((got > 0.5 * absent) & here, value, 0.0)
                for j in range(3):
                    shifted[j, at(i), :] = shift_columns(value, 1 - j).astype(bf16)
                return 0

            loop(size // chunk, piece, 0)
            new = None
            for j in range(3):
                term = dot_back(shifted[j], w[j * part : (j + 1) * part, :])
                new = term if new is None else new + term
            acc[row] += new

    @pl.when(step == 1)
    def _():
        finish_back(rows, size, acc, first, sums_one, inv, gain_one, bias_one, mask,
                    part_one, pay, None, None)


def run_conv_back_edge(before, part_low, part_high, second_low, second_high, edge, back_sums, sums_two,
                       gain_two, bias_two, inv, mask, layer, w, first, sums_one, gain_one, bias_one):
    rows, size = before.shape[:2]
    devices = sums_two.shape[0]
    args = (before, part_low, part_high, second_low, second_high, edge, back_sums, sums_two,
            gain_two, bias_two, inv, mask, w, first, sums_one, gain_one, bias_one)
    specs = [None if a is w else whole(a) for a in args]
    specs[5] = smem
    specs[12] = pl.BlockSpec((None, 3 * part, part), lambda i: (layer, 2 * i, 0))
    shapes = (shape_of((rows, size, part), f32), shape_of((devices, 8, 128), f32))
    return pl.pallas_call(
        functools.partial(conv_back_edge_kernel, rows, size),
        grid=(2,),
        in_specs=specs,
        out_specs=tuple(full(s.shape) for s in shapes),
        out_shape=shapes,
        scratch_shapes=[pltpu.VMEM((3, size, part), bf16), pltpu.VMEM((rows, size, part), f32)],
        compiler_params=params(),
        cost_estimate=cost(2 * size * 6 * part * part, 8 * MB),
        name="conv_back_edge",
    )(*[in_hbm(a) if a is w else a for a in args])


def conv_weight_kernel(rows, size, fixed, me, hidden, hidden_edge, grad_second, buffer, out, hidden_t, shifted):
    step = pl.program_id(0)
    owners, per = out.shape[:2]

    @pl.when(step == 0)
    def _():
        hidden_t[:, 0:size] = hidden_edge[0].T
        for r in range(rows):
            hidden_t[:, (r + 1) * size : (r + 2) * size] = hidden[r].T
        hidden_t[:, (rows + 1) * size : (rows + 2) * size] = hidden_edge[1].T

        def piece(i, _):
            for r in range(rows):
                value = grad_second[r, at(i), :].astype(f32)
                for j in range(3):
                    shifted[j, r, at(i), :] = shift_columns(value, 1 - j).astype(bf16)
            return 0

        loop(size // chunk, piece, 0)

    for i in range(3):

        @pl.when(step == i)
        def _():
            left = hidden_t[:, i * size : (i + rows) * size]
            for j in range(3):
                right = shifted[j].reshape(rows * size, part)
                value = dot(left, right).astype(bf16)
                put_rows(out, None if fixed else me, (3 * i + j) * part, per, value)


def run_conv_weight(me, fixed, hidden, hidden_edge, grad_second, buffer):
    rows, size = grad_second.shape[:2]
    owners = buffer.shape[0]
    return pl.pallas_call(
        functools.partial(conv_weight_kernel, rows, size, fixed),
        grid=(3,),
        in_specs=[smem, whole(hidden), whole(hidden_edge), whole(grad_second),
                  pl.BlockSpec(memory_space=pl.ANY)],
        out_specs=full((owners, 9 * part // owners, part)),
        out_shape=hbm_shape(buffer.shape, bf16),
        scratch_shapes=[pltpu.VMEM((part, (rows + 2) * size), bf16), pltpu.VMEM((3, rows, size, part), bf16)],
        input_output_aliases={4: 0},
        compiler_params=params(),
        cost_estimate=cost(2 * rows * size * 9 * part * part, 8 * MB),
        name="conv_weight",
    )(me, hidden, hidden_edge, grad_second, in_hbm(buffer))


def first_grad(rows, size, part_one, first, back_sums, sums_one, inv, gain, bias, mask, out):
    inv_count = inv[0:1, 0:1]
    mean, inverse, scale, offset = norm_scale(pair_sum(sums_one), inv_count, gain[...], bias[...])
    sum_bias, sum_gain = pair_sum(back_sums)
    slope = -scale * inv_count * sum_gain * inverse
    const = -scale * inv_count * sum_bias

    def own(i, _):
        for r in range(rows):
            centred = first[r, at(i), :] - mean
            value = part_one[r, at(i), :] + mask[r, at(i), :] * (const + slope * centred)
            out[r, at(i), :] = value.astype(bf16)
        return 0

    loop(size // chunk, own, 0)


def mask_gate(grad_rows, mask, out, rows, size):
    for r in range(rows):
        for g in range(size // (group * 8)):
            lo = g * group * 8
            value = grad_rows[g, r].astype(f32) * mask[r, lo : lo + group * 8, :]
            out[r, lo : lo + group * 8, :] = value.astype(bf16)


def between_kernel(rows, size, steps, part_one, first, back_sums, sums_one, inv, gain, bias, mask,
                   grad_rows, w_in, w_red, grad_above, slope, sig, branch, gain_three, bias_three,
                   gate, w_exp, me,
                   first_out, rows_out, grad_in, grad_branch, grad_exp, grad_gate, pay,
                   prod, pre_grad, acc):
    step = pl.program_id(0)

    @pl.when(step == 0)
    def _():
        first_grad(rows, size, part_one, first, back_sums, sums_one, inv, gain, bias, mask, first_out)
        mask_gate(grad_rows, mask, rows_out, rows, size)

    prod[...] = (
        dot_back(first_out[...].reshape(rows * size, part), w_in[...])
        + dot_back(rows_out[...].reshape(rows * size, rows_out.shape[2]), w_red[...])
    ).reshape(rows, size, part)
    inv_gain = 1.0 / gain_three[...]
    offset = bias_three[...] * inv_gain

    def piece(i, carry):
        s, q = carry
        for r in range(rows):
            dy = grad_above[r, at(i), :].astype(f32) + prod[r, at(i), :]
            dz = dy * slope[r, at(i), :].astype(f32)
            sg = sig[r, at(i), :].astype(f32)
            b = branch[r, at(i), :].astype(f32)
            db = dz * sg
            s = s + fold(db)
            q = q + fold(db * (b * inv_gain - offset))
            grad_branch[r, at(i), :] = db.astype(bf16)
            grad_in[r, at(i), :] = dz.astype(bf16)
            pre_grad[r, at(i), :] = (db * b * (1.0 - sg)).astype(bf16)
        return s, q

    zero = jnp.zeros((8, part), f32)
    s, q = loop(size // chunk, piece, (zero, zero))
    store_pair(pay, squash(s), squash(q))
    gate_grads(step, steps, rows, size, me, pre_grad, gate, w_exp, grad_exp, grad_gate, acc)


def run_between(me, owners, layer, part_one, first, back_sums, sums_one, inv, gain, bias, mask, grad_rows, w_in, w_red,
                grad_above, slope, sig, branch, gain_three, bias_three, gate, w_exp):
    rows, size, channels = branch.shape
    steps = channels // part
    devices = sums_one.shape[0]
    reduced = w_exp.shape[1]
    slab = pl.BlockSpec((rows, size, part), lambda k: (0, 0, k))
    pays = pl.BlockSpec((devices, 8, 128), lambda k: (0, k, 0))
    row = pl.BlockSpec((1, part), lambda k: (0, k))
    wide = hbm_shape(branch.shape, bf16)
    return pl.pallas_call(
        functools.partial(between_kernel, rows, size, steps),
        grid=(steps,),
        in_specs=[whole(part_one), whole(first), whole(back_sums), whole(sums_one), whole(inv),
                  whole(gain), whole(bias), whole(mask), whole(grad_rows),
                  pl.BlockSpec((None, part, part), lambda k: (layer, k, 0)),
                  pl.BlockSpec((None, part, reduced), lambda k: (layer, k, 0)),
                  slab, slab, slab, slab, row, row, whole(gate),
                  pl.BlockSpec((None, reduced, part), lambda k: (layer - 1, 0, k)), smem],
        out_specs=(full((rows, size, part)), full((rows, size, reduced)), slab, slab,
                   expand_spec(owners, channels), full(gate.shape), pays),
        out_shape=(shape_of((rows, size, part), bf16), shape_of((rows, size, reduced), bf16), wide, wide,
                   hbm_shape((owners, sum(wide_rows(owners, channels)), part), bf16),
                   shape_of(gate.shape, bf16), shape_of((devices, 8 * steps, 128), f32)),
        scratch_shapes=[pltpu.VMEM((rows, size, part), f32), pltpu.VMEM((rows, size, part), bf16),
                        pltpu.VMEM((rows, size, reduced), f32)],
        compiler_params=params(),
        cost_estimate=cost(2 * rows * size * channels * (part + 512), 20 * MB),
        name="between",
    )(part_one, first, back_sums, sums_one, inv, gain, bias, mask, grad_rows, in_hbm(w_in),
      in_hbm(w_red), in_hbm(grad_above), in_hbm(slope), in_hbm(sig), in_hbm(branch), gain_three,
      bias_three, gate, in_hbm(w_exp), me)


def first_back_kernel(rows, size, part_one, first, back_sums, sums_one, inv, gain, bias, mask, grad_rows,
                      first_out, rows_out):
    first_grad(rows, size, part_one, first, back_sums, sums_one, inv, gain, bias, mask, first_out)
    mask_gate(grad_rows, mask, rows_out, rows, size)


def run_first_back(part_one, first, back_sums, sums_one, inv, gain, bias, mask, grad_rows):
    rows, size = first.shape[:2]
    reduced = grad_rows.shape[3]
    args = (part_one, first, back_sums, sums_one, inv, gain, bias, mask, grad_rows)
    return pl.pallas_call(
        functools.partial(first_back_kernel, rows, size),
        grid=(1,),
        in_specs=[whole(a) for a in args],
        out_specs=(full((rows, size, part)), full((rows, size, reduced))),
        out_shape=(shape_of((rows, size, part), bf16), shape_of((rows, size, reduced), bf16)),
        compiler_params=params(),
        cost_estimate=cost(rows * size * part * 8, 5 * MB),
        name="first_back",
    )(*args)


def input_kernel(rows, size, first_out, rows_out, w_in, w_red, grad_above, mask, out, prod):
    prod[...] = (
        dot_back(first_out[...].reshape(rows * size, part), w_in[...])
        + dot_back(rows_out[...].reshape(rows * size, rows_out.shape[2]), w_red[...])
    ).reshape(rows, size, part)
    frames = chunk // 8

    def piece(i, _):
        for r in range(rows):
            value = grad_above[r, at(i), :].astype(f32) + prod[r, at(i), :] * mask[r, at(i), :]
            out[pl.ds(i * frames, frames), r] = value.reshape(frames, 8, part).astype(bf16)
        return 0

    loop(size // chunk, piece, 0)


def run_input(layer, first_out, rows_out, w_in, w_red, grad_above, mask, frames):
    rows, size, channels = grad_above.shape
    steps = channels // part
    reduced = w_red.shape[2]
    return pl.pallas_call(
        functools.partial(input_kernel, rows, size),
        grid=(steps,),
        in_specs=[whole(first_out), whole(rows_out),
                  pl.BlockSpec((None, part, part), lambda k: (layer, k, 0)),
                  pl.BlockSpec((None, part, reduced), lambda k: (layer, k, 0)),
                  pl.BlockSpec((rows, size, part), lambda k: (0, 0, k)), whole(mask)],
        out_specs=pl.BlockSpec((frames, rows, 8, part), lambda k: (0, 0, 0, k)),
        out_shape=hbm_shape((frames, rows, 8, channels), bf16),
        scratch_shapes=[pltpu.VMEM((rows, size, part), f32)],
        compiler_params=params(),
        cost_estimate=cost(2 * rows * size * channels * 640, 10 * MB),
        name="input",
    )(first_out, rows_out, in_hbm(w_in), in_hbm(w_red), in_hbm(grad_above), mask)


def weight_kernel(rows, size, steps, outside, fixed, me, x, first_out, rows_out, out):
    step = pl.program_id(0)
    for r in range(rows):
        value = x[:, r].reshape(size, part) if outside else x[r]
        turned = value.T
        new, new_red = dot(turned, first_out[r]), dot(turned, rows_out[r])
        total = new if r == 0 else total + new
        total_red = new_red if r == 0 else total_red + new_red
    owners = out.shape[0]
    here = owners // steps
    per = part // here
    quarter = per // 4
    for i in range(steps):

        @pl.when(step == i)
        def _():
            for d in range(here):
                where = place(i * here + d, owners, None if fixed else me)
                out[where, 0:per, :] = total[d * per : (d + 1) * per].astype(bf16)
                piece = total_red[d * per : (d + 1) * per]
                wide = [piece[j * quarter : (j + 1) * quarter] for j in range(4)]
                out[where, per : per + quarter, :] = jnp.concatenate(wide, axis=1).astype(bf16)


def run_weight(me, fixed, owners, x, first_out, rows_out):
    rows, size = first_out.shape[:2]
    channels = x.shape[-1]
    steps = channels // part
    per = channels // owners
    outside = x.ndim == 4
    if outside:
        x_spec = pl.BlockSpec((x.shape[0], rows, 8, part), lambda k: (0, 0, 0, k))
    else:
        x_spec = pl.BlockSpec((rows, size, part), lambda k: (0, 0, k))
    return pl.pallas_call(
        functools.partial(weight_kernel, rows, size, steps, outside, fixed),
        grid=(steps,),
        in_specs=[smem, x_spec, whole(first_out), whole(rows_out)],
        out_specs=full((owners, per + per // 4, part)),
        out_shape=hbm_shape((owners, per + per // 4, part), bf16),
        compiler_params=params(),
        cost_estimate=cost(2 * rows * size * channels * 640, 8 * MB),
        name="weight",
    )(me, in_hbm(x), first_out, rows_out)


def three_shifts(value, step, sign):
    height, size, channels = value.shape
    flat = value.reshape(height * size, channels)
    wide = jnp.concatenate(
        [shift_columns(flat, sign * (j - 1) * step).astype(bf16) for j in range(3)], axis=1
    ).reshape(height, size, 3 * channels)
    blank = jnp.zeros((1, size, 3 * channels), bf16)
    return jnp.concatenate([blank, wide, blank], axis=0)


def small_conv(taps, w):
    height, size = taps.shape[0] - 2, taps.shape[1]
    depth = taps.shape[2]
    total = None
    for i in range(3):
        new = dot(taps[i : i + height].reshape(height * size, depth), w[i * depth : (i + 1) * depth])
        total = new if total is None else total + new
    return total.reshape(height, size, -1)


def small_conv_back(taps, w):
    height, size = taps.shape[0] - 2, taps.shape[1]
    channels = taps.shape[2] // 3
    total = None
    for i in range(3):
        left = taps[2 - i : 2 - i + height].reshape(height * size, 3 * channels)
        for j in range(3):
            tap = (3 * i + j) * channels
            new = dot_back(left[:, j * channels : (j + 1) * channels], w[tap : tap + channels])
            total = new if total is None else total + new
    return total.reshape(height, size, channels)


def small_weight(taps, grad, out, me, which, factor):
    height, size = taps.shape[0] - 2, taps.shape[1]
    depth = taps.shape[2]
    right = grad.reshape(height * size, -1)
    for i in range(3):
        left = taps[i : i + height].reshape(height * size, depth)
        value = (dot_inner(left, right) * factor).astype(bf16)
        for j in range(3):
            block = 9 * which + 3 * i + j
            lane = block % 4 * 128
            put_rows(out.at[:, :, lane : lane + 128], me, block // 4 * 128, out.shape[1],
                     value[j * 128 : (j + 1) * 128])


def add_rows(value):
    height, size, channels = value.shape
    pairs = value.reshape(height // 2, 2, size, channels)
    return pairs[:, 0] + pairs[:, 1]


def add_columns(value, step):
    height, size, channels = value.shape
    flat = value.reshape(height * size, channels)
    count = height * size
    lower = columns(flat.shape) % (2 * step) < step
    moved = jnp.where(lower, pltpu.roll(flat, count - step, 0), pltpu.roll(flat, step, 0))
    return (flat + moved).reshape(height, size, channels)


def spread_rows(value, factor):
    height, size, channels = value.shape
    wide = jnp.broadcast_to(value[:, None], (height, factor, size, channels))
    return wide.reshape(height * factor, size, channels)


def take_frames(dest, source, index):
    height = dest.shape[0]
    for f in range(group):
        dest[:, f] = source[:, index[f]]


def gate_kernel(reduce_ref, index, w, out, coarse_two, coarse_four, plain, moved):
    height, size, channels = reduce_ref.shape
    plain[...] = reduce_ref[...].astype(f32).reshape(height, group, 8, channels)
    take_frames(moved, plain, index)
    diff = small_conv(three_shifts(moved[...].reshape(height, size, channels), 1, 1), w[0])
    diff = diff - plain[...].reshape(height, size, channels)
    sum_two = add_columns(add_rows(diff), 1)
    sum_four = add_columns(add_rows(sum_two), 2)
    two = (sum_two * 0.25).astype(bf16)
    four = (sum_four * 0.0625).astype(bf16)
    coarse_two[...] = two
    coarse_four[...] = four
    conv_two = small_conv(three_shifts(two.astype(f32), 2, 1), w[1])
    conv_four = small_conv(three_shifts(four.astype(f32), 4, 1), w[2])
    out[...] = (diff + spread_rows(conv_two, 2) + spread_rows(conv_four, 4)).astype(bf16)


def run_gate(layer, reduce_full, index, w):
    height, size, channels = reduce_full.shape
    shapes = (
        shape_of((height, size, channels), bf16),
        shape_of((height // 2, size, channels), bf16),
        shape_of((height // 4, size, channels), bf16),
    )
    return pl.pallas_call(
        gate_kernel,
        grid=(1,),
        in_specs=[whole(reduce_full), smem, pl.BlockSpec((None,) + w.shape[1:], lambda k: (layer, 0, 0, 0))],
        out_specs=tuple(full(s.shape) for s in shapes),
        out_shape=shapes,
        scratch_shapes=[pltpu.VMEM((height, group, 8, channels), f32)] * 2,
        compiler_params=params(),
        cost_estimate=cost(2 * height * size * 9 * channels * channels * 2, 2 * MB),
        name="gate",
    )(reduce_full, index, in_hbm(w))


def gate_back_kernel(fixed, me, buffer, grad, reduce_ref, index, w, coarse_two, coarse_four, out, grad_w,
                     plain, moved, total, back):
    height, size, channels = reduce_ref.shape
    me = None if fixed else me
    plain[...] = reduce_ref[...].astype(f32).reshape(height, group, 8, channels)
    take_frames(moved, plain, index)
    g = grad[...].astype(f32)
    sum_two = add_columns(add_rows(g), 1)
    sum_four = add_columns(add_rows(sum_two), 2)
    two = sum_two.astype(bf16)
    four = sum_four.astype(bf16)
    small_weight(three_shifts(coarse_two[...].astype(f32), 2, 1), two, grad_w, me, 1, 0.5)
    small_weight(three_shifts(coarse_four[...].astype(f32), 4, 1), four, grad_w, me, 2, 0.25)
    back_two = small_conv_back(three_shifts(two.astype(f32), 2, -1), w.at[1])
    back_four = small_conv_back(three_shifts(four.astype(f32), 4, -1), w.at[2])
    diff = g + spread_rows(back_two * 0.25, 2) + spread_rows(back_four * 0.0625, 4)
    low = diff.astype(bf16)
    small_weight(three_shifts(moved[...].reshape(height, size, channels), 1, 1), low, grad_w, me, 0, 1.0)
    back[...] = small_conv_back(three_shifts(low.astype(f32), 1, -1), w.at[0]).reshape(
        height, group, 8, channels
    )
    total[...] = -diff.reshape(height, group, 8, channels)
    for f in range(group):
        total[:, index[f]] += back[:, f]
    out[...] = total[...].reshape(height, size, channels).astype(bf16)


def run_gate_back(me, fixed, buffer, layer, grad, reduce_full, index, w, coarse_two, coarse_four):
    height, size, channels = reduce_full.shape
    owners, total = buffer.shape[:2]
    per = gate_conv_rows(owners)
    return pl.pallas_call(
        functools.partial(gate_back_kernel, fixed),
        grid=(1,),
        in_specs=[smem, pl.BlockSpec(memory_space=pl.ANY), whole(grad), whole(reduce_full), smem,
                  pl.BlockSpec((None,) + w.shape[1:], lambda k: (layer, 0, 0, 0)),
                  whole(coarse_two), whole(coarse_four)],
        out_specs=(full((height, size, channels)),
                   pl.BlockSpec((owners, per, part), lambda k: (0, (total - per) // per, 0))),
        out_shape=(shape_of((height, size, channels), bf16), hbm_shape(buffer.shape, bf16)),
        scratch_shapes=[pltpu.VMEM((height, group, 8, channels), f32)] * 4,
        compiler_params=params(),
        cost_estimate=cost(2 * height * size * 9 * channels * channels * 4, 3 * MB),
        input_output_aliases={1: 1},
        name="gate_back",
    )(me, in_hbm(buffer), grad, reduce_full, index, in_hbm(w), coarse_two, coarse_four)


def small_kernel(counts, owners, channels, places, first, second, convs, expand):
    wide, per = counts[2], counts[3]
    for layer, ref in ((0, first), (1, second)):
        for owner in range(owners):
            where = places[layer, owner]
            value = ref[where].astype(f32)
            done = 0
            while done < wide:
                row = owner * wide + done
                length = min(wide - done, 128 - row % 128)
                lane = row // 128 * part
                expand[layer, row % 128 : row % 128 + length, lane : lane + part] = value[done : done + length]
                done += length
            done = 0
            while done < per and owner * per + done < 7 * 128:
                row = owner * per + done
                length = min(per - done, 128 - row % 128)
                for j in range(4):
                    block = row // 128 * 4 + j
                    if block < 27:
                        top = block % 9 * 128 + row % 128
                        convs[layer, block // 9, top : top + length, :] = value[
                            wide + done : wide + done + length, j * 128 : (j + 1) * 128
                        ]
                done += length


def run_small(halves, places, counts, owners, channels):
    shapes = (shape_of((2, 3, 9 * 128, 128), f32), shape_of((2, 128, channels), f32))
    return pl.pallas_call(
        functools.partial(small_kernel, counts, owners, channels),
        grid=(1,),
        in_specs=[smem, whole(halves[0]), whole(halves[1])],
        out_specs=tuple(full(s.shape) for s in shapes),
        out_shape=shapes,
        compiler_params=params(),
        cost_estimate=cost(0, 8 * MB),
        name="small",
    )(places, *halves)


def large_kernel(counts, owners, channels, wide0, wide1, proj0, proj1, proj, conv, out, red):
    for layer, (wide, first) in enumerate(((wide0, proj0), (wide1, proj1))):
        rows = channels // owners
        proj[layer] = first[0:rows, :].astype(f32)
        quarter = rows // 4
        for j in range(4):
            red[layer, j * quarter : (j + 1) * quarter, :] = first[
                rows : rows + quarter, j * 128 : (j + 1) * 128
            ].astype(f32)
        conv[layer] = wide[0 : counts[0], :].astype(f32)
        per = part // owners
        for k in range(channels // part):
            at_row = counts[0] + k * per
            out[layer, :, k * part : (k + 1) * part] = wide[at_row : at_row + per, :].astype(f32)


def run_large(wide, proj, counts, owners, channels):
    rows = channels // owners
    shapes = (
        shape_of((2, rows, part), f32),
        shape_of((2, counts[0], part), f32),
        shape_of((2, part // owners, channels), f32),
        shape_of((2, rows, 128), f32),
    )
    args = (*wide, *proj)
    return pl.pallas_call(
        functools.partial(large_kernel, counts, owners, channels),
        grid=(1,),
        in_specs=[whole(a) for a in args],
        out_specs=tuple(full(s.shape) for s in shapes),
        out_shape=shapes,
        compiler_params=params(),
        cost_estimate=cost(0, 8 * MB),
        name="large",
    )(*args)


def exchange(block):
    return lax.all_to_all(block, both, 0, 0, tiled=True)


def to_frames(own):
    space, rows, size, channels = own.shape
    return lax.all_to_all(own, "space", 0, 0, tiled=True).reshape(space * rows, size, channels)


def to_rows(all_rows, rows):
    height, size, channels = all_rows.shape
    return lax.all_to_all(all_rows.reshape(height // rows, rows, size, channels), "space", 0, 0, tiled=True)


def neighbours(low, high):
    count = lax.axis_size("space")
    from_low = lax.ppermute(high, "space", [(i, i + 1) for i in range(count - 1)])
    from_high = lax.ppermute(low, "space", [(i + 1, i) for i in range(count - 1)])
    return from_low, from_high


def add(left, right):
    return (left.astype(f32) + right.astype(f32)).astype(bf16)


def swap(block, bit):
    count = lax.axis_size("dp")
    return lax.ppermute(block, "dp", [(i, i ^ bit) for i in range(count)])


def core_sum(grad):
    half = grad.shape[0] // 2
    return grad[:half], swap(grad[half:], 1)


def gather_owners(own):
    count = lax.axis_size("dp")
    bits = chip_bits()
    half = len(bits) // 2
    mine = lax.axis_index("dp")
    rows = own.shape[0] // 2
    sequences = (bits + [1], bits[half:] + bits[:half] + [1])
    got = [own[None, which * rows : (which + 1) * rows] for which in range(2)]
    for stage in range(len(sequences[0])):
        got = together(*got)
        new = [swap(g, sequence[stage]) for g, sequence in zip(got, sequences)]
        got = [jnp.concatenate(pair, axis=0) for pair in zip(got, new)]
    places = []
    for sequence in sequences:
        row = []
        for owner in range(count):
            other = jnp.bitwise_xor(mine, owner)
            row.append(sum(jnp.where(other & bit, 1 << i, 0) for i, bit in enumerate(sequence)))
        places.append(jnp.stack(row))
    return got, jnp.stack(places).astype(jnp.int32)


def chip_bits():
    count = lax.axis_size("dp")
    bits = []
    bit = 2
    while bit < count:
        bits.append(bit)
        bit *= 2
    return bits


def reduce_start(kept, got):
    bits = chip_bits()
    rows, cols = kept.shape[1:]
    half = len(bits) // 2
    state = []
    for which, sequence in enumerate((bits, bits[half:] + bits[:half])):
        span = slice(which * (rows // 2), (which + 1) * (rows // 2))
        shape = (2,) * len(bits) + (rows // 2, cols)
        state.append((kept[:, span].reshape(shape), got[:, span].reshape(shape), bits, sequence))
    return reduce_step(state)


def reduce_step(state):
    stays, goes = [], []
    for keep, new, left, sequence in state:
        where = len(left) - 1 - left.index(sequence[0])
        stay, go = [
            add(
                lax.index_in_dim(keep, side, where, keepdims=False),
                lax.index_in_dim(new, side, where, keepdims=False),
            )
            for side in (0, 1)
        ]
        stays.append(stay)
        goes.append(go)
    goes = together(*goes)
    return [
        (stay, swap(go, sequence[0]), [b for b in left if b != sequence[0]], sequence[1:])
        for stay, go, (_, _, left, sequence) in zip(stays, goes, state)
    ]


def reduce_finish(state):
    while state[0][3]:
        state = reduce_step(state)
    return jnp.concatenate([add(keep, new) for keep, new, _, _ in state], axis=0)


def space_sum(value):
    count = lax.axis_size("space")
    rows, cols = value.shape
    parts = lax.all_to_all(value.reshape(count, rows // count, cols), "space", 0, 0, tiled=True)
    own = jnp.sum(parts.astype(f32), axis=0).astype(bf16)
    spread = jnp.broadcast_to(own[None], (count,) + own.shape)
    return lax.all_to_all(spread, "space", 0, 0, tiled=True).reshape(rows, cols)


def together(*values):
    return lax.optimization_barrier(values)


def body(
    clip_maps,
    next_frame,
    valid_rows,
    proj_in,
    conv_mid,
    proj_out,
    gate_reduce,
    gate_convs,
    gate_expand,
    norm_gain,
    norm_bias,
    out_grad,
):
    frames, rows, cols, channels = clip_maps.shape
    size = frames * cols
    space, here = lax.axis_size("space"), lax.axis_index("space")
    devices = lax.axis_size("dp") * space
    valid = valid_rows.astype(f32)
    mask = jnp.broadcast_to(valid.T[:, :, None], (rows, frames, cols)).reshape(rows, size, 1)
    edge = jnp.stack([(here > 0).astype(jnp.int32), (here < space - 1).astype(jnp.int32)])
    padded = jnp.pad(next_frame, (0, space * group - frames))
    own_next = lax.dynamic_slice_in_dim(padded, here * group, group)
    base = lax.axis_index("dp") * frames + here * group
    index = jnp.clip(own_next - base, 0, group - 1)
    count = exchange(jnp.full((devices, 1, 128), jnp.sum(valid) * cols))
    inv = 1.0 / jnp.sum(count, axis=0)

    def vectors(layer):
        out = []
        for source in (norm_gain, norm_bias):
            row = source[layer][None]
            out.append((row[:, :part], row[:, part : 2 * part], row[:, 2 * part :]))
        return out

    gains, biases = zip(vectors(0), vectors(1))
    owners = lax.axis_size("dp")
    firsts = [run_first(clip_maps, 0, proj_in, gate_reduce, mask, devices, space), None]
    sums_one, sums_two, sums_three = [None, None], [None, None], [None, None]
    seconds, hidden_twos, gates, reduces = [None, None], [None, None], [None, None], [None, None]
    gate_kept, halos, hidden_ones = [None, None], [None, None], [None, None]
    firsts[0] = list(firsts[0])
    for layer in range(2):
        gain, bias = gains[layer], biases[layer]
        first, red, pay, low, high = firsts[layer]
        sums_one[layer] = exchange(pay)
        halo = neighbours(low, high)
        reduces[layer] = to_frames(red)
        hidden_own, before = run_conv(
            first, sums_one[layer], inv, gain[0], bias[0], mask, layer, conv_mid
        )
        second, hidden_edge, pay, low, high = run_conv_edge(
            before, *halo, edge, sums_one[layer], inv, gain[0], bias[0], mask, layer, conv_mid
        )
        hidden_ones[layer] = hidden_own, hidden_edge
        seconds[layer] = second
        sums_two[layer] = exchange(pay)
        gate_full, *gate_kept[layer] = run_gate(layer, reduces[layer], index, gate_convs)
        sums_two[layer], gate_full = together(sums_two[layer], gate_full)
        gates[layer] = to_rows(gate_full, rows)
        hidden_twos[layer], pay = run_third(
            second, sums_two[layer], inv, gain[1], bias[1], mask, layer, proj_out
        )
        sums_three[layer] = exchange(pay)
        low, high = together(sums_three[layer], low, high)[1:]
        halos[layer] = neighbours(low, high)
        if layer == 0:
            mid, branch_zero, sig_zero, slope_zero, *firsts[1] = run_mid(
                0, hidden_twos[0], proj_out, sums_three[0], inv, gain[2], bias[2], clip_maps,
                gates[0], gate_expand, mask, proj_in, gate_reduce,
            )
            firsts[1][2], *halos[0] = together(firsts[1][2], *halos[0])
    out_maps, branch_one, grad_branch, grad_in, buffer, grad_gate, pay = run_last(
        owners, 1, hidden_twos[1], proj_out, sums_three[1], inv, gains[1][2], biases[1][2], mid,
        gates[1], gate_expand, mask, out_grad,
    )
    pay, *halos[1] = together(pay, *halos[1])
    branches = [branch_zero, branch_one]
    me = lax.axis_index("dp").astype(jnp.int32)[None]
    results = [None, None]
    vectors_of = [None, None]

    def scatter(grad):
        return lax.psum_scatter(grad, "dp", scatter_dimension=0, tiled=False)

    for layer in (1, 0):
        fixed = layer == 1
        gain, bias = gains[layer], biases[layer]
        first, second = firsts[layer][0], seconds[layer]
        back_three = exchange(pay)
        grad_full = to_frames(grad_gate)
        if layer == 0:
            grad_proj = run_weight(me, True, owners, mid, first_out, rows_out)
            back_three, grad_proj = together(back_three, grad_proj)
            results[1] = results[1] + (scatter(grad_proj),)
        buffer, part_two, pay, low, high = run_third_back(
            me, fixed, buffer, layer, grad_branch, branches[layer], back_three, sums_three[layer], inv,
            gain[2], bias[2], mask, hidden_twos[layer], proj_out, second, sums_two[layer],
            gain[1], bias[1],
        )
        back_two = exchange(pay)
        halo = neighbours(low, high)
        rows_full, buffer = run_gate_back(
            me, fixed, buffer, layer, grad_full, reduces[layer], index, gate_convs, *gate_kept[layer]
        )
        back_two, rows_full = together(back_two, rows_full)
        grad_second, before = run_conv_back(
            part_two, second, back_two, sums_two[layer], gain[1], bias[1], inv, mask, layer, conv_mid
        )
        grad_rows = to_rows(rows_full, rows)
        if layer == 0:
            before, scattered = together(before, results[1][0])
            results[1] = (scattered,) + results[1][1:]
        part_one, pay = run_conv_back_edge(
            before, *halo, *halos[layer], edge, back_two, sums_two[layer], gain[1], bias[1], inv, mask,
            layer, conv_mid, first, sums_one[layer], gain[0], bias[0],
        )
        pay, grad_second, grad_rows = together(pay, grad_second, grad_rows)
        back_one = exchange(pay)
        buffer = run_conv_weight(me, fixed, *hidden_ones[layer], grad_second, buffer)
        if layer == 0:
            back_one, buffer, scattered = together(back_one, buffer, results[1][1])
            results[1] = (results[1][0], scattered)
        else:
            back_one, buffer = together(back_one, buffer)
        common = (part_one, first, back_one, sums_one[layer], inv, gain[0], bias[0], mask, grad_rows)
        if layer == 1:
            results[1] = (scatter(buffer),)
            first_out, rows_out, grad_in, grad_branch, buffer, grad_gate, pay = run_between(
                me, owners, 1, *common, proj_in, gate_reduce, grad_in, slope_zero, sig_zero,
                branch_zero, gains[0][2], biases[0][2], gates[0], gate_expand,
            )
        else:
            wide_sum = core_sum(buffer)
            first_out, rows_out = run_first_back(*common)
            grad_proj = run_weight(me, False, owners, clip_maps, first_out, rows_out)
            wide_state = reduce_start(*wide_sum)
            grad_proj, *arrived = together(grad_proj, *[half[1] for half in wide_state])
            wide_state = [(half[0], new) + half[2:] for half, new in zip(wide_state, arrived)]
            results[0] = reduce_finish(wide_state), reduce_finish(reduce_start(*core_sum(grad_proj)))
            grad_maps = run_input(0, first_out, rows_out, proj_in, gate_reduce, grad_in, mask, frames)
        vecs = [jnp.sum(back, axis=0) for back in (back_one, back_two, back_three)]

        def pick(which):
            return jnp.concatenate(
                [v.reshape(-1, 2, 4, 128)[:, which].reshape(-1) for v in vecs]
            )

        vectors_of[layer] = pick(1), pick(0)

    counts = wide_rows(owners, channels)
    ends = [sum(counts[: i + 1]) for i in range(4)]
    wide, proj = results[0]
    wide, *later = together(wide, *lax.psum(results[1], "space"))
    wide = space_sum(wide)
    proj = space_sum(proj)
    halves, places = gather_owners(jnp.concatenate([v[ends[1] :] for v in (wide, later[0])], axis=0))
    convs, expand = run_small(halves, places, counts, owners, channels)
    large = run_large([wide, later[0]], [proj, later[1]], counts, owners, channels)
    little = [jnp.stack(pair) for pair in zip(*vectors_of)]
    return (out_maps, grad_maps, *large, convs, expand, *little)


def solution(mesh):
    maps = P("dp", "space", None, None)
    in_specs = (maps, P("dp"), P("dp", "space")) + (P(),) * 8 + (maps,)
    out_specs = (maps, maps) + (P(None, "dp", None),) * 4 + (P(),) * 4
    return jax.shard_map(body, mesh=mesh, in_specs=in_specs, out_specs=out_specs, check_vma=False)
```

time: 805 us -> 646 us (0.80)
  Pallas kernels: 0 us -> 219 us
  matrix products: 169 us -> 0 us
  other arithmetic: 125 us -> 25.4 us
  local copies, waits for them, and re-layouts: 117 us -> 25.2 us
  waiting for transfers between devices: 217 us -> 143 us
  blocking collectives: 0 us -> 53 us
    pallas_call x0 -> x28, Pallas kernels: none -> 219 us  [the longest x2 24.3 us: run_third_back(): pl.pallas_call(functools.partial(third_back_kernel, rows, size, steps, fi...]
    dot_general x48 -> x0, matrix products: 169 us -> none  [the longest x22 81.2 us: mm(): return jnp.dot(left, right, preferred_element_type=f32)]
    ppermute x31 -> x28, waiting for transfers between devices: 109 us -> 38.7 us  [the longest x16 38.7 us: swap(): return lax.ppermute(block, 'dp', [(i, i ^ bit) for i in range(count)])]
    all_to_all x0 -> x3, blocking collectives: none -> 53 us  [exchange(): return lax.all_to_all(block, both, 0, 0, tiled=True)]
    convert_element_type x35 -> x12, other arithmetic: 55.1 us -> 10.4 us  [add(): return (left.astype(f32) + right.astype(f32)).astype(bf16)]
    transpose x6 -> x0, local copies, waits for them, and re-layouts: 20.6 us -> none  [flip_weight(): return jnp.swapaxes(tap_blocks, 1, 2).reshape(-1, channels_in)]
    all_to_all x20 -> x22, starting transfers between devices: 87.3 us -> 106 us  [the longest x10 55.2 us: exchange(): return lax.all_to_all(block, both, 0, 0, tiled=True)]
    unnamed x402 -> x100, local copies, waits for them, and re-layouts: 28.5 us -> 10.4 us
  transfers between devices with their start and end apart: 55 -> 53, of which waited for: 26 -> 22; matrix products, arithmetic and copies ran while one was open for 30% -> 5% of each run, Pallas kernels for 0% -> 32%
where the time goes in v2:
time: 646 us; the launch traced here: 634 us
  Pallas kernels  219 us (34%)
  starting transfers between devices  153 us (24%)
  waiting for transfers between devices  143 us (22%)
  blocking collectives  53 us (8%)
  other arithmetic  25.4 us (4%)
  local copies, waits for them, and re-layouts  25.2 us (4%)
  between operations  15.7 us (2%)
    all_to_all x10, starting transfers between devices, exchange(): return lax.all_to_all(block, both, 0, 0, tiled=True)  55.2 us
    all_to_all x3, blocking collectives, exchange(): return lax.all_to_all(block, both, 0, 0, tiled=True)  53 us
    ppermute x16, waiting for transfers between devices, swap(): return lax.ppermute(block, 'dp', [(i, i ^ bit) for i in range(count)])  38.7 us
    pallas_call x2, Pallas kernels, run_third_back(): pl.pallas_call(functools.partial(third_back_kernel, rows, size, steps, fi...  24.3 us
    all_to_all x2, waiting for transfers between devices, space_sum(): lax.all_to_all(value.reshape(count, rows // count, cols), 'space', 0, 0,...  24.1 us
    ppermute x6, starting transfers between devices, neighbours(): lax.ppermute(high, 'space', [(i, i + 1) for i in range(count - 1)])  22.7 us
    all_to_all x10, waiting for transfers between devices, exchange(): return lax.all_to_all(block, both, 0, 0, tiled=True)  22.4 us
    psum x1, waiting for transfers between devices, body(): wide, *later = together(wide, *lax.psum(results[1], 'space'))  22.2 us
  transfers between devices with their start and end apart: 53, of which 22 were waited for; matrix products, arithmetic and copies ran while one was open for 5% of the time, Pallas kernels for 32%

profile of v2, /device:TPU:0, one launch (start us, length us, event | category | flops | bytes accessed | tf_op | source)
XLA Modules:
  0.0 634.4 jit_solution(7719069974142082644)
XLA Ops:
  9.7 7.3 %all-to-all-start.1 = ((f32[32,1,128]{2,1,0:T(1,128)}), f32[32,1,128]{2,1,0:T(1,128)S(1)}, u32[]{:S(2)}, u32[]{:S(2)}) async-start(f32[32,1,128]{2,1,0:T(1,128)} %broadcast_in_dim.15), calls=%async_computation.1 | async-start | bytes 32768 | tf_op jit(solution)/shard_map/all_to_all | solution.py:1354
  18.7 9.0 %first.1 = (f32[2,384,512]{2,1,0:T(8,128)}, bf16[4,2,128,128]{3,2,1,0:T(8,128)(2,1)}, f32[32,8,128]{2,1,0:T(8,128)}, bf16[400,512]{1,0:T(8,128)(2,1)}, bf16[400,512]{1,0:T(8,128)(2,1)}) custom-call(bf16[48,2,8,2048]{3,2,1,0:T(8,128)(2,1)} %x.7, bf16[2,2048,512]{2,1,0:T(8,128)(2,1)} %w_in.3, bf16[2,2048,128]{2,1,0:T(8,128)(2,1)} %w_red.5, ...), custom_call_target="tpu_custom_call" | custom-call | flops 503316480 | bytes 2097152 | tf_op jit(solution)/shard_map/first/pallas_call | solution.py:226
  46.6 7.7 %conv.2 = (bf16[2,384,512]{2,1,0:T(8,128)(2,1)}, f32[2,384,512]{2,1,0:T(8,128)}) custom-call(f32[2,384,512]{2,1,0:T(8,128)} %get-tuple-element.145.first, f32[32,8,128]{2,1,0:T(8,128)} %copy-done.7, f32[1,128]{1,0:T(1,128)} %divide_bitcast_fusion.inv, f32[1,512]{1,0:T(1,128)} %get-tuple-element.314.gain.gain_one, f32[1,512]{1,0:T(1,128)} %get-tuple-element.297.bias.bias_one, ...), custom_call_target="tpu_custom_call" | custom-call | flops 603979776 | bytes 2097152 | tf_op jit(solution)/shard_map/conv/pallas_call | solution.py:300
  82.5 17.7 %all_to_all.125.sums = f32[32,32,128]{2,1,0:T(8,128)} all-to-all(f32[32,32,128]{2,1,0:T(8,128)} %get-tuple-element.156), channel_id=1, replica_groups=mesh['dp'=8,'space'=4] {'dp','space'}, dimensions={0} | all-to-all | bytes 1048576 | tf_op jit(solution)/shard_map/all_to_all | solution.py:1354
  115.0 15.1 %mid.1 = (bf16[2,384,2048]{2,1,0:T(8,128)(2,1)}, bf16[2,384,2048]{2,1,0:T(8,128)(2,1)}, bf16[2,384,2048]{2,1,0:T(8,128)(2,1)}, bf16[2,384,2048]{2,1,0:T(8,128)(2...) custom-call(bf16[2,384,512]{2,1,0:T(8,128)(2,1)} %get-tuple-element., ...), custom_call_target="tpu_custom_call" | custom-call | flops 1006632960 | bytes 5242880 | tf_op jit(solution)/shard_map/mid/pallas_call | solution.py:494
  144.9 7.8 %conv.3 = (bf16[2,384,512]{2,1,0:T(8,128)(2,1)}, f32[2,384,512]{2,1,0:T(8,128)}) custom-call(f32[2,384,512]{2,1,0:T(8,128)} %get-tuple-element.158.first, f32[32,8,128]{2,1,0:T(8,128)} %copy-done.6, f32[1,128]{1,0:T(1,128)} %divide_bitcast_fusion.inv, f32[1,512]{1,0:T(1,128)} %get-tuple-element.316.gain.gain_one, f32[1,512]{1,0:T(1,128)} %get-tuple-element.295.bias.bias_one, ...), custom_call_target="tpu_custom_call" | custom-call | flops 603979776 | bytes 2097152 | tf_op jit(solution)/shard_map/conv/pallas_call | solution.py:300
  180.2 17.7 %all_to_all.126.sums = f32[32,32,128]{2,1,0:T(8,128)} all-to-all(f32[32,32,128]{2,1,0:T(8,128)} %get-tuple-element.174), channel_id=1, replica_groups=mesh['dp'=8,'space'=4] {'dp','space'}, dimensions={0} | all-to-all | bytes 1048576 | tf_op jit(solution)/shard_map/all_to_all | solution.py:1354
  212.8 15.8 %last.1 = (bf16[48,2,8,2048]{3,2,1,0:T(8,128)(2,1)}, bf16[2,384,2048]{2,1,0:T(8,128)(2,1)}, bf16[2,384,2048]{2,1,0:T(8,128)(2,1)}, bf16[2,384,2048]{2,1,0:T(8,12...) custom-call(bf16[2,384,512]{2,1,0:T(8,128)(2,1)} %get-tuple-element.173.hidden, ...), custom_call_target="tpu_custom_call" | custom-call | flops 805306368 | bytes 5242880 | tf_op jit(solution)/shard_map/last/pallas_call | solution.py:623
  228.7 17.7 %all_to_all.127.back_sums = f32[32,32,128]{2,1,0:T(8,128)} all-to-all(f32[32,32,128]{2,1,0:T(8,128)} %get-tuple-element.186), channel_id=1, replica_groups=mesh['dp'=8,'space'=4] {'dp','space'}, dimensions={0} | all-to-all | bytes 1048576 | tf_op jit(solution)/shard_map/all_to_all | solution.py:1354
  250.4 12.1 %third_back.2 = (bf16[8,1008,512]{2,1,0:T(8,128)(2,1)}, f32[2,384,512]{2,1,0:T(8,128)}, f32[32,8,128]{2,1,0:T(8,128)}, bf16[400,512]{1,0:T(8,128)(2,1)}, bf16[400,512]{1,0:T(8,128)(2,1)}) custom-call(s32[1]{0:T(128)} %bitcast.9.me, bf16[8,1008,512]{2,1,0:T(8,128)(2,1)} %get-tuple-element.178.buffer, ...), custom_call_target="tpu_custom_call", output_to_operand_aliasing={{0}: (1, {})} | custom-call | flops 805306368 | bytes 3145728 | tf_op jit(solution)/shard_map/third_back/pallas_call | solution.py:718
  284.1 8.1 %conv_back.2 = (bf16[2,384,512]{2,1,0:T(8,128)(2,1)}, f32[2,384,512]{2,1,0:T(8,128)}) custom-call(f32[2,384,512]{2,1,0:T(8,128)} %get-tuple-element.187.part_two, f32[2,384,512]{2,1,0:T(8,128)} %get-tuple-element.168.second, f32[32,8,128]{2,1,0:T(8,128)} %copy-done.13, f32[32,8,128]{2,1,0:T(8,128)} %copy-done.9, f32[1,512]{1,0:T(1,128)} %get-tuple-element.317.gain.gain_two, ...), custom_call_target="tpu_custom_call" | custom-call | flops 603979776 | bytes 2097152 | tf_op jit(solution)/shard_map/conv_back/pallas_call | solution.py:780
  306.2 8.1 %conv_weight.2 = bf16[8,1008,512]{2,1,0:T(8,128)(2,1)} custom-call(s32[1]{0:T(128)} %bitcast.9.me, bf16[2,384,512]{2,1,0:T(8,128)(2,1)} %get-tuple-element.205.hidden, bf16[2,384,512]{2,1,0:T(8,128)(2,1)} %get-tuple-element.206.hidden_edge, bf16[2,384,512]{2,1,0:T(8,128)(2,1)} %get-tuple-element.207.grad_second, ...), custom_call_target="tpu_custom_call", output_to_operand_aliasing={{}: (4, {})} | custom-call | flops 905969664 | bytes 2097152 | tf_op jit(solution)/shard_map/conv_weight/pallas_call | solution.py:898
  315.3 16.7 %between.1 = (bf16[2,384,512]{2,1,0:T(8,128)(2,1)}, bf16[2,384,128]{2,1,0:T(8,128)(2,1)}, bf16[2,384,2048]{2,1,0:T(8,128)(2,1)}, bf16[2,384,2048]{2,1,0:T(8,128)...) custom-call(f32[2,384,512]{2,1,0:T(8,128)} %get-tuple-element.200.part_one, ...), custom_call_target="tpu_custom_call" | custom-call | flops 805306368 | bytes 5242880 | tf_op jit(solution)/shard_map/between/pallas_call | solution.py:988
  337.6 7.4 %weight.2 = bf16[8,320,512]{2,1,0:T(8,128)(2,1)} custom-call(s32[1]{0:T(128)} %bitcast.9.me, bf16[2,384,2048]{2,1,0:T(8,128)(2,1)} %get-tuple-element.175.x, bf16[2,384,512]{2,1,0:T(8,128)(2,1)} %get-tuple-element.218.first_out, bf16[2,384,128]{2,1,0:T(8,128)(2,1)} %get-tuple-element.219.rows_out), custom_call_target="tpu_custom_call" | custom-call | flops 503316480 | bytes 2097152 | tf_op jit(solution)/shard_map/weight/pallas_call | solution.py:1104
  356.1 12.2 %third_back.3 = (bf16[8,1008,512]{2,1,0:T(8,128)(2,1)}, f32[2,384,512]{2,1,0:T(8,128)}, f32[32,8,128]{2,1,0:T(8,128)}, bf16[400,512]{1,0:T(8,128)(2,1)}, bf16[400,512]{1,0:T(8,128)(2,1)}) custom-call(s32[1]{0:T(128)} %bitcast.9.me, bf16[8,1008,512]{2,1,0:T(8,128)(2,1)} %get-tuple-element.215.buffer, ...), custom_call_target="tpu_custom_call", output_to_operand_aliasing={{0}: (1, {})} | custom-call | flops 805306368 | bytes 3145728 | tf_op jit(solution)/shard_map/third_back/pallas_call | solution.py:718
  390.2 8.2 %conv_back.3 = (bf16[2,384,512]{2,1,0:T(8,128)(2,1)}, f32[2,384,512]{2,1,0:T(8,128)}) custom-call(f32[2,384,512]{2,1,0:T(8,128)} %get-tuple-element.221.part_two, f32[2,384,512]{2,1,0:T(8,128)} %get-tuple-element.150.second, f32[32,8,128]{2,1,0:T(8,128)} %copy-done.15, f32[32,8,128]{2,1,0:T(8,128)} %copy-done.8, f32[1,512]{1,0:T(1,128)} %get-tuple-element.315.gain.gain_two, ...), custom_call_target="tpu_custom_call" | custom-call | flops 603979776 | bytes 2097152 | tf_op jit(solution)/shard_map/conv_back/pallas_call | solution.py:780
  399.9 7.3 %conv_back_edge.3 = (f32[2,384,512]{2,1,0:T(8,128)}, f32[32,8,128]{2,1,0:T(8,128)}) custom-call(f32[2,384,512]{2,1,0:T(8,128)} %get-tuple-element.231.before, bf16[400,512]{1,0:T(8,128)(2,1)} %copy-done.33, bf16[400,512]{1,0:T(8,128)(2,1)} %copy-done.34, bf16[400,512]{1,0:T(8,128)(2,1)} %copy-done.29, bf16[400,512]{1,0:T(8,128)(2,1)} %copy-done.30, ...), custom_call_target="tpu_custom_call" | custom-call | flops 301989888 | bytes 2097152 | tf_op jit(solution)/shard_map/conv_back_edge/pallas_call | solution.py:851
  413.5 8.1 %conv_weight.3 = bf16[8,1008,512]{2,1,0:T(8,128)(2,1)} custom-call(s32[1]{0:T(128)} %bitcast.9.me, bf16[2,384,512]{2,1,0:T(8,128)(2,1)} %get-tuple-element.241.hidden, bf16[2,384,512]{2,1,0:T(8,128)(2,1)} %get-tuple-element.242.hidden_edge, bf16[2,384,512]{2,1,0:T(8,128)(2,1)} %get-tuple-element.243.grad_second, ...), custom_call_target="tpu_custom_call", output_to_operand_aliasing={{}: (4, {})} | custom-call | flops 905969664 | bytes 2097152 | tf_op jit(solution)/shard_map/conv_weight/pallas_call | solution.py:898
  421.7 16.9 %reduce-scatter.5.cloned.1.call-done = bf16[1,320,512]{2,1,0:T(8,128)(2,1)} async-done(((bf16[8,320,512]{2,1,0:T(8,128)(2,1)}), bf16[1,320,512]{2,1,0:T(8,128)(2,1)}) %reduce-scatter.5.cloned.1.call-update) | async-done | bytes 327696 | tf_op jit(solution)/shard_map/reduce_scatter | solution.py:1554
  464.3 12.5 %collective-permute-done.13 = bf16[2,504,512]{2,1,0:T(8,128)(2,1)} collective-permute-done((bf16[2,504,512]{2,1,0:T(8,128)(2,1)}, bf16[2,504,512]{2,1,0:T(8,128)(2,1)}, u32[]{:S(2)}, u32[]{:S(2)}) %collective-permute-start.13) | collective-permute-done | bytes 1032224 | tf_op jit(solution)/shard_map/ppermute | solution.py:1380
  481.6 10.7 %collective-permute-done.15 = bf16[504,512]{1,0:T(8,128)(2,1)S(1)} collective-permute-done((bf16[504,512]{1,0:T(8,128)(2,1)S(1)}, bf16[504,512]{1,0:T(8,128)(2,1)S(1)}, u32[]{:S(2)}, u32[]{:S(2)}) %collective-permute-start.15) | collective-permute-done | bytes 516128 | tf_op jit(solution)/shard_map/ppermute | solution.py:1380
  494.0 22.2 %all-reduce.4.cloned.1.call-done = (bf16[1008,512]{1,0:T(8,128)(2,1)}, bf16[320,512]{1,0:T(8,128)(2,1)}) async-done(((bf16[1008,512]{1,0:T(8,128)(2,1)}, bf16[320,512]{1,0:T(8,128)(2,1)}), (bf16[1008,512]{1,0:T(8,128)(2,1)}, bf16[320,512]{1,0:T(8,128)(2,1)})) %all-reduce.4.cloned.1.call-update) | async-done | bytes 1359888 | tf_op jit(solution)/shard_map/psum | solution.py:1624
  527.4 20.3 %all-to-all-done.21 = bf16[4,252,512]{2,1,0:T(8,128)(2,1)} async-done(((bf16[4,252,512]{2,1,0:T(8,128)(2,1)}), bf16[4,252,512]{2,1,0:T(8,128)(2,1)}, u32[]{:S(2)}, u32[]{:S(2)}) %all-to-all-start.21) | async-done | bytes 1032224 | tf_op jit(solution)/shard_map/all_to_all | solution.py:1461
  569.6 10.1 %all-to-all-done.22 = bf16[4,252,512]{2,1,0:T(8,128)(2,1)} async-done(((bf16[4,252,512]{2,1,0:T(8,128)(2,1)}), bf16[4,252,512]{2,1,0:T(8,128)(2,1)}, u32[]{:S(2)}, u32[]{:S(2)}) %all-to-all-start.22) | async-done | bytes 1032224 | tf_op jit(solution)/shard_map/all_to_all | solution.py:1464
  (282 shorter events, 321.9 us)
Async XLA Ops:
  33.5 20.8 %collective-permute-start = (bf16[400,512]{1,0:T(8,128)(2,1)}, bf16[400,512]{1,0:T(8,128)(2,1)S(1)}, u32[]{:S(2)}, u32[]{:S(2)}) collective-permute-start(bf16[400,512]{1,0:T(8,128)(2,1)} %get-tuple-element.148), channel_id=1, source_target_pairs={{0,1},{1,2},{2,3},{4,5},{5,6},{6,7},{8,9},{9,10},{10,11},{12,13},{... | collective-permute-start | bytes 1228808 | tf_op jit(solution)/shard_map/ppermute | solution.py:1369
  104.2 26.0 %collective-permute-start.2 = (bf16[400,512]{1,0:T(8,128)(2,1)S(1)}, bf16[400,512]{1,0:T(8,128)(2,1)S(1)}, u32[]{:S(2)}, u32[]{:S(2)}) collective-permute-start(bf16[400,512]{1,0:T(8,128)(2,1)S(1)} %copy-done.47), channel_id=1, source_target_pairs={{0,1},{1,2},{2,3},{4,5},{5,6},{6,7},{8,9},{9,10},{10,11},{12,13},{... | collective-permute-start | bytes 1228808 | tf_op jit(solution)/shard_map/ppermute | solution.py:1369
  108.1 22.1 %collective-permute-start.3 = (bf16[400,512]{1,0:T(8,128)(2,1)S(1)}, bf16[400,512]{1,0:T(8,128)(2,1)S(1)}, u32[]{:S(2)}, u32[]{:S(2)}) collective-permute-start(bf16[400,512]{1,0:T(8,128)(2,1)S(1)} %copy-done.46), channel_id=1, source_target_pairs={{1,0},{2,1},{3,2},{5,4},{6,5},{7,6},{9,8},{10,9},{11,10},{13,12},{... | collective-permute-start | bytes 1228808 | tf_op jit(solution)/shard_map/ppermute | solution.py:1370
  201.9 26.7 %collective-permute-start.6 = (bf16[400,512]{1,0:T(8,128)(2,1)S(1)}, bf16[400,512]{1,0:T(8,128)(2,1)S(1)}, u32[]{:S(2)}, u32[]{:S(2)}) collective-permute-start(bf16[400,512]{1,0:T(8,128)(2,1)S(1)} %copy-done.49), channel_id=1, source_target_pairs={{0,1},{1,2},{2,3},{4,5},{5,6},{6,7},{8,9},{9,10},{10,11},{12,13},{... | collective-permute-start | bytes 1228808 | tf_op jit(solution)/shard_map/ppermute | solution.py:1369
  205.9 22.8 %collective-permute-start.7 = (bf16[400,512]{1,0:T(8,128)(2,1)S(1)}, bf16[400,512]{1,0:T(8,128)(2,1)S(1)}, u32[]{:S(2)}, u32[]{:S(2)}) collective-permute-start(bf16[400,512]{1,0:T(8,128)(2,1)S(1)} %copy-done.48), channel_id=1, source_target_pairs={{1,0},{2,1},{3,2},{5,4},{6,5},{7,6},{9,8},{10,9},{11,10},{13,12},{... | collective-permute-start | bytes 1228808 | tf_op jit(solution)/shard_map/ppermute | solution.py:1370
  267.7 24.5 %collective-permute-start.8 = (bf16[400,512]{1,0:T(8,128)(2,1)}, bf16[400,512]{1,0:T(8,128)(2,1)S(1)}, u32[]{:S(2)}, u32[]{:S(2)}) collective-permute-start(bf16[400,512]{1,0:T(8,128)(2,1)} %get-tuple-element.196), channel_id=1, source_target_pairs={{0,1},{1,2},{2,3},{4,5},{5,6},{6,7},{8,9},{9,10},{10,11},{12,13},{... | collective-permute-start | bytes 1228808 | tf_op jit(solution)/shard_map/ppermute | solution.py:1369
  271.4 20.8 %collective-permute-start.9 = (bf16[400,512]{1,0:T(8,128)(2,1)}, bf16[400,512]{1,0:T(8,128)(2,1)S(1)}, u32[]{:S(2)}, u32[]{:S(2)}) collective-permute-start(bf16[400,512]{1,0:T(8,128)(2,1)} %get-tuple-element.197), channel_id=1, source_target_pairs={{1,0},{2,1},{3,2},{5,4},{6,5},{7,6},{9,8},{10,9},{11,10},{13,12},{... | collective-permute-start | bytes 1228808 | tf_op jit(solution)/shard_map/ppermute | solution.py:1370
  278.0 22.1 %all-to-all-start.14 = ((bf16[4,2,128,128]{3,2,1,0:T(8,128)(2,1)}), bf16[4,2,128,128]{3,2,1,0:T(8,128)(2,1)S(1)}, u32[]{:S(2)}, u32[]{:S(2)}) async-start(bf16[4,2,128,128]{3,2,1,0:T(8,128)(2,1)} %bitcast.142), calls=%async_computation.14 | async-start | bytes 524288 | tf_op jit(solution)/shard_map/all_to_all | solution.py:1364
  306.2 92.2 %reduce-scatter.3.cloned.1.call-start = ((), (), s32[]{:S(2)}) async-start(), calls=%async_computation.27 | async-start | bytes 9289728 | tf_op jit(solution)/shard_map/reduce_scatter | solution.py:1554
  332.0 20.0 %all-to-all-start.16 = ((f32[32,32,128]{2,1,0:T(8,128)}), f32[32,32,128]{2,1,0:T(8,128)S(1)}, u32[]{:S(2)}, u32[]{:S(2)}) async-start(f32[32,32,128]{2,1,0:T(8,128)} %get-tuple-element.217), calls=%async_computation.16 | async-start | bytes 1048576 | tf_op jit(solution)/shard_map/all_to_all | solution.py:1354
  337.5 101.0 %reduce-scatter.5.cloned.1.call-start = ((), (), s32[]{:S(2)}) async-start(), calls=%async_computation.28 | async-start | bytes 2949120 | tf_op jit(solution)/shard_map/reduce_scatter | solution.py:1554
  374.1 24.3 %collective-permute-start.10 = (bf16[400,512]{1,0:T(8,128)(2,1)}, bf16[400,512]{1,0:T(8,128)(2,1)S(1)}, u32[]{:S(2)}, u32[]{:S(2)}) collective-permute-start(bf16[400,512]{1,0:T(8,128)(2,1)} %get-tuple-element.232), channel_id=1, source_target_pairs={{0,1},{1,2},{2,3},{4,5},{5,6},{6,7},{8,9},{9,10},{10,11},{12,13},{... | collective-permute-start | bytes 1228808 | tf_op jit(solution)/shard_map/ppermute | solution.py:1369
  377.8 20.7 %collective-permute-start.11 = (bf16[400,512]{1,0:T(8,128)(2,1)}, bf16[400,512]{1,0:T(8,128)(2,1)S(1)}, u32[]{:S(2)}, u32[]{:S(2)}) collective-permute-start(bf16[400,512]{1,0:T(8,128)(2,1)} %get-tuple-element.233), channel_id=1, source_target_pairs={{1,0},{2,1},{3,2},{5,4},{6,5},{7,6},{9,8},{10,9},{11,10},{13,12},{... | collective-permute-start | bytes 1228808 | tf_op jit(solution)/shard_map/ppermute | solution.py:1370
  384.4 22.9 %all-to-all-start.19 = ((bf16[4,2,128,128]{3,2,1,0:T(8,128)(2,1)}), bf16[4,2,128,128]{3,2,1,0:T(8,128)(2,1)S(1)}, u32[]{:S(2)}, u32[]{:S(2)}) async-start(bf16[4,2,128,128]{3,2,1,0:T(8,128)(2,1)} %bitcast.141), calls=%async_computation.20 | async-start | bytes 524288 | tf_op jit(solution)/shard_map/all_to_all | solution.py:1364
  407.3 31.3 %all-to-all-start.20 = ((f32[32,8,128]{2,1,0:T(8,128)}), f32[32,8,128]{2,1,0:T(8,128)S(1)}, u32[]{:S(2)}, u32[]{:S(2)}) async-start(f32[32,8,128]{2,1,0:T(8,128)} %get-tuple-element.240), calls=%async_computation.21 | async-start | bytes 262144 | tf_op jit(solution)/shard_map/all_to_all | solution.py:1354
  413.3 102.8 %all-reduce.4.cloned.1.call-start = ((), (), s32[]{:S(2)}) async-start(), calls=%async_computation.29 | async-start | bytes 2719744 | tf_op jit(solution)/shard_map/psum | solution.py:1624
  451.7 25.2 %collective-permute-start.13 = (bf16[2,504,512]{2,1,0:T(8,128)(2,1)}, bf16[2,504,512]{2,1,0:T(8,128)(2,1)}, u32[]{:S(2)}, u32[]{:S(2)}) collective-permute-start(bf16[2,504,512]{2,1,0:T(8,128)(2,1)} %get-tuple-element.252), channel_id=1, source_target_pairs={{0,8},{4,12},{8,0},{12,4},{16,24},{20,28},{24,16},{28,20},{1,9},{5... | collective-permute-start | bytes 3096584 | tf_op jit(solution)/shard_map/ppermute | solution.py:1380
  453.1 24.8 %collective-permute-start.14 = (bf16[2,504,512]{2,1,0:T(8,128)(2,1)}, bf16[2,504,512]{2,1,0:T(8,128)(2,1)S(1)}, u32[]{:S(2)}, u32[]{:S(2)}) collective-permute-start(bf16[2,504,512]{2,1,0:T(8,128)(2,1)} %get-tuple-element.253), channel_id=1, source_target_pairs={{0,16},{4,20},{8,24},{12,28},{16,0},{20,4},{24,8},{28,12},{1,17},{... | collective-permute-start | bytes 3096584 | tf_op jit(solution)/shard_map/ppermute | solution.py:1380
  517.3 30.4 %all-to-all-start.21 = ((bf16[4,252,512]{2,1,0:T(8,128)(2,1)}), bf16[4,252,512]{2,1,0:T(8,128)(2,1)}, u32[]{:S(2)}, u32[]{:S(2)}) async-start(bf16[4,252,512]{2,1,0:T(8,128)(2,1)} %reshape.208), calls=%async_computation.23 | async-start | bytes 2097152 | tf_op jit(solution)/shard_map/all_to_all | solution.py:1461
  524.7 29.9 %collective-permute-start.17 = (bf16[4,320,512]{2,1,0:T(8,128)(2,1)}, bf16[4,320,512]{2,1,0:T(8,128)(2,1)}, u32[]{:S(2)}, u32[]{:S(2)}) collective-permute-start(bf16[4,320,512]{2,1,0:T(8,128)(2,1)} %slice.271), channel_id=1, source_target_pairs={{0,4},{4,0},{8,12},{12,8},{16,20},{20,16},{24,28},{28,24},{1,5},{5... | collective-permute-start | bytes 3932168 | tf_op jit(solution)/shard_map/ppermute | solution.py:1380
  550.2 29.6 %all-to-all-start.22 = ((bf16[4,252,512]{2,1,0:T(8,128)(2,1)}), bf16[4,252,512]{2,1,0:T(8,128)(2,1)}, u32[]{:S(2)}, u32[]{:S(2)}) async-start(bf16[4,252,512]{2,1,0:T(8,128)(2,1)} %broadcast_in_dim.33), calls=%async_computation.24 | async-start | bytes 2097152 | tf_op jit(solution)/shard_map/all_to_all | solution.py:1464
  568.2 22.2 %collective-permute-start.21 = (bf16[160,512]{1,0:T(8,128)(2,1)}, bf16[160,512]{1,0:T(8,128)(2,1)}, u32[]{:S(2)}, u32[]{:S(2)}) collective-permute-start(bf16[160,512]{1,0:T(8,128)(2,1)} %fusion.14), channel_id=1, source_target_pairs={{0,8},{4,12},{8,0},{12,4},{16,24},{20,28},{24,16},{28,20},{1,9},{5... | collective-permute-start | bytes 491528 | tf_op jit(solution)/shard_map/ppermute | solution.py:1380
  597.8 21.6 %collective-permute-start.27 = (bf16[4,176,512]{2,1,0:T(8,128)(2,1)S(1)}, bf16[4,176,512]{2,1,0:T(8,128)(2,1)}, u32[]{:S(2)}, u32[]{:S(2)}) collective-permute-start(bf16[4,176,512]{2,1,0:T(8,128)(2,1)S(1)} %pad_maximum_fusion.4), channel_id=1, source_target_pairs={{0,4},{4,0},{8,12},{12,8},{16,20},{20,16},{24,28},{28,24},{1,5},{5... | collective-permute-start | bytes 2162696 | tf_op jit(solution)/shard_map/ppermute | solution.py:1380
  597.9 23.9 %collective-permute-start.26 = (bf16[4,176,512]{2,1,0:T(8,128)(2,1)S(1)}, bf16[4,176,512]{2,1,0:T(8,128)(2,1)S(1)}, u32[]{:S(2)}, u32[]{:S(2)}) collective-permute-start(bf16[4,176,512]{2,1,0:T(8,128)(2,1)S(1)} %pad_maximum_fusion.3), channel_id=1, source_target_pairs={{0,4},{4,0},{8,12},{12,8},{16,20},{20,16},{24,28},{28,24},{1,5},{5... | collective-permute-start | bytes 2162696 | tf_op jit(solution)/shard_map/ppermute | solution.py:1380
  (79 other events, 840.8 us)
Sparse Core Ops, SparseCore 0:
  314.7 76.1 reduce-scatter.2
  394.7 43.8 reduce-scatter.4
  453.9 62.2 all-reduce.3

commit v3 on v2

--- a/solution.py
+++ b/solution.py
@@ -68,7 +68,7 @@
 
 def store_pair(ref, first, second):
     rows = jnp.concatenate([unlanes(first), unlanes(second)], axis=0)
-    ref[...] = jnp.broadcast_to(rows[None], (ref.shape[0], 8, 128))
+    ref[:, 0:8, :] = jnp.broadcast_to(rows[None], (ref.shape[0], 8, 128))
 
 
 def fold(value):
@@ -181,6 +181,12 @@
     s, q = loop(size // chunk, piece, (zero, zero))
     s, q = squash(s), squash(q)
     store_pair(pay, s, q)
+    if pay.shape[1] > 8:
+        total = mask_ref[0]
+        for r in range(1, rows):
+            total = total + mask_ref[r]
+        total = jnp.broadcast_to(jnp.sum(total, axis=0, keepdims=True), (1, 128))
+        pay[:, 8:9, :] = jnp.broadcast_to(total[None], (pay.shape[0], 1, 128))
     store_halo(low, high, lambda r, i: first[r, at(i), :], mask_ref, s, rows, size)
     store_reduce(red, acc_red, mask_ref, rows, size)
 
@@ -206,11 +212,11 @@
         finish_first(acc, acc_red, mask, first, red, pay, low, high, rows, size)
 
 
-def first_outputs(rows, size, devices, space, reduced):
+def first_outputs(rows, size, devices, space, reduced, pay_rows=8):
     shapes = (
         shape_of((rows, size, part), f32),
         shape_of((space, rows, group * 8, reduced), bf16),
-        shape_of((devices, 8, 128), f32),
+        shape_of((devices, pay_rows, 128), f32),
         shape_of((size + 16, part), bf16),
         shape_of((size + 16, part), bf16),
     )
@@ -222,7 +228,7 @@
     size = frames * cols
     steps = channels // part
     reduced = w_red.shape[2]
-    shapes, specs = first_outputs(rows, size, devices, space, reduced)
+    shapes, specs = first_outputs(rows, size, devices, space, reduced, 9)
     return pl.pallas_call(
         functools.partial(first_kernel, rows, size, steps),
         grid=(steps,),
@@ -1455,13 +1461,21 @@
     return jnp.concatenate([add(keep, new) for keep, new, _, _ in state], axis=0)
 
 
-def space_sum(value):
+def space_scatter(value):
     count = lax.axis_size("space")
     rows, cols = value.shape
     parts = lax.all_to_all(value.reshape(count, rows // count, cols), "space", 0, 0, tiled=True)
-    own = jnp.sum(parts.astype(f32), axis=0).astype(bf16)
+    return jnp.sum(parts.astype(f32), axis=0).astype(bf16)
+
+
+def space_gather(own):
+    count = lax.axis_size("space")
     spread = jnp.broadcast_to(own[None], (count,) + own.shape)
-    return lax.all_to_all(spread, "space", 0, 0, tiled=True).reshape(rows, cols)
+    return lax.all_to_all(spread, "space", 0, 0, tiled=True).reshape(-1, own.shape[1])
+
+
+def space_sum(value):
+    return space_gather(space_scatter(value))
 
 
 def together(*values):
@@ -1493,8 +1507,6 @@
     own_next = lax.dynamic_slice_in_dim(padded, here * group, group)
     base = lax.axis_index("dp") * frames + here * group
     index = jnp.clip(own_next - base, 0, group - 1)
-    count = exchange(jnp.full((devices, 1, 128), jnp.sum(valid) * cols))
-    inv = 1.0 / jnp.sum(count, axis=0)
 
     def vectors(layer):
         out = []
@@ -1514,6 +1526,8 @@
         gain, bias = gains[layer], biases[layer]
         first, red, pay, low, high = firsts[layer]
         sums_one[layer] = exchange(pay)
+        if layer == 0:
+            inv = 1.0 / jnp.sum(sums_one[0][:, 8:9], axis=0).reshape(1, 128)
         halo = neighbours(low, high)
         reduces[layer] = to_frames(red)
         hidden_own, before = run_conv(
@@ -1531,8 +1545,8 @@
         hidden_twos[layer], pay = run_third(
             second, sums_two[layer], inv, gain[1], bias[1], mask, layer, proj_out
         )
+        pay, gates[layer], low, high = together(pay, gates[layer], low, high)
         sums_three[layer] = exchange(pay)
-        low, high = together(sums_three[layer], low, high)[1:]
         halos[layer] = neighbours(low, high)
         if layer == 0:
             mid, branch_zero, sig_zero, slope_zero, *firsts[1] = run_mid(
@@ -1604,8 +1618,12 @@
             wide_sum = core_sum(buffer)
             first_out, rows_out = run_first_back(*common)
             grad_proj = run_weight(me, False, owners, clip_maps, first_out, rows_out)
+            earlier = space_scatter(jnp.concatenate(results[1], axis=0))
             wide_state = reduce_start(*wide_sum)
-            grad_proj, *arrived = together(grad_proj, *[half[1] for half in wide_state])
+            grad_proj, earlier, *arrived = together(
+                grad_proj, earlier, *[half[1] for half in wide_state]
+            )
+            earlier = space_gather(earlier)
             wide_state = [(half[0], new) + half[2:] for half, new in zip(wide_state, arrived)]
             results[0] = reduce_finish(wide_state), reduce_finish(reduce_start(*core_sum(grad_proj)))
             grad_maps = run_input(0, first_out, rows_out, proj_in, gate_reduce, grad_in, mask, frames)
@@ -1621,10 +1639,13 @@
     counts = wide_rows(owners, channels)
     ends = [sum(counts[: i + 1]) for i in range(4)]
     wide, proj = results[0]
-    wide, *later = together(wide, *lax.psum(results[1], "space"))
-    wide = space_sum(wide)
-    proj = space_sum(proj)
-    halves, places = gather_owners(jnp.concatenate([v[ends[1] :] for v in (wide, later[0])], axis=0))
+    wide, earlier = together(wide, earlier)
+    later = earlier[: wide.shape[0]], earlier[wide.shape[0] :]
+    small = space_sum(wide[ends[1] :])
+    small, wide, proj, grad_maps = together(small, wide, proj, grad_maps)
+    summed = space_sum(jnp.concatenate([wide[: ends[1]], proj], axis=0))
+    wide, proj = summed[: ends[1]], summed[ends[1] :]
+    halves, places = gather_owners(jnp.concatenate([small, later[0][ends[1] :]], axis=0))
     convs, expand = run_small(halves, places, counts, owners, channels)
     large = run_large([wide, later[0]], [proj, later[1]], counts, owners, channels)
     little = [jnp.stack(pair) for pair in zip(*vectors_of)]

time: 646 us -> 617 us (0.955)
  blocking collectives: 53 us -> 18.6 us
    all_to_all x3 -> x1, blocking collectives: 53 us -> 18.6 us  [exchange(): return lax.all_to_all(block, both, 0, 0, tiled=True)]
    psum x1 -> x0, waiting for transfers between devices: 22.2 us -> none  [body(): wide, *later = together(wide, *lax.psum(results[1], 'space'))]
    all_to_all x10 -> x11, waiting for transfers between devices: 22.4 us -> 40.9 us  [exchange(): return lax.all_to_all(block, both, 0, 0, tiled=True)]
    all_to_all x4 -> x6, starting transfers between devices: 15.8 us -> 25.9 us  [the longest x3 13.4 us: space_gather(): lax.all_to_all(spread, 'space', 0, 0, tiled=True).reshape(-1, own.shape[1])]
    all_to_all x4 -> x6, waiting for transfers between devices: 34.2 us -> 44.3 us  [the longest x3 27.3 us: space_scatter(): lax.all_to_all(value.reshape(count, rows // count, cols), 'space', 0, 0,...]
    ppermute x16, waiting for transfers between devices: 38.7 us -> 30.9 us  [swap(): return lax.ppermute(block, 'dp', [(i, i ^ bit) for i in range(count)])]
    all_to_all x10 -> x11, starting transfers between devices: 55.2 us -> 54.9 us  [exchange(): return lax.all_to_all(block, both, 0, 0, tiled=True)]
  transfers between devices with their start and end apart: 53 -> 55, of which waited for: 22 -> 24; matrix products, arithmetic and copies ran while one was open for 5% -> 6% of each run, Pallas kernels for 32% -> 34%
where the time goes in v3:
time: 617 us; the launch traced here: 605 us
  Pallas kernels  220 us (36%)
  starting transfers between devices  157 us (25%)
  waiting for transfers between devices  138 us (22%)
  local copies, waits for them, and re-layouts  29.8 us (5%)
  other arithmetic  26.7 us (4%)
  blocking collectives  18.6 us (3%)
  between operations  15.5 us (3%)
    all_to_all x11, starting transfers between devices, exchange(): return lax.all_to_all(block, both, 0, 0, tiled=True)  54.9 us
    all_to_all x11, waiting for transfers between devices, exchange(): return lax.all_to_all(block, both, 0, 0, tiled=True)  40.9 us
    ppermute x16, waiting for transfers between devices, swap(): return lax.ppermute(block, 'dp', [(i, i ^ bit) for i in range(count)])  30.9 us
    all_to_all x3, waiting for transfers between devices, space_scatter(): lax.all_to_all(value.reshape(count, rows // count, cols), 'space', 0, 0,...  27.3 us
    pallas_call x2, Pallas kernels, run_third_back(): pl.pallas_call(functools.partial(third_back_kernel, rows, size, steps, fi...  24.2 us
    ppermute x6, starting transfers between devices, neighbours(): lax.ppermute(high, 'space', [(i, i + 1) for i in range(count - 1)])  22 us
    all_to_all x4, starting transfers between devices, to_rows(): lax.all_to_all(all_rows.reshape(height // rows, rows, size, channels), 's...  18.6 us
    all_to_all x1, blocking collectives, exchange(): return lax.all_to_all(block, both, 0, 0, tiled=True)  18.6 us
  transfers between devices with their start and end apart: 55, of which 24 were waited for; matrix products, arithmetic and copies ran while one was open for 6% of the time, Pallas kernels for 34%

profile of v3, /device:TPU:0, one launch (start us, length us, event | category | flops | bytes accessed | tf_op | source)
XLA Modules:
  0.0 605.2 jit_solution(296880226415092230)
XLA Ops:
  8.9 9.0 %first.1 = (f32[2,384,512]{2,1,0:T(8,128)}, bf16[4,2,128,128]{3,2,1,0:T(8,128)(2,1)}, f32[32,9,128]{2,1,0:T(8,128)}, bf16[400,512]{1,0:T(8,128)(2,1)}, bf16[400,512]{1,0:T(8,128)(2,1)}) custom-call(bf16[48,2,8,2048]{3,2,1,0:T(8,128)(2,1)} %x.7, bf16[2,2048,512]{2,1,0:T(8,128)(2,1)} %w_in.3, bf16[2,2048,128]{2,1,0:T(8,128)(2,1)} %w_red.5, ...), custom_call_target="tpu_custom_call" | custom-call | flops 503316480 | bytes 2097152 | tf_op jit(solution)/shard_map/first/pallas_call | solution.py:232
  17.9 7.3 %all-to-all-start = ((f32[32,9,128]{2,1,0:T(8,128)}), f32[32,9,128]{2,1,0:T(8,128)S(1)}, u32[]{:S(2)}, u32[]{:S(2)}) async-start(f32[32,9,128]{2,1,0:T(8,128)} %get-tuple-element.154), calls=%async_computation | async-start | bytes 524288 | tf_op jit(solution)/shard_map/all_to_all | solution.py:1360
  39.4 7.8 %conv.2 = (bf16[2,384,512]{2,1,0:T(8,128)(2,1)}, f32[2,384,512]{2,1,0:T(8,128)}) custom-call(f32[2,384,512]{2,1,0:T(8,128)} %get-tuple-element.153.first, f32[32,9,128]{2,1,0:T(8,128)} %copy-done.1, f32[1,128]{1,0:T(1,128)} %divide_bitcast_fusion.inv, f32[1,512]{1,0:T(1,128)} %get-tuple-element.328.gain.gain_one, f32[1,512]{1,0:T(1,128)} %get-tuple-element.311.bias.bias_one, ...), custom_call_target="tpu_custom_call" | custom-call | flops 603979776 | bytes 2097152 | tf_op jit(solution)/shard_map/conv/pallas_call | solution.py:306
  88.1 8.5 %all-to-all-done.4.sums = f32[32,32,128]{2,1,0:T(8,128)S(1)} async-done(((f32[32,32,128]{2,1,0:T(8,128)}), f32[32,32,128]{2,1,0:T(8,128)S(1)}, u32[]{:S(2)}, u32[]{:S(2)}) %all-to-all-start.4) | async-done | bytes 524320 | tf_op jit(solution)/shard_map/all_to_all | solution.py:1360
  97.4 15.1 %mid.1 = (bf16[2,384,2048]{2,1,0:T(8,128)(2,1)}, bf16[2,384,2048]{2,1,0:T(8,128)(2,1)}, bf16[2,384,2048]{2,1,0:T(8,128)(2,1)}, bf16[2,384,2048]{2,1,0:T(8,128)(2...) custom-call(bf16[2,384,512]{2,1,0:T(8,128)(2,1)} %get-tuple-element., ...), custom_call_target="tpu_custom_call" | custom-call | flops 1006632960 | bytes 5242880 | tf_op jit(solution)/shard_map/mid/pallas_call | solution.py:500
  128.5 7.8 %conv.3 = (bf16[2,384,512]{2,1,0:T(8,128)(2,1)}, f32[2,384,512]{2,1,0:T(8,128)}) custom-call(f32[2,384,512]{2,1,0:T(8,128)} %get-tuple-element.170.first, f32[32,8,128]{2,1,0:T(8,128)} %copy-done.9, f32[1,128]{1,0:T(1,128)} %divide_bitcast_fusion.inv, f32[1,512]{1,0:T(1,128)} %get-tuple-element.330.gain.gain_one, f32[1,512]{1,0:T(1,128)} %get-tuple-element.309.bias.bias_one, ...), custom_call_target="tpu_custom_call" | custom-call | flops 603979776 | bytes 2097152 | tf_op jit(solution)/shard_map/conv/pallas_call | solution.py:306
  177.3 8.9 %all-to-all-done.9.sums = f32[32,32,128]{2,1,0:T(8,128)S(1)} async-done(((f32[32,32,128]{2,1,0:T(8,128)}), f32[32,32,128]{2,1,0:T(8,128)S(1)}, u32[]{:S(2)}, u32[]{:S(2)}) %all-to-all-start.9) | async-done | bytes 524320 | tf_op jit(solution)/shard_map/all_to_all | solution.py:1360
  187.0 15.8 %last.1 = (bf16[48,2,8,2048]{3,2,1,0:T(8,128)(2,1)}, bf16[2,384,2048]{2,1,0:T(8,128)(2,1)}, bf16[2,384,2048]{2,1,0:T(8,128)(2,1)}, bf16[2,384,2048]{2,1,0:T(8,12...) custom-call(bf16[2,384,512]{2,1,0:T(8,128)(2,1)} %get-tuple-element.183.hidden, ...), custom_call_target="tpu_custom_call" | custom-call | flops 805306368 | bytes 5242880 | tf_op jit(solution)/shard_map/last/pallas_call | solution.py:629
  202.9 18.6 %all_to_all.130.back_sums = f32[32,32,128]{2,1,0:T(8,128)} all-to-all(f32[32,32,128]{2,1,0:T(8,128)} %get-tuple-element.198), channel_id=1, replica_groups=mesh['dp'=8,'space'=4] {'dp','space'}, dimensions={0} | all-to-all | bytes 1048576 | tf_op jit(solution)/shard_map/all_to_all | solution.py:1360
  225.5 12.1 %third_back.2 = (bf16[8,1008,512]{2,1,0:T(8,128)(2,1)}, f32[2,384,512]{2,1,0:T(8,128)}, f32[32,8,128]{2,1,0:T(8,128)}, bf16[400,512]{1,0:T(8,128)(2,1)}, bf16[400,512]{1,0:T(8,128)(2,1)}) custom-call(s32[1]{0:T(128)} %bitcast.8.me, bf16[8,1008,512]{2,1,0:T(8,128)(2,1)} %get-tuple-element.192.buffer, ...), custom_call_target="tpu_custom_call", output_to_operand_aliasing={{0}: (1, {})} | custom-call | flops 805306368 | bytes 3145728 | tf_op jit(solution)/shard_map/third_back/pallas_call | solution.py:724
  259.1 8.2 %conv_back.2 = (bf16[2,384,512]{2,1,0:T(8,128)(2,1)}, f32[2,384,512]{2,1,0:T(8,128)}) custom-call(f32[2,384,512]{2,1,0:T(8,128)} %get-tuple-element.199.part_two, f32[2,384,512]{2,1,0:T(8,128)} %get-tuple-element.178.second, f32[32,8,128]{2,1,0:T(8,128)} %copy-done.15, f32[32,8,128]{2,1,0:T(8,128)} %copy-done.11, f32[1,512]{1,0:T(1,128)} %get-tuple-element.331.gain.gain_two, ...), custom_call_target="tpu_custom_call" | custom-call | flops 603979776 | bytes 2097152 | tf_op jit(solution)/shard_map/conv_back/pallas_call | solution.py:786
  281.4 8.1 %conv_weight.2 = bf16[8,1008,512]{2,1,0:T(8,128)(2,1)} custom-call(s32[1]{0:T(128)} %bitcast.8.me, bf16[2,384,512]{2,1,0:T(8,128)(2,1)} %get-tuple-element.217.hidden, bf16[2,384,512]{2,1,0:T(8,128)(2,1)} %get-tuple-element.218.hidden_edge, bf16[2,384,512]{2,1,0:T(8,128)(2,1)} %get-tuple-element.219.grad_second, ...), custom_call_target="tpu_custom_call", output_to_operand_aliasing={{}: (4, {})} | custom-call | flops 905969664 | bytes 2097152 | tf_op jit(solution)/shard_map/conv_weight/pallas_call | solution.py:904
  290.4 16.7 %between.1 = (bf16[2,384,512]{2,1,0:T(8,128)(2,1)}, bf16[2,384,128]{2,1,0:T(8,128)(2,1)}, bf16[2,384,2048]{2,1,0:T(8,128)(2,1)}, bf16[2,384,2048]{2,1,0:T(8,128)...) custom-call(f32[2,384,512]{2,1,0:T(8,128)} %get-tuple-element.212.part_one, ...), custom_call_target="tpu_custom_call" | custom-call | flops 805306368 | bytes 5242880 | tf_op jit(solution)/shard_map/between/pallas_call | solution.py:994
  312.8 7.4 %weight.2 = bf16[8,320,512]{2,1,0:T(8,128)(2,1)} custom-call(s32[1]{0:T(128)} %bitcast.8.me, bf16[2,384,2048]{2,1,0:T(8,128)(2,1)} %get-tuple-element.189.x, bf16[2,384,512]{2,1,0:T(8,128)(2,1)} %get-tuple-element.230.first_out, bf16[2,384,128]{2,1,0:T(8,128)(2,1)} %get-tuple-element.231.rows_out), custom_call_target="tpu_custom_call" | custom-call | flops 503316480 | bytes 2097152 | tf_op jit(solution)/shard_map/weight/pallas_call | solution.py:1110
  331.3 12.1 %third_back.3 = (bf16[8,1008,512]{2,1,0:T(8,128)(2,1)}, f32[2,384,512]{2,1,0:T(8,128)}, f32[32,8,128]{2,1,0:T(8,128)}, bf16[400,512]{1,0:T(8,128)(2,1)}, bf16[400,512]{1,0:T(8,128)(2,1)}) custom-call(s32[1]{0:T(128)} %bitcast.8.me, bf16[8,1008,512]{2,1,0:T(8,128)(2,1)} %get-tuple-element.227.buffer, ...), custom_call_target="tpu_custom_call", output_to_operand_aliasing={{0}: (1, {})} | custom-call | flops 805306368 | bytes 3145728 | tf_op jit(solution)/shard_map/third_back/pallas_call | solution.py:724
  365.2 8.2 %conv_back.3 = (bf16[2,384,512]{2,1,0:T(8,128)(2,1)}, f32[2,384,512]{2,1,0:T(8,128)}) custom-call(f32[2,384,512]{2,1,0:T(8,128)} %get-tuple-element.233.part_two, f32[2,384,512]{2,1,0:T(8,128)} %get-tuple-element.158.second, f32[32,8,128]{2,1,0:T(8,128)} %copy-done.17, f32[32,8,128]{2,1,0:T(8,128)} %copy-done.10, f32[1,512]{1,0:T(1,128)} %get-tuple-element.329.gain.gain_two, ...), custom_call_target="tpu_custom_call" | custom-call | flops 603979776 | bytes 2097152 | tf_op jit(solution)/shard_map/conv_back/pallas_call | solution.py:786
  374.9 7.4 %conv_back_edge.3 = (f32[2,384,512]{2,1,0:T(8,128)}, f32[32,8,128]{2,1,0:T(8,128)}) custom-call(f32[2,384,512]{2,1,0:T(8,128)} %get-tuple-element.243.before, bf16[400,512]{1,0:T(8,128)(2,1)} %copy-done.37, bf16[400,512]{1,0:T(8,128)(2,1)} %copy-done.38, bf16[400,512]{1,0:T(8,128)(2,1)} %copy-done.33, bf16[400,512]{1,0:T(8,128)(2,1)} %copy-done.34, ...), custom_call_target="tpu_custom_call" | custom-call | flops 301989888 | bytes 2097152 | tf_op jit(solution)/shard_map/conv_back_edge/pallas_call | solution.py:857
  388.7 8.1 %conv_weight.3 = bf16[8,1008,512]{2,1,0:T(8,128)(2,1)} custom-call(s32[1]{0:T(128)} %bitcast.8.me, bf16[2,384,512]{2,1,0:T(8,128)(2,1)} %get-tuple-element.252.hidden, bf16[2,384,512]{2,1,0:T(8,128)(2,1)} %get-tuple-element.253.hidden_edge, bf16[2,384,512]{2,1,0:T(8,128)(2,1)} %get-tuple-element.254.grad_second, ...), custom_call_target="tpu_custom_call", output_to_operand_aliasing={{}: (4, {})} | custom-call | flops 905969664 | bytes 2097152 | tf_op jit(solution)/shard_map/conv_weight/pallas_call | solution.py:904
  396.8 16.8 %reduce-scatter.5.cloned.1.call-done = bf16[1,320,512]{2,1,0:T(8,128)(2,1)} async-done(((bf16[8,320,512]{2,1,0:T(8,128)(2,1)}), bf16[1,320,512]{2,1,0:T(8,128)(2,1)}) %reduce-scatter.5.cloned.1.call-update) | async-done | bytes 327696 | tf_op jit(solution)/shard_map/reduce_scatter | solution.py:1568
  439.1 7.2 %weight.3 = bf16[8,320,512]{2,1,0:T(8,128)(2,1)} custom-call(s32[1]{0:T(128)} %bitcast.8.me, bf16[48,2,8,2048]{3,2,1,0:T(8,128)(2,1)} %x.7, bf16[2,384,512]{2,1,0:T(8,128)(2,1)} %get-tuple-element.261.first_out, bf16[2,384,128]{2,1,0:T(8,128)(2,1)} %get-tuple-element.262.rows_out), custom_call_target="tpu_custom_call" | custom-call | flops 503316480 | bytes 2097152 | tf_op jit(solution)/shard_map/weight/pallas_call | solution.py:1110
  446.2 11.3 %all-to-all-done.20 = bf16[4,332,512]{2,1,0:T(8,128)(2,1)S(1)} async-done(((bf16[4,332,512]{2,1,0:T(8,128)(2,1)}), bf16[4,332,512]{2,1,0:T(8,128)(2,1)S(1)}, u32[]{:S(2)}, u32[]{:S(2)}) %all-to-all-start.20) | async-done | bytes 1359904 | tf_op jit(solution)/shard_map/all_to_all | solution.py:1467
  476.9 9.1 %collective-permute-done.15 = bf16[504,512]{1,0:T(8,128)(2,1)S(1)} collective-permute-done((bf16[504,512]{1,0:T(8,128)(2,1)S(1)}, bf16[504,512]{1,0:T(8,128)(2,1)S(1)}, u32[]{:S(2)}, u32[]{:S(2)}) %collective-permute-start.15) | collective-permute-done | bytes 516128 | tf_op jit(solution)/shard_map/ppermute | solution.py:1386
  542.3 16.0 %all-to-all-done.24 = bf16[4,288,512]{2,1,0:T(8,128)(2,1)} async-done(((bf16[4,288,512]{2,1,0:T(8,128)(2,1)}), bf16[4,288,512]{2,1,0:T(8,128)(2,1)}, u32[]{:S(2)}, u32[]{:S(2)}) %all-to-all-start.24) | async-done | bytes 1179680 | tf_op jit(solution)/shard_map/all_to_all | solution.py:1467
  584.9 7.7 %all-to-all-done.25 = bf16[4,288,512]{2,1,0:T(8,128)(2,1)S(1)} async-done(((bf16[4,288,512]{2,1,0:T(8,128)(2,1)}), bf16[4,288,512]{2,1,0:T(8,128)(2,1)S(1)}, u32[]{:S(2)}, u32[]{:S(2)}) %all-to-all-start.25) | async-done | bytes 1179680 | tf_op jit(solution)/shard_map/all_to_all | solution.py:1474
  (306 shorter events, 334.4 us)
Async XLA Ops:
  25.2 22.0 %collective-permute-start = (bf16[400,512]{1,0:T(8,128)(2,1)}, bf16[400,512]{1,0:T(8,128)(2,1)S(1)}, u32[]{:S(2)}, u32[]{:S(2)}) collective-permute-start(bf16[400,512]{1,0:T(8,128)(2,1)} %get-tuple-element.156), channel_id=1, source_target_pairs={{0,1},{1,2},{2,3},{4,5},{5,6},{6,7},{8,9},{9,10},{10,11},{12,13},{... | collective-permute-start | bytes 1228808 | tf_op jit(solution)/shard_map/ppermute | solution.py:1375
  35.4 19.3 %all-to-all-start.2 = ((bf16[4,2,128,128]{3,2,1,0:T(8,128)(2,1)}), bf16[4,2,128,128]{3,2,1,0:T(8,128)(2,1)S(1)}, u32[]{:S(2)}, u32[]{:S(2)}) async-start(bf16[4,2,128,128]{3,2,1,0:T(8,128)(2,1)} %get-tuple-element.160), calls=%async_computation.2 | async-start | bytes 524288 | tf_op jit(solution)/shard_map/all_to_all | solution.py:1365
  82.3 30.3 %collective-permute-start.2 = (bf16[400,512]{1,0:T(8,128)(2,1)S(1)}, bf16[400,512]{1,0:T(8,128)(2,1)S(1)}, u32[]{:S(2)}, u32[]{:S(2)}) collective-permute-start(bf16[400,512]{1,0:T(8,128)(2,1)S(1)} %copy-done.53), channel_id=1, source_target_pairs={{0,1},{1,2},{2,3},{4,5},{5,6},{6,7},{8,9},{9,10},{10,11},{12,13},{... | collective-permute-start | bytes 1228808 | tf_op jit(solution)/shard_map/ppermute | solution.py:1375
  85.9 26.7 %collective-permute-start.3 = (bf16[400,512]{1,0:T(8,128)(2,1)S(1)}, bf16[400,512]{1,0:T(8,128)(2,1)S(1)}, u32[]{:S(2)}, u32[]{:S(2)}) collective-permute-start(bf16[400,512]{1,0:T(8,128)(2,1)S(1)} %copy-done.52), channel_id=1, source_target_pairs={{1,0},{2,1},{3,2},{5,4},{6,5},{7,6},{9,8},{10,9},{11,10},{13,12},{... | collective-permute-start | bytes 1228808 | tf_op jit(solution)/shard_map/ppermute | solution.py:1376
  116.7 19.6 %collective-permute-start.4 = (bf16[400,512]{1,0:T(8,128)(2,1)}, bf16[400,512]{1,0:T(8,128)(2,1)S(1)}, u32[]{:S(2)}, u32[]{:S(2)}) collective-permute-start(bf16[400,512]{1,0:T(8,128)(2,1)} %get-tuple-element.176), channel_id=1, source_target_pairs={{0,1},{1,2},{2,3},{4,5},{5,6},{6,7},{8,9},{9,10},{10,11},{12,13},{... | collective-permute-start | bytes 1228808 | tf_op jit(solution)/shard_map/ppermute | solution.py:1375
  171.8 31.0 %collective-permute-start.6 = (bf16[400,512]{1,0:T(8,128)(2,1)S(1)}, bf16[400,512]{1,0:T(8,128)(2,1)S(1)}, u32[]{:S(2)}, u32[]{:S(2)}) collective-permute-start(bf16[400,512]{1,0:T(8,128)(2,1)S(1)} %copy-done.55), channel_id=1, source_target_pairs={{0,1},{1,2},{2,3},{4,5},{5,6},{6,7},{8,9},{9,10},{10,11},{12,13},{... | collective-permute-start | bytes 1228808 | tf_op jit(solution)/shard_map/ppermute | solution.py:1375
  175.4 27.4 %collective-permute-start.7 = (bf16[400,512]{1,0:T(8,128)(2,1)S(1)}, bf16[400,512]{1,0:T(8,128)(2,1)S(1)}, u32[]{:S(2)}, u32[]{:S(2)}) collective-permute-start(bf16[400,512]{1,0:T(8,128)(2,1)S(1)} %copy-done.54), channel_id=1, source_target_pairs={{1,0},{2,1},{3,2},{5,4},{6,5},{7,6},{9,8},{10,9},{11,10},{13,12},{... | collective-permute-start | bytes 1228808 | tf_op jit(solution)/shard_map/ppermute | solution.py:1376
  242.8 24.6 %collective-permute-start.8 = (bf16[400,512]{1,0:T(8,128)(2,1)}, bf16[400,512]{1,0:T(8,128)(2,1)S(1)}, u32[]{:S(2)}, u32[]{:S(2)}) collective-permute-start(bf16[400,512]{1,0:T(8,128)(2,1)} %get-tuple-element.208), channel_id=1, source_target_pairs={{0,1},{1,2},{2,3},{4,5},{5,6},{6,7},{8,9},{9,10},{10,11},{12,13},{... | collective-permute-start | bytes 1228808 | tf_op jit(solution)/shard_map/ppermute | solution.py:1375
  246.5 20.9 %collective-permute-start.9 = (bf16[400,512]{1,0:T(8,128)(2,1)}, bf16[400,512]{1,0:T(8,128)(2,1)S(1)}, u32[]{:S(2)}, u32[]{:S(2)}) collective-permute-start(bf16[400,512]{1,0:T(8,128)(2,1)} %get-tuple-element.209), channel_id=1, source_target_pairs={{1,0},{2,1},{3,2},{5,4},{6,5},{7,6},{9,8},{10,9},{11,10},{13,12},{... | collective-permute-start | bytes 1228808 | tf_op jit(solution)/shard_map/ppermute | solution.py:1376
  253.1 22.2 %all-to-all-start.13 = ((bf16[4,2,128,128]{3,2,1,0:T(8,128)(2,1)}), bf16[4,2,128,128]{3,2,1,0:T(8,128)(2,1)S(1)}, u32[]{:S(2)}, u32[]{:S(2)}) async-start(bf16[4,2,128,128]{3,2,1,0:T(8,128)(2,1)} %bitcast.144), calls=%async_computation.13 | async-start | bytes 524288 | tf_op jit(solution)/shard_map/all_to_all | solution.py:1370
  281.4 92.0 %reduce-scatter.3.cloned.1.call-start = ((), (), s32[]{:S(2)}) async-start(), calls=%async_computation.28 | async-start | bytes 9289728 | tf_op jit(solution)/shard_map/reduce_scatter | solution.py:1568
  307.2 19.9 %all-to-all-start.15 = ((f32[32,32,128]{2,1,0:T(8,128)}), f32[32,32,128]{2,1,0:T(8,128)S(1)}, u32[]{:S(2)}, u32[]{:S(2)}) async-start(f32[32,32,128]{2,1,0:T(8,128)} %get-tuple-element.229), calls=%async_computation.15 | async-start | bytes 1048576 | tf_op jit(solution)/shard_map/all_to_all | solution.py:1360
  312.7 100.9 %reduce-scatter.5.cloned.1.call-start = ((), (), s32[]{:S(2)}) async-start(), calls=%async_computation.29 | async-start | bytes 2949120 | tf_op jit(solution)/shard_map/reduce_scatter | solution.py:1568
  349.0 24.4 %collective-permute-start.10 = (bf16[400,512]{1,0:T(8,128)(2,1)}, bf16[400,512]{1,0:T(8,128)(2,1)S(1)}, u32[]{:S(2)}, u32[]{:S(2)}) collective-permute-start(bf16[400,512]{1,0:T(8,128)(2,1)} %get-tuple-element.244), channel_id=1, source_target_pairs={{0,1},{1,2},{2,3},{4,5},{5,6},{6,7},{8,9},{9,10},{10,11},{12,13},{... | collective-permute-start | bytes 1228808 | tf_op jit(solution)/shard_map/ppermute | solution.py:1375
  352.7 20.7 %collective-permute-start.11 = (bf16[400,512]{1,0:T(8,128)(2,1)}, bf16[400,512]{1,0:T(8,128)(2,1)S(1)}, u32[]{:S(2)}, u32[]{:S(2)}) collective-permute-start(bf16[400,512]{1,0:T(8,128)(2,1)} %get-tuple-element.245), channel_id=1, source_target_pairs={{1,0},{2,1},{3,2},{5,4},{6,5},{7,6},{9,8},{10,9},{11,10},{13,12},{... | collective-permute-start | bytes 1228808 | tf_op jit(solution)/shard_map/ppermute | solution.py:1376
  359.4 22.9 %all-to-all-start.18 = ((bf16[4,2,128,128]{3,2,1,0:T(8,128)(2,1)}), bf16[4,2,128,128]{3,2,1,0:T(8,128)(2,1)S(1)}, u32[]{:S(2)}, u32[]{:S(2)}) async-start(bf16[4,2,128,128]{3,2,1,0:T(8,128)(2,1)} %bitcast.143), calls=%async_computation.19 | async-start | bytes 524288 | tf_op jit(solution)/shard_map/all_to_all | solution.py:1370
  382.3 31.3 %all-to-all-start.19 = ((f32[32,8,128]{2,1,0:T(8,128)}), f32[32,8,128]{2,1,0:T(8,128)S(1)}, u32[]{:S(2)}, u32[]{:S(2)}) async-start(f32[32,8,128]{2,1,0:T(8,128)} %get-tuple-element.251), calls=%async_computation.20 | async-start | bytes 262144 | tf_op jit(solution)/shard_map/all_to_all | solution.py:1360
  419.5 38.0 %all-to-all-start.20 = ((bf16[4,332,512]{2,1,0:T(8,128)(2,1)}), bf16[4,332,512]{2,1,0:T(8,128)(2,1)S(1)}, u32[]{:S(2)}, u32[]{:S(2)}) async-start(bf16[4,332,512]{2,1,0:T(8,128)(2,1)} %reshape.215), calls=%async_computation.22 | async-start | bytes 2752512 | tf_op jit(solution)/shard_map/all_to_all | solution.py:1467
  433.5 25.2 %collective-permute-start.13 = (bf16[2,504,512]{2,1,0:T(8,128)(2,1)}, bf16[2,504,512]{2,1,0:T(8,128)(2,1)}, u32[]{:S(2)}, u32[]{:S(2)}) collective-permute-start(bf16[2,504,512]{2,1,0:T(8,128)(2,1)} %get-tuple-element.265), channel_id=1, source_target_pairs={{0,8},{4,12},{8,0},{12,4},{16,24},{20,28},{24,16},{28,20},{1,9},{5... | collective-permute-start | bytes 3096584 | tf_op jit(solution)/shard_map/ppermute | solution.py:1386
  435.0 24.9 %collective-permute-start.14 = (bf16[2,504,512]{2,1,0:T(8,128)(2,1)}, bf16[2,504,512]{2,1,0:T(8,128)(2,1)S(1)}, u32[]{:S(2)}, u32[]{:S(2)}) collective-permute-start(bf16[2,504,512]{2,1,0:T(8,128)(2,1)} %get-tuple-element.266), channel_id=1, source_target_pairs={{0,16},{4,20},{8,24},{12,28},{16,0},{20,4},{24,8},{28,12},{1,17},{... | collective-permute-start | bytes 3096584 | tf_op jit(solution)/shard_map/ppermute | solution.py:1386
  463.8 38.2 %all-to-all-start.21 = ((bf16[4,332,512]{2,1,0:T(8,128)(2,1)}), bf16[4,332,512]{2,1,0:T(8,128)(2,1)S(1)}, u32[]{:S(2)}, u32[]{:S(2)}) async-start(bf16[4,332,512]{2,1,0:T(8,128)(2,1)} %broadcast_in_dim.16), calls=%async_computation.23 | async-start | bytes 2752512 | tf_op jit(solution)/shard_map/all_to_all | solution.py:1474
  527.3 31.0 %all-to-all-start.24 = ((bf16[4,288,512]{2,1,0:T(8,128)(2,1)}), bf16[4,288,512]{2,1,0:T(8,128)(2,1)}, u32[]{:S(2)}, u32[]{:S(2)}) async-start(bf16[4,288,512]{2,1,0:T(8,128)(2,1)} %bitcast.128), calls=%async_computation.26 | async-start | bytes 2359296 | tf_op jit(solution)/shard_map/all_to_all | solution.py:1467
  541.6 24.4 %collective-permute-start.25 = (bf16[2,176,512]{2,1,0:T(8,128)(2,1)S(1)}, bf16[2,176,512]{2,1,0:T(8,128)(2,1)}, u32[]{:S(2)}, u32[]{:S(2)}) collective-permute-start(bf16[2,176,512]{2,1,0:T(8,128)(2,1)S(1)} %pad_maximum_fusion.8), channel_id=1, source_target_pairs={{0,8},{4,12},{8,0},{12,4},{16,24},{20,28},{24,16},{28,20},{1,9},{5... | collective-permute-start | bytes 1081352 | tf_op jit(solution)/shard_map/ppermute | solution.py:1386
  561.0 31.5 %all-to-all-start.25 = ((bf16[4,288,512]{2,1,0:T(8,128)(2,1)}), bf16[4,288,512]{2,1,0:T(8,128)(2,1)S(1)}, u32[]{:S(2)}, u32[]{:S(2)}) async-start(bf16[4,288,512]{2,1,0:T(8,128)(2,1)} %broadcast_in_dim.18), calls=%async_computation.27 | async-start | bytes 2359296 | tf_op jit(solution)/shard_map/all_to_all | solution.py:1474
  (89 other events, 904.8 us)
Sparse Core Ops, SparseCore 0:
  289.9 76.1 reduce-scatter.2
  369.8 43.8 reduce-scatter.4

commit v4 on v3

--- a/solution.py
+++ b/solution.py
@@ -462,8 +462,10 @@
             z = x[pl.ds(i * frames, frames), r].astype(f32).reshape(chunk, part) + b * sig
             zs = sigmoid(z)
             m = mask[r, at(i), :]
-            out[r, at(i), :] = (z * zs * m).astype(bf16)
-            slope[r, at(i), :] = (zs * (1.0 + z * (1.0 - zs)) * m).astype(bf16)
+            zm = zs * m
+            y = z * zm
+            out[r, at(i), :] = y.astype(bf16)
+            slope[r, at(i), :] = (zm + y * (1.0 - zs)).astype(bf16)
             branch[r, at(i), :] = b.astype(bf16)
             sig_out[r, at(i), :] = sig.astype(bf16)
         return 0
@@ -592,9 +594,11 @@
             z = x[r, at(i), :].astype(f32) + b * sig
             zs = sigmoid(z)
             m = mask[r, at(i), :]
-            out[pl.ds(i * frames, frames), r] = (z * zs * m).reshape(frames, 8, part).astype(bf16)
+            zm = zs * m
+            y = z * zm
+            out[pl.ds(i * frames, frames), r] = y.reshape(frames, 8, part).astype(bf16)
             dz = grad_out[pl.ds(i * frames, frames), r].astype(f32).reshape(chunk, part)
-            dz = dz * m * (zs * (1.0 + z * (1.0 - zs)))
+            dz = dz * (zm + y * (1.0 - zs))
             db = dz * sig
             s = s + fold(db)
             q = q + fold(db * n)

time: 617 us -> 616 us (level)
  no operation moved by 1% of the time
where the time goes in v4:
time: 616 us; the launch traced here: 604 us
  Pallas kernels  219 us (36%)
  starting transfers between devices  157 us (25%)
  waiting for transfers between devices  138 us (22%)
  local copies, waits for them, and re-layouts  29.8 us (5%)
  other arithmetic  26.7 us (4%)
  blocking collectives  18.6 us (3%)
  between operations  15.5 us (3%)
    all_to_all x11, starting transfers between devices, exchange(): return lax.all_to_all(block, both, 0, 0, tiled=True)  54.9 us
    all_to_all x11, waiting for transfers between devices, exchange(): return lax.all_to_all(block, both, 0, 0, tiled=True)  40.9 us
    ppermute x16, waiting for transfers between devices, swap(): return lax.ppermute(block, 'dp', [(i, i ^ bit) for i in range(count)])  30.9 us
    all_to_all x3, waiting for transfers between devices, space_scatter(): lax.all_to_all(value.reshape(count, rows // count, cols), 'space', 0, 0,...  27.3 us
    pallas_call x2, Pallas kernels, run_third_back(): pl.pallas_call(functools.partial(third_back_kernel, rows, size, steps, fi...  24.2 us
    ppermute x6, starting transfers between devices, neighbours(): lax.ppermute(high, 'space', [(i, i + 1) for i in range(count - 1)])  22 us
    all_to_all x4, starting transfers between devices, to_rows(): lax.all_to_all(all_rows.reshape(height // rows, rows, size, channels), 's...  18.6 us
    all_to_all x1, blocking collectives, exchange(): return lax.all_to_all(block, both, 0, 0, tiled=True)  18.6 us
  transfers between devices with their start and end apart: 55, of which 24 were waited for; matrix products, arithmetic and copies ran while one was open for 6% of the time, Pallas kernels for 34%

profile of v4, /device:TPU:0, one launch (start us, length us, event | category | flops | bytes accessed | tf_op | source)
XLA Modules:
  0.0 604.4 jit_solution(5330321192351027494)
XLA Ops:
  8.9 9.0 %first.1 = (f32[2,384,512]{2,1,0:T(8,128)}, bf16[4,2,128,128]{3,2,1,0:T(8,128)(2,1)}, f32[32,9,128]{2,1,0:T(8,128)}, bf16[400,512]{1,0:T(8,128)(2,1)}, bf16[400,512]{1,0:T(8,128)(2,1)}) custom-call(bf16[48,2,8,2048]{3,2,1,0:T(8,128)(2,1)} %x.7, bf16[2,2048,512]{2,1,0:T(8,128)(2,1)} %w_in.3, bf16[2,2048,128]{2,1,0:T(8,128)(2,1)} %w_red.5, ...), custom_call_target="tpu_custom_call" | custom-call | flops 503316480 | bytes 2097152 | tf_op jit(solution)/shard_map/first/pallas_call | solution.py:232
  17.9 7.3 %all-to-all-start = ((f32[32,9,128]{2,1,0:T(8,128)}), f32[32,9,128]{2,1,0:T(8,128)S(1)}, u32[]{:S(2)}, u32[]{:S(2)}) async-start(f32[32,9,128]{2,1,0:T(8,128)} %get-tuple-element.154), calls=%async_computation | async-start | bytes 524288 | tf_op jit(solution)/shard_map/all_to_all | solution.py:1364
  39.4 7.8 %conv.2 = (bf16[2,384,512]{2,1,0:T(8,128)(2,1)}, f32[2,384,512]{2,1,0:T(8,128)}) custom-call(f32[2,384,512]{2,1,0:T(8,128)} %get-tuple-element.153.first, f32[32,9,128]{2,1,0:T(8,128)} %copy-done.1, f32[1,128]{1,0:T(1,128)} %divide_bitcast_fusion.inv, f32[1,512]{1,0:T(1,128)} %get-tuple-element.328.gain.gain_one, f32[1,512]{1,0:T(1,128)} %get-tuple-element.311.bias.bias_one, ...), custom_call_target="tpu_custom_call" | custom-call | flops 603979776 | bytes 2097152 | tf_op jit(solution)/shard_map/conv/pallas_call | solution.py:306
  88.1 8.5 %all-to-all-done.4.sums = f32[32,32,128]{2,1,0:T(8,128)S(1)} async-done(((f32[32,32,128]{2,1,0:T(8,128)}), f32[32,32,128]{2,1,0:T(8,128)S(1)}, u32[]{:S(2)}, u32[]{:S(2)}) %all-to-all-start.4) | async-done | bytes 524320 | tf_op jit(solution)/shard_map/all_to_all | solution.py:1364
  97.4 14.8 %mid.1 = (bf16[2,384,2048]{2,1,0:T(8,128)(2,1)}, bf16[2,384,2048]{2,1,0:T(8,128)(2,1)}, bf16[2,384,2048]{2,1,0:T(8,128)(2,1)}, bf16[2,384,2048]{2,1,0:T(8,128)(2...) custom-call(bf16[2,384,512]{2,1,0:T(8,128)(2,1)} %get-tuple-element., ...), custom_call_target="tpu_custom_call" | custom-call | flops 1006632960 | bytes 5242880 | tf_op jit(solution)/shard_map/mid/pallas_call | solution.py:502
  128.2 7.8 %conv.3 = (bf16[2,384,512]{2,1,0:T(8,128)(2,1)}, f32[2,384,512]{2,1,0:T(8,128)}) custom-call(f32[2,384,512]{2,1,0:T(8,128)} %get-tuple-element.170.first, f32[32,8,128]{2,1,0:T(8,128)} %copy-done.9, f32[1,128]{1,0:T(1,128)} %divide_bitcast_fusion.inv, f32[1,512]{1,0:T(1,128)} %get-tuple-element.330.gain.gain_one, f32[1,512]{1,0:T(1,128)} %get-tuple-element.309.bias.bias_one, ...), custom_call_target="tpu_custom_call" | custom-call | flops 603979776 | bytes 2097152 | tf_op jit(solution)/shard_map/conv/pallas_call | solution.py:306
  177.0 8.9 %all-to-all-done.9.sums = f32[32,32,128]{2,1,0:T(8,128)S(1)} async-done(((f32[32,32,128]{2,1,0:T(8,128)}), f32[32,32,128]{2,1,0:T(8,128)S(1)}, u32[]{:S(2)}, u32[]{:S(2)}) %all-to-all-start.9) | async-done | bytes 524320 | tf_op jit(solution)/shard_map/all_to_all | solution.py:1364
  186.7 15.4 %last.1 = (bf16[48,2,8,2048]{3,2,1,0:T(8,128)(2,1)}, bf16[2,384,2048]{2,1,0:T(8,128)(2,1)}, bf16[2,384,2048]{2,1,0:T(8,128)(2,1)}, bf16[2,384,2048]{2,1,0:T(8,12...) custom-call(bf16[2,384,512]{2,1,0:T(8,128)(2,1)} %get-tuple-element.183.hidden, ...), custom_call_target="tpu_custom_call" | custom-call | flops 805306368 | bytes 5242880 | tf_op jit(solution)/shard_map/last/pallas_call | solution.py:633
  202.1 18.6 %all_to_all.130.back_sums = f32[32,32,128]{2,1,0:T(8,128)} all-to-all(f32[32,32,128]{2,1,0:T(8,128)} %get-tuple-element.198), channel_id=1, replica_groups=mesh['dp'=8,'space'=4] {'dp','space'}, dimensions={0} | all-to-all | bytes 1048576 | tf_op jit(solution)/shard_map/all_to_all | solution.py:1364
  224.8 12.1 %third_back.2 = (bf16[8,1008,512]{2,1,0:T(8,128)(2,1)}, f32[2,384,512]{2,1,0:T(8,128)}, f32[32,8,128]{2,1,0:T(8,128)}, bf16[400,512]{1,0:T(8,128)(2,1)}, bf16[400,512]{1,0:T(8,128)(2,1)}) custom-call(s32[1]{0:T(128)} %bitcast.8.me, bf16[8,1008,512]{2,1,0:T(8,128)(2,1)} %get-tuple-element.192.buffer, ...), custom_call_target="tpu_custom_call", output_to_operand_aliasing={{0}: (1, {})} | custom-call | flops 805306368 | bytes 3145728 | tf_op jit(solution)/shard_map/third_back/pallas_call | solution.py:728
  258.4 8.2 %conv_back.2 = (bf16[2,384,512]{2,1,0:T(8,128)(2,1)}, f32[2,384,512]{2,1,0:T(8,128)}) custom-call(f32[2,384,512]{2,1,0:T(8,128)} %get-tuple-element.199.part_two, f32[2,384,512]{2,1,0:T(8,128)} %get-tuple-element.178.second, f32[32,8,128]{2,1,0:T(8,128)} %copy-done.15, f32[32,8,128]{2,1,0:T(8,128)} %copy-done.11, f32[1,512]{1,0:T(1,128)} %get-tuple-element.331.gain.gain_two, ...), custom_call_target="tpu_custom_call" | custom-call | flops 603979776 | bytes 2097152 | tf_op jit(solution)/shard_map/conv_back/pallas_call | solution.py:790
  280.7 8.1 %conv_weight.2 = bf16[8,1008,512]{2,1,0:T(8,128)(2,1)} custom-call(s32[1]{0:T(128)} %bitcast.8.me, bf16[2,384,512]{2,1,0:T(8,128)(2,1)} %get-tuple-element.217.hidden, bf16[2,384,512]{2,1,0:T(8,128)(2,1)} %get-tuple-element.218.hidden_edge, bf16[2,384,512]{2,1,0:T(8,128)(2,1)} %get-tuple-element.219.grad_second, ...), custom_call_target="tpu_custom_call", output_to_operand_aliasing={{}: (4, {})} | custom-call | flops 905969664 | bytes 2097152 | tf_op jit(solution)/shard_map/conv_weight/pallas_call | solution.py:908
  289.7 16.7 %between.1 = (bf16[2,384,512]{2,1,0:T(8,128)(2,1)}, bf16[2,384,128]{2,1,0:T(8,128)(2,1)}, bf16[2,384,2048]{2,1,0:T(8,128)(2,1)}, bf16[2,384,2048]{2,1,0:T(8,128)...) custom-call(f32[2,384,512]{2,1,0:T(8,128)} %get-tuple-element.212.part_one, ...), custom_call_target="tpu_custom_call" | custom-call | flops 805306368 | bytes 5242880 | tf_op jit(solution)/shard_map/between/pallas_call | solution.py:998
  312.0 7.4 %weight.2 = bf16[8,320,512]{2,1,0:T(8,128)(2,1)} custom-call(s32[1]{0:T(128)} %bitcast.8.me, bf16[2,384,2048]{2,1,0:T(8,128)(2,1)} %get-tuple-element.189.x, bf16[2,384,512]{2,1,0:T(8,128)(2,1)} %get-tuple-element.230.first_out, bf16[2,384,128]{2,1,0:T(8,128)(2,1)} %get-tuple-element.231.rows_out), custom_call_target="tpu_custom_call" | custom-call | flops 503316480 | bytes 2097152 | tf_op jit(solution)/shard_map/weight/pallas_call | solution.py:1114
  330.6 12.1 %third_back.3 = (bf16[8,1008,512]{2,1,0:T(8,128)(2,1)}, f32[2,384,512]{2,1,0:T(8,128)}, f32[32,8,128]{2,1,0:T(8,128)}, bf16[400,512]{1,0:T(8,128)(2,1)}, bf16[400,512]{1,0:T(8,128)(2,1)}) custom-call(s32[1]{0:T(128)} %bitcast.8.me, bf16[8,1008,512]{2,1,0:T(8,128)(2,1)} %get-tuple-element.227.buffer, ...), custom_call_target="tpu_custom_call", output_to_operand_aliasing={{0}: (1, {})} | custom-call | flops 805306368 | bytes 3145728 | tf_op jit(solution)/shard_map/third_back/pallas_call | solution.py:728
  364.4 8.2 %conv_back.3 = (bf16[2,384,512]{2,1,0:T(8,128)(2,1)}, f32[2,384,512]{2,1,0:T(8,128)}) custom-call(f32[2,384,512]{2,1,0:T(8,128)} %get-tuple-element.233.part_two, f32[2,384,512]{2,1,0:T(8,128)} %get-tuple-element.158.second, f32[32,8,128]{2,1,0:T(8,128)} %copy-done.17, f32[32,8,128]{2,1,0:T(8,128)} %copy-done.10, f32[1,512]{1,0:T(1,128)} %get-tuple-element.329.gain.gain_two, ...), custom_call_target="tpu_custom_call" | custom-call | flops 603979776 | bytes 2097152 | tf_op jit(solution)/shard_map/conv_back/pallas_call | solution.py:790
  374.1 7.4 %conv_back_edge.3 = (f32[2,384,512]{2,1,0:T(8,128)}, f32[32,8,128]{2,1,0:T(8,128)}) custom-call(f32[2,384,512]{2,1,0:T(8,128)} %get-tuple-element.243.before, bf16[400,512]{1,0:T(8,128)(2,1)} %copy-done.37, bf16[400,512]{1,0:T(8,128)(2,1)} %copy-done.38, bf16[400,512]{1,0:T(8,128)(2,1)} %copy-done.33, bf16[400,512]{1,0:T(8,128)(2,1)} %copy-done.34, ...), custom_call_target="tpu_custom_call" | custom-call | flops 301989888 | bytes 2097152 | tf_op jit(solution)/shard_map/conv_back_edge/pallas_call | solution.py:861
  387.9 8.1 %conv_weight.3 = bf16[8,1008,512]{2,1,0:T(8,128)(2,1)} custom-call(s32[1]{0:T(128)} %bitcast.8.me, bf16[2,384,512]{2,1,0:T(8,128)(2,1)} %get-tuple-element.252.hidden, bf16[2,384,512]{2,1,0:T(8,128)(2,1)} %get-tuple-element.253.hidden_edge, bf16[2,384,512]{2,1,0:T(8,128)(2,1)} %get-tuple-element.254.grad_second, ...), custom_call_target="tpu_custom_call", output_to_operand_aliasing={{}: (4, {})} | custom-call | flops 905969664 | bytes 2097152 | tf_op jit(solution)/shard_map/conv_weight/pallas_call | solution.py:908
  396.0 16.8 %reduce-scatter.5.cloned.1.call-done = bf16[1,320,512]{2,1,0:T(8,128)(2,1)} async-done(((bf16[8,320,512]{2,1,0:T(8,128)(2,1)}), bf16[1,320,512]{2,1,0:T(8,128)(2,1)}) %reduce-scatter.5.cloned.1.call-update) | async-done | bytes 327696 | tf_op jit(solution)/shard_map/reduce_scatter | solution.py:1572
  438.3 7.1 %weight.3 = bf16[8,320,512]{2,1,0:T(8,128)(2,1)} custom-call(s32[1]{0:T(128)} %bitcast.8.me, bf16[48,2,8,2048]{3,2,1,0:T(8,128)(2,1)} %x.7, bf16[2,384,512]{2,1,0:T(8,128)(2,1)} %get-tuple-element.261.first_out, bf16[2,384,128]{2,1,0:T(8,128)(2,1)} %get-tuple-element.262.rows_out), custom_call_target="tpu_custom_call" | custom-call | flops 503316480 | bytes 2097152 | tf_op jit(solution)/shard_map/weight/pallas_call | solution.py:1114
  445.4 11.3 %all-to-all-done.20 = bf16[4,332,512]{2,1,0:T(8,128)(2,1)S(1)} async-done(((bf16[4,332,512]{2,1,0:T(8,128)(2,1)}), bf16[4,332,512]{2,1,0:T(8,128)(2,1)S(1)}, u32[]{:S(2)}, u32[]{:S(2)}) %all-to-all-start.20) | async-done | bytes 1359904 | tf_op jit(solution)/shard_map/all_to_all | solution.py:1471
  476.1 9.1 %collective-permute-done.15 = bf16[504,512]{1,0:T(8,128)(2,1)S(1)} collective-permute-done((bf16[504,512]{1,0:T(8,128)(2,1)S(1)}, bf16[504,512]{1,0:T(8,128)(2,1)S(1)}, u32[]{:S(2)}, u32[]{:S(2)}) %collective-permute-start.15) | collective-permute-done | bytes 516128 | tf_op jit(solution)/shard_map/ppermute | solution.py:1390
  541.5 16.0 %all-to-all-done.24 = bf16[4,288,512]{2,1,0:T(8,128)(2,1)} async-done(((bf16[4,288,512]{2,1,0:T(8,128)(2,1)}), bf16[4,288,512]{2,1,0:T(8,128)(2,1)}, u32[]{:S(2)}, u32[]{:S(2)}) %all-to-all-start.24) | async-done | bytes 1179680 | tf_op jit(solution)/shard_map/all_to_all | solution.py:1471
  584.1 7.7 %all-to-all-done.25 = bf16[4,288,512]{2,1,0:T(8,128)(2,1)S(1)} async-done(((bf16[4,288,512]{2,1,0:T(8,128)(2,1)}), bf16[4,288,512]{2,1,0:T(8,128)(2,1)S(1)}, u32[]{:S(2)}, u32[]{:S(2)}) %all-to-all-start.25) | async-done | bytes 1179680 | tf_op jit(solution)/shard_map/all_to_all | solution.py:1478
  (306 shorter events, 334.4 us)
Async XLA Ops:
  25.2 22.0 %collective-permute-start = (bf16[400,512]{1,0:T(8,128)(2,1)}, bf16[400,512]{1,0:T(8,128)(2,1)S(1)}, u32[]{:S(2)}, u32[]{:S(2)}) collective-permute-start(bf16[400,512]{1,0:T(8,128)(2,1)} %get-tuple-element.156), channel_id=1, source_target_pairs={{0,1},{1,2},{2,3},{4,5},{5,6},{6,7},{8,9},{9,10},{10,11},{12,13},{... | collective-permute-start | bytes 1228808 | tf_op jit(solution)/shard_map/ppermute | solution.py:1379
  35.4 19.3 %all-to-all-start.2 = ((bf16[4,2,128,128]{3,2,1,0:T(8,128)(2,1)}), bf16[4,2,128,128]{3,2,1,0:T(8,128)(2,1)S(1)}, u32[]{:S(2)}, u32[]{:S(2)}) async-start(bf16[4,2,128,128]{3,2,1,0:T(8,128)(2,1)} %get-tuple-element.160), calls=%async_computation.2 | async-start | bytes 524288 | tf_op jit(solution)/shard_map/all_to_all | solution.py:1369
  82.3 30.0 %collective-permute-start.2 = (bf16[400,512]{1,0:T(8,128)(2,1)S(1)}, bf16[400,512]{1,0:T(8,128)(2,1)S(1)}, u32[]{:S(2)}, u32[]{:S(2)}) collective-permute-start(bf16[400,512]{1,0:T(8,128)(2,1)S(1)} %copy-done.53), channel_id=1, source_target_pairs={{0,1},{1,2},{2,3},{4,5},{5,6},{6,7},{8,9},{9,10},{10,11},{12,13},{... | collective-permute-start | bytes 1228808 | tf_op jit(solution)/shard_map/ppermute | solution.py:1379
  85.9 26.4 %collective-permute-start.3 = (bf16[400,512]{1,0:T(8,128)(2,1)S(1)}, bf16[400,512]{1,0:T(8,128)(2,1)S(1)}, u32[]{:S(2)}, u32[]{:S(2)}) collective-permute-start(bf16[400,512]{1,0:T(8,128)(2,1)S(1)} %copy-done.52), channel_id=1, source_target_pairs={{1,0},{2,1},{3,2},{5,4},{6,5},{7,6},{9,8},{10,9},{11,10},{13,12},{... | collective-permute-start | bytes 1228808 | tf_op jit(solution)/shard_map/ppermute | solution.py:1380
  116.4 19.6 %collective-permute-start.4 = (bf16[400,512]{1,0:T(8,128)(2,1)}, bf16[400,512]{1,0:T(8,128)(2,1)S(1)}, u32[]{:S(2)}, u32[]{:S(2)}) collective-permute-start(bf16[400,512]{1,0:T(8,128)(2,1)} %get-tuple-element.176), channel_id=1, source_target_pairs={{0,1},{1,2},{2,3},{4,5},{5,6},{6,7},{8,9},{9,10},{10,11},{12,13},{... | collective-permute-start | bytes 1228808 | tf_op jit(solution)/shard_map/ppermute | solution.py:1379
  171.5 30.6 %collective-permute-start.6 = (bf16[400,512]{1,0:T(8,128)(2,1)S(1)}, bf16[400,512]{1,0:T(8,128)(2,1)S(1)}, u32[]{:S(2)}, u32[]{:S(2)}) collective-permute-start(bf16[400,512]{1,0:T(8,128)(2,1)S(1)} %copy-done.55), channel_id=1, source_target_pairs={{0,1},{1,2},{2,3},{4,5},{5,6},{6,7},{8,9},{9,10},{10,11},{12,13},{... | collective-permute-start | bytes 1228808 | tf_op jit(solution)/shard_map/ppermute | solution.py:1379
  175.1 27.0 %collective-permute-start.7 = (bf16[400,512]{1,0:T(8,128)(2,1)S(1)}, bf16[400,512]{1,0:T(8,128)(2,1)S(1)}, u32[]{:S(2)}, u32[]{:S(2)}) collective-permute-start(bf16[400,512]{1,0:T(8,128)(2,1)S(1)} %copy-done.54), channel_id=1, source_target_pairs={{1,0},{2,1},{3,2},{5,4},{6,5},{7,6},{9,8},{10,9},{11,10},{13,12},{... | collective-permute-start | bytes 1228808 | tf_op jit(solution)/shard_map/ppermute | solution.py:1380
  242.1 24.6 %collective-permute-start.8 = (bf16[400,512]{1,0:T(8,128)(2,1)}, bf16[400,512]{1,0:T(8,128)(2,1)S(1)}, u32[]{:S(2)}, u32[]{:S(2)}) collective-permute-start(bf16[400,512]{1,0:T(8,128)(2,1)} %get-tuple-element.208), channel_id=1, source_target_pairs={{0,1},{1,2},{2,3},{4,5},{5,6},{6,7},{8,9},{9,10},{10,11},{12,13},{... | collective-permute-start | bytes 1228808 | tf_op jit(solution)/shard_map/ppermute | solution.py:1379
  245.8 20.9 %collective-permute-start.9 = (bf16[400,512]{1,0:T(8,128)(2,1)}, bf16[400,512]{1,0:T(8,128)(2,1)S(1)}, u32[]{:S(2)}, u32[]{:S(2)}) collective-permute-start(bf16[400,512]{1,0:T(8,128)(2,1)} %get-tuple-element.209), channel_id=1, source_target_pairs={{1,0},{2,1},{3,2},{5,4},{6,5},{7,6},{9,8},{10,9},{11,10},{13,12},{... | collective-permute-start | bytes 1228808 | tf_op jit(solution)/shard_map/ppermute | solution.py:1380
  252.4 22.2 %all-to-all-start.13 = ((bf16[4,2,128,128]{3,2,1,0:T(8,128)(2,1)}), bf16[4,2,128,128]{3,2,1,0:T(8,128)(2,1)S(1)}, u32[]{:S(2)}, u32[]{:S(2)}) async-start(bf16[4,2,128,128]{3,2,1,0:T(8,128)(2,1)} %bitcast.144), calls=%async_computation.13 | async-start | bytes 524288 | tf_op jit(solution)/shard_map/all_to_all | solution.py:1374
  280.6 92.0 %reduce-scatter.3.cloned.1.call-start = ((), (), s32[]{:S(2)}) async-start(), calls=%async_computation.28 | async-start | bytes 9289728 | tf_op jit(solution)/shard_map/reduce_scatter | solution.py:1572
  306.4 19.9 %all-to-all-start.15 = ((f32[32,32,128]{2,1,0:T(8,128)}), f32[32,32,128]{2,1,0:T(8,128)S(1)}, u32[]{:S(2)}, u32[]{:S(2)}) async-start(f32[32,32,128]{2,1,0:T(8,128)} %get-tuple-element.229), calls=%async_computation.15 | async-start | bytes 1048576 | tf_op jit(solution)/shard_map/all_to_all | solution.py:1364
  312.0 100.9 %reduce-scatter.5.cloned.1.call-start = ((), (), s32[]{:S(2)}) async-start(), calls=%async_computation.29 | async-start | bytes 2949120 | tf_op jit(solution)/shard_map/reduce_scatter | solution.py:1572
  348.3 24.3 %collective-permute-start.10 = (bf16[400,512]{1,0:T(8,128)(2,1)}, bf16[400,512]{1,0:T(8,128)(2,1)S(1)}, u32[]{:S(2)}, u32[]{:S(2)}) collective-permute-start(bf16[400,512]{1,0:T(8,128)(2,1)} %get-tuple-element.244), channel_id=1, source_target_pairs={{0,1},{1,2},{2,3},{4,5},{5,6},{6,7},{8,9},{9,10},{10,11},{12,13},{... | collective-permute-start | bytes 1228808 | tf_op jit(solution)/shard_map/ppermute | solution.py:1379
  352.0 20.7 %collective-permute-start.11 = (bf16[400,512]{1,0:T(8,128)(2,1)}, bf16[400,512]{1,0:T(8,128)(2,1)S(1)}, u32[]{:S(2)}, u32[]{:S(2)}) collective-permute-start(bf16[400,512]{1,0:T(8,128)(2,1)} %get-tuple-element.245), channel_id=1, source_target_pairs={{1,0},{2,1},{3,2},{5,4},{6,5},{7,6},{9,8},{10,9},{11,10},{13,12},{... | collective-permute-start | bytes 1228808 | tf_op jit(solution)/shard_map/ppermute | solution.py:1380
  358.6 22.9 %all-to-all-start.18 = ((bf16[4,2,128,128]{3,2,1,0:T(8,128)(2,1)}), bf16[4,2,128,128]{3,2,1,0:T(8,128)(2,1)S(1)}, u32[]{:S(2)}, u32[]{:S(2)}) async-start(bf16[4,2,128,128]{3,2,1,0:T(8,128)(2,1)} %bitcast.143), calls=%async_computation.19 | async-start | bytes 524288 | tf_op jit(solution)/shard_map/all_to_all | solution.py:1374
  381.5 31.3 %all-to-all-start.19 = ((f32[32,8,128]{2,1,0:T(8,128)}), f32[32,8,128]{2,1,0:T(8,128)S(1)}, u32[]{:S(2)}, u32[]{:S(2)}) async-start(f32[32,8,128]{2,1,0:T(8,128)} %get-tuple-element.251), calls=%async_computation.20 | async-start | bytes 262144 | tf_op jit(solution)/shard_map/all_to_all | solution.py:1364
  418.7 38.0 %all-to-all-start.20 = ((bf16[4,332,512]{2,1,0:T(8,128)(2,1)}), bf16[4,332,512]{2,1,0:T(8,128)(2,1)S(1)}, u32[]{:S(2)}, u32[]{:S(2)}) async-start(bf16[4,332,512]{2,1,0:T(8,128)(2,1)} %reshape.215), calls=%async_computation.22 | async-start | bytes 2752512 | tf_op jit(solution)/shard_map/all_to_all | solution.py:1471
  432.7 25.2 %collective-permute-start.13 = (bf16[2,504,512]{2,1,0:T(8,128)(2,1)}, bf16[2,504,512]{2,1,0:T(8,128)(2,1)}, u32[]{:S(2)}, u32[]{:S(2)}) collective-permute-start(bf16[2,504,512]{2,1,0:T(8,128)(2,1)} %get-tuple-element.265), channel_id=1, source_target_pairs={{0,8},{4,12},{8,0},{12,4},{16,24},{20,28},{24,16},{28,20},{1,9},{5... | collective-permute-start | bytes 3096584 | tf_op jit(solution)/shard_map/ppermute | solution.py:1390
  434.2 24.9 %collective-permute-start.14 = (bf16[2,504,512]{2,1,0:T(8,128)(2,1)}, bf16[2,504,512]{2,1,0:T(8,128)(2,1)S(1)}, u32[]{:S(2)}, u32[]{:S(2)}) collective-permute-start(bf16[2,504,512]{2,1,0:T(8,128)(2,1)} %get-tuple-element.266), channel_id=1, source_target_pairs={{0,16},{4,20},{8,24},{12,28},{16,0},{20,4},{24,8},{28,12},{1,17},{... | collective-permute-start | bytes 3096584 | tf_op jit(solution)/shard_map/ppermute | solution.py:1390
  463.0 38.2 %all-to-all-start.21 = ((bf16[4,332,512]{2,1,0:T(8,128)(2,1)}), bf16[4,332,512]{2,1,0:T(8,128)(2,1)S(1)}, u32[]{:S(2)}, u32[]{:S(2)}) async-start(bf16[4,332,512]{2,1,0:T(8,128)(2,1)} %broadcast_in_dim.16), calls=%async_computation.23 | async-start | bytes 2752512 | tf_op jit(solution)/shard_map/all_to_all | solution.py:1478
  526.5 31.0 %all-to-all-start.24 = ((bf16[4,288,512]{2,1,0:T(8,128)(2,1)}), bf16[4,288,512]{2,1,0:T(8,128)(2,1)}, u32[]{:S(2)}, u32[]{:S(2)}) async-start(bf16[4,288,512]{2,1,0:T(8,128)(2,1)} %bitcast.128), calls=%async_computation.26 | async-start | bytes 2359296 | tf_op jit(solution)/shard_map/all_to_all | solution.py:1471
  540.8 24.4 %collective-permute-start.25 = (bf16[2,176,512]{2,1,0:T(8,128)(2,1)S(1)}, bf16[2,176,512]{2,1,0:T(8,128)(2,1)}, u32[]{:S(2)}, u32[]{:S(2)}) collective-permute-start(bf16[2,176,512]{2,1,0:T(8,128)(2,1)S(1)} %pad_maximum_fusion.8), channel_id=1, source_target_pairs={{0,8},{4,12},{8,0},{12,4},{16,24},{20,28},{24,16},{28,20},{1,9},{5... | collective-permute-start | bytes 1081352 | tf_op jit(solution)/shard_map/ppermute | solution.py:1390
  560.2 31.5 %all-to-all-start.25 = ((bf16[4,288,512]{2,1,0:T(8,128)(2,1)}), bf16[4,288,512]{2,1,0:T(8,128)(2,1)S(1)}, u32[]{:S(2)}, u32[]{:S(2)}) async-start(bf16[4,288,512]{2,1,0:T(8,128)(2,1)} %broadcast_in_dim.18), calls=%async_computation.27 | async-start | bytes 2359296 | tf_op jit(solution)/shard_map/all_to_all | solution.py:1478
  (89 other events, 904.8 us)
Sparse Core Ops, SparseCore 0:
  289.2 76.1 reduce-scatter.2
  369.0 43.7 reduce-scatter.4
